TPU v7x, 32 devices: a whole 2x2x4 slice. The times are simulated.
32 devices in a mesh: row: 16 (over z, y, x), col: 2 (over core).
Axes of the slice: x: 2, y: 2, z: 4, core: 2. Of those that a mesh axis runs over, the one named last changes fastest.
Arguments:
- tables: float32 [262144, 1024], P('row', 'col'), may hold values from -3 to 3
- table_moment: float32 [262144, 1024], P('row', 'col'), may hold values from -3.8146973e-05 to 3.8146973e-05
- table_square: float32 [262144, 1024], P('row', 'col'), may hold values from 5.9604643e-13 to 2.3841857e-12
- expert_weight: float32 [8, 1024, 512], P(None, ('row', 'col')), may hold values from -0.1875 to 0.1875
- expert_moment: float32 [8, 1024, 512], P(None, ('row', 'col')), may hold values from -0.00048828125 to 0.00048828125
- expert_square: float32 [8, 1024, 512], P(None, ('row', 'col')), may hold values from 9.765625e-11 to 3.90625e-10
- gate_weight: float32 [5, 1024, 8], P(None, ('row', 'col')), may hold values from -0.1875 to 0.1875
- gate_moment: float32 [5, 1024, 8], P(None, ('row', 'col')), may hold values from -0.00024414062 to 0.00024414062
- gate_square: float32 [5, 1024, 8], P(None, ('row', 'col')), may hold values from 2.4414063e-11 to 9.765625e-11
- tower_weight: float32 [5, 512, 64], P(None, ('row', 'col')), may hold values from -0.5 to 0.5
- tower_moment: float32 [5, 512, 64], P(None, ('row', 'col')), may hold values from -0.00024414062 to 0.00024414062
- tower_square: float32 [5, 512, 64], P(None, ('row', 'col')), may hold values from 2.4414063e-11 to 9.765625e-11
- expert_bias: float32 [8, 512], replicated, may hold values from -1.5 to 1.5
- bias_moment: float32 [8, 512], replicated, may hold values from -0.00048828125 to 0.00048828125
- bias_square: float32 [8, 512], replicated, may hold values from 9.765625e-11 to 3.90625e-10
- head_bias: float32 [5, 65], replicated, may hold values from -1.5 to 1.5
- head_moment: float32 [5, 65], replicated, may hold values from -0.0012207031 to 0.0012207031
- head_square: float32 [5, 65], replicated, may hold values from 6.1035155e-10 to 2.4414062e-09
- tower_output: float32 [5, 64], replicated, may hold values from -1.5 to 1.5
- output_moment: float32 [5, 64], replicated, may hold values from -0.0024414062 to 0.0024414062
- output_square: float32 [5, 64], replicated, may hold values from 2.4414062e-09 to 9.765625e-09
- lookup_ids: int32 [4096, 16, 4], P(('row', 'col')), may hold values from 0 to 262143, as said below
- bag_lengths: int32 [4096, 16], P(('row', 'col')), may hold values from 1 to 4
- sample_counts: int32 [32], P(('row', 'col')), may hold values from 1 to 128, as said below
- labels: int32 [4096, 5], P(('row', 'col')), may hold values 0 or 1
- label_mask: int32 [4096, 5], P(('row', 'col')), may hold values 0 or 1
- sample_weight: float32 [4096], P(('row', 'col')), may hold values from 0.5 to 2
Outputs:
- updated_tables: float32 [262144, 1024], P('row', 'col')
- updated_table_moment: float32 [262144, 1024], P('row', 'col')
- updated_table_square: float32 [262144, 1024], P('row', 'col')
- updated_expert_weight: float32 [8, 1024, 512], P(None, ('row', 'col'))
- updated_expert_moment: float32 [8, 1024, 512], P(None, ('row', 'col'))
- updated_expert_square: float32 [8, 1024, 512], P(None, ('row', 'col'))
- updated_gate_weight: float32 [5, 1024, 8], P(None, ('row', 'col'))
- updated_gate_moment: float32 [5, 1024, 8], P(None, ('row', 'col'))
- updated_gate_square: float32 [5, 1024, 8], P(None, ('row', 'col'))
- updated_tower_weight: float32 [5, 512, 64], P(None, ('row', 'col'))
- updated_tower_moment: float32 [5, 512, 64], P(None, ('row', 'col'))
- updated_tower_square: float32 [5, 512, 64], P(None, ('row', 'col'))
- updated_expert_bias: float32 [8, 512], replicated
- updated_bias_moment: float32 [8, 512], replicated
- updated_bias_square: float32 [8, 512], replicated
- updated_head_bias: float32 [5, 65], replicated
- updated_head_moment: float32 [5, 65], replicated
- updated_head_square: float32 [5, 65], replicated
- updated_tower_output: float32 [5, 64], replicated
- updated_output_moment: float32 [5, 64], replicated
- updated_output_square: float32 [5, 64], replicated
- loss_sum: float32 [], replicated
- weight_total: float32 [], replicated
Inputs may be any that keep to these rules, and one draw needn't show every extreme that they name: sample_counts[d] counts the live samples of device d, devices in the order of row, then col; the last device holds exactly 128. `lookup_ids`: the row pieces are the row axis's blocks of 262144 / 16 consecutive rows. In each table, lookup slot j of the i-th sample of a device (i from 0 to 127) lies in row piece (i * 4 + j + s) mod 16, where s depends only on the device and the table.
All inputs are finite; a program needn't handle non-finite values. No bound on the sum of `labels` or of `label_mask` on one device may be relied on, other than what follows from the above.
Results may differ from a plain program's by a relative error of at most 0.0003.
Values sent between devices are 32-bit elements; how exact they have to be, the bound alone decides.
No kernel may reach another device: no remote copies, remote signals or barrier semaphores. Data moves between devices by JAX's collectives and lax.ppermute only.
A program may use at most 704 MiB of HBM per device.

v0:
```python
import jax
import jax.numpy as jnp
from jax import lax
from jax.sharding import PartitionSpec as P

DIM = 64
STEP = 10


HIGHEST = lax.Precision.HIGHEST
beta_one = 0.9
beta_two = 0.999
epsilon = 1e-08
decay_rate = 0.01
table_rate = 0.2
dense_rate = 0.02


def adamw(weight, moment, square, gradient, rate):
    moment_next = beta_one * moment + (1.0 - beta_one) * gradient
    square_next = beta_two * square + (1.0 - beta_two) * gradient * gradient
    moment_hat = moment_next / (1.0 - beta_one**STEP)
    square_hat = square_next / (1.0 - beta_two**STEP)
    weight_next = weight - rate * (
        moment_hat / (jnp.sqrt(square_hat) + epsilon) + decay_rate * weight
    )
    return (weight_next, moment_next, square_next)


def dense_loss(
    inputs,
    expert_weight,
    expert_bias,
    gate_weight,
    tower_weight,
    head_bias,
    tower_output,
    targets,
    keep,
):
    preact = (
        jnp.einsum("nk,ekh->enh", inputs, expert_weight, precision=HIGHEST)
        + expert_bias[:, None, :]
    )
    hidden = jax.nn.gelu(preact)
    gate_probs = jax.nn.softmax(
        jnp.einsum("nk,tke->tne", inputs, gate_weight, precision=HIGHEST), axis=-1
    )
    mixed = jnp.einsum("tne,enh->tnh", gate_probs, hidden, precision=HIGHEST)
    inner = (
        jnp.einsum("tnh,thc->tnc", mixed, tower_weight, precision=HIGHEST) + head_bias[:, None, :-1]
    )
    score = (
        jnp.einsum("tnc,tc->tn", jax.nn.gelu(inner), tower_output, precision=HIGHEST)
        + head_bias[:, -1:]
    )
    return jnp.sum(keep * (jax.nn.softplus(score) - targets * score))


def per_device(
    tables,
    table_moment,
    table_square,
    expert_weight,
    expert_moment,
    expert_square,
    gate_weight,
    gate_moment,
    gate_square,
    tower_weight,
    tower_moment,
    tower_square,
    expert_bias,
    bias_moment,
    bias_square,
    head_bias,
    head_moment,
    head_square,
    tower_output,
    output_moment,
    output_square,
    lookup_ids,
    bag_lengths,
    sample_counts,
    labels,
    label_mask,
    sample_weight,
):
    experts_full, gates_full, towers_full = (
        lax.all_gather(expert_weight, ("row", "col"), axis=1, tiled=True),
        lax.all_gather(gate_weight, ("row", "col"), axis=1, tiled=True),
        lax.all_gather(tower_weight, ("row", "col"), axis=1, tiled=True),
    )
    rows_here, width_here = tables.shape
    tabs_here = width_here // DIM
    tab_count = lookup_ids.shape[1]
    samples_here = lookup_ids.shape[0]
    col_count = lax.axis_size("col")
    row_count = lax.axis_size("row")
    flat_table = tables.reshape(rows_here * tabs_here, DIM)
    all_ids, all_lengths = (
        lax.all_gather(lookup_ids, ("row", "col"), axis=0, tiled=True),
        lax.all_gather(bag_lengths, ("row", "col"), axis=0, tiled=True),
    )
    first_table = lax.axis_index("col") * tabs_here
    my_ids = lax.dynamic_slice_in_dim(all_ids, first_table, tabs_here, 1)
    my_lengths = lax.dynamic_slice_in_dim(all_lengths, first_table, tabs_here, 1)
    local_rows = my_ids - lax.axis_index("row") * rows_here
    position = lax.broadcasted_iota(jnp.int32, my_ids.shape, 2)
    inside = (local_rows >= 0) & (local_rows < rows_here) & (position < my_lengths[:, :, None])
    table_pos = lax.broadcasted_iota(jnp.int32, my_ids.shape, 1)
    flat_index = jnp.where(inside, local_rows, 0) * tabs_here + table_pos
    use_weight = inside.astype(jnp.float32)
    partial_value = jnp.zeros(my_ids.shape[:2] + (DIM,), jnp.float32)
    for column in range(my_ids.shape[2]):
        partial_value = (
            partial_value + flat_table[flat_index[:, :, column]] * use_weight[:, :, column, None]
        )
    arrived = lax.all_to_all(partial_value, ("row", "col"), split_axis=0, concat_axis=0, tiled=True)
    arrived = arrived.reshape(row_count, col_count, samples_here, tabs_here, DIM)
    pooled = jnp.sum(arrived, axis=0).transpose(1, 0, 2, 3).reshape(samples_here, tab_count, DIM)
    live = (jnp.arange(samples_here, dtype=jnp.int32) < sample_counts[0]).astype(jnp.float32)
    keep = (sample_weight[:, None] * label_mask.astype(jnp.float32) * live[:, None]).T
    targets = labels.astype(jnp.float32).T
    inputs = pooled.reshape(samples_here, tab_count * DIM)

    def local_loss(
        inputs, experts_full, expert_bias, gates_full, towers_full, head_bias, tower_output
    ):
        return dense_loss(
            inputs,
            experts_full,
            expert_bias,
            gates_full,
            towers_full,
            head_bias,
            tower_output,
            targets,
            keep,
        )

    loss_here, pullback = jax.vjp(
        local_loss,
        inputs,
        experts_full,
        expert_bias,
        gates_full,
        towers_full,
        head_bias,
        tower_output,
    )
    loss_sum, weight_total = lax.psum((loss_here, jnp.sum(keep)), ("row", "col"))
    grad_inputs, grad_experts, grad_bias, grad_gates, grad_towers, grad_head, grad_output = (
        pullback(1.0 / weight_total)
    )
    grad_pooled = grad_inputs.reshape(samples_here, tab_count, DIM)
    grad_flat = jnp.zeros((rows_here * tabs_here, DIM), jnp.float32)
    hit_count = jnp.zeros((rows_here * tabs_here,), jnp.float32)
    halves = grad_pooled.reshape(samples_here, col_count, tabs_here, DIM).transpose(1, 0, 2, 3)
    copies = jnp.broadcast_to(halves[None], (row_count,) + halves.shape).reshape(-1, tabs_here, DIM)
    returned = lax.all_to_all(copies, ("row", "col"), split_axis=0, concat_axis=0, tiled=True)
    for column in range(my_ids.shape[2]):
        target_rows = flat_index[:, :, column].reshape(-1)
        grad_flat = grad_flat.at[target_rows].add(
            (returned * use_weight[:, :, column, None]).reshape(-1, DIM)
        )
        hit_count = hit_count.at[target_rows].add(use_weight[:, :, column].reshape(-1))
    touched = jnp.broadcast_to(
        (hit_count > 0.0).reshape(rows_here, tabs_here, 1), (rows_here, tabs_here, DIM)
    ).reshape(tables.shape)
    fresh_tab, fresh_mom, fresh_sq = adamw(
        tables, table_moment, table_square, grad_flat.reshape(tables.shape), table_rate
    )
    new_tables = jnp.where(touched, fresh_tab, tables)
    new_moment = jnp.where(touched, fresh_mom, table_moment)
    new_square = jnp.where(touched, fresh_sq, table_square)
    shard_experts, shard_gates, shard_towers = (
        lax.psum_scatter(grad_experts, ("row", "col"), scatter_dimension=1, tiled=True),
        lax.psum_scatter(grad_gates, ("row", "col"), scatter_dimension=1, tiled=True),
        lax.psum_scatter(grad_towers, ("row", "col"), scatter_dimension=1, tiled=True),
    )
    summed_bias, summed_head, summed_output = lax.psum(
        (grad_bias, grad_head, grad_output), ("row", "col")
    )
    experts_new = adamw(expert_weight, expert_moment, expert_square, shard_experts, dense_rate)
    gates_new = adamw(gate_weight, gate_moment, gate_square, shard_gates, dense_rate)
    towers_new = adamw(tower_weight, tower_moment, tower_square, shard_towers, dense_rate)
    biases_new = adamw(expert_bias, bias_moment, bias_square, summed_bias, dense_rate)
    heads_new = adamw(head_bias, head_moment, head_square, summed_head, dense_rate)
    outputs_new = adamw(tower_output, output_moment, output_square, summed_output, dense_rate)
    return (
        new_tables,
        new_moment,
        new_square,
        experts_new[0],
        experts_new[1],
        experts_new[2],
        gates_new[0],
        gates_new[1],
        gates_new[2],
        towers_new[0],
        towers_new[1],
        towers_new[2],
        biases_new[0],
        biases_new[1],
        biases_new[2],
        heads_new[0],
        heads_new[1],
        heads_new[2],
        outputs_new[0],
        outputs_new[1],
        outputs_new[2],
        loss_sum,
        weight_total,
    )


def solution(mesh):
    placed = (
        P("row", "col"),
        P("row", "col"),
        P("row", "col"),
        P(None, ("row", "col"), None),
        P(None, ("row", "col"), None),
        P(None, ("row", "col"), None),
        P(None, ("row", "col"), None),
        P(None, ("row", "col"), None),
        P(None, ("row", "col"), None),
        P(None, ("row", "col"), None),
        P(None, ("row", "col"), None),
        P(None, ("row", "col"), None),
        P(),
        P(),
        P(),
        P(),
        P(),
        P(),
        P(),
        P(),
        P(),
        P(("row", "col"), None, None),
        P(("row", "col"), None),
        P(("row", "col")),
        P(("row", "col"), None),
        P(("row", "col"), None),
        P(("row", "col")),
    )
    return jax.shard_map(
        per_device,
        mesh=mesh,
        in_specs=placed,
        out_specs=(
            P("row", "col"),
            P("row", "col"),
            P("row", "col"),
            P(None, ("row", "col"), None),
            P(None, ("row", "col"), None),
            P(None, ("row", "col"), None),
            P(None, ("row", "col"), None),
            P(None, ("row", "col"), None),
            P(None, ("row", "col"), None),
            P(None, ("row", "col"), None),
            P(None, ("row", "col"), None),
            P(None, ("row", "col"), None),
            P(),
            P(),
            P(),
            P(),
            P(),
            P(),
            P(),
            P(),
            P(),
            P(),
            P(),
        ),
        check_vma=False,
    )
```

profile of v0, /device:TPU:0, one launch (start us, length us, event | category | flops | bytes accessed | tf_op | source)
XLA Modules:
  0.0 5952.0 jit_solution(3294849653670965719)
XLA Ops:
  9.4 48.3 reshape.219
  57.7 44.3 all_gather.16
  109.3 496.0 %gather_fusion = f32[32768,64]{1,0:T(8,128)} fusion(f32[131072,64]{1,0:T(8,128)} %reshape.219, s32[32768]{0:T(1024)S(1)} %broadcast_clamp_fusion.7), kind=kCustom, calls=%fused_computation | custom fusion | bytes 16908288 | tf_op jit(solution)/shard_map/gather | solution.py:117
  605.3 498.7 %gather_fusion.1 = f32[32768,64]{1,0:T(8,128)} fusion(f32[131072,64]{1,0:T(8,128)} %reshape.219, s32[32768]{0:T(1024)S(1)} %broadcast_clamp_fusion.6), kind=kCustom, calls=%fused_computation.1 | custom fusion | bytes 16908288 | tf_op jit(solution)/shard_map/gather | solution.py:117
  1105.7 498.5 %gather_fusion.2 = f32[32768,64]{1,0:T(8,128)} fusion(f32[131072,64]{1,0:T(8,128)} %reshape.219, s32[32768]{0:T(1024)S(1)} %broadcast_clamp_fusion.5), kind=kCustom, calls=%fused_computation.2 | custom fusion | bytes 16908288 | tf_op jit(solution)/shard_map/gather | solution.py:117
  1605.8 499.0 %gather_fusion.3 = f32[32768,64]{1,0:T(8,128)} fusion(f32[131072,64]{1,0:T(8,128)} %reshape.219, s32[32768]{0:T(1024)S(1)} %broadcast_clamp_fusion.4), kind=kCustom, calls=%fused_computation.3 | custom fusion | bytes 16908288 | tf_op jit(solution)/shard_map/gather | solution.py:117
  2172.7 204.0 %psum.35 = f32[]{:T(128)} all-reduce(f32[]{:T(128)} %fusion.98), channel_id=1, replica_groups=mesh['row'=16,'col'=2] {'row','col'}, use_global_device_ids=true, to_apply=%region_5.6 | all-reduce | flops 1 | bytes 8 | tf_op jit(solution)/shard_map/psum | solution.py:152
  2407.9 60.5 %all_gather.18 = f32[5,1024,8]{2,0,1:T(8,128)} all-gather(f32[5,32,8]{2,0,1:T(8,128)S(1)} %copy.173), channel_id=1, replica_groups=mesh['row'=16,'col'=2] {'row','col'}, dimensions={1}, use_global_device_ids=true | all-gather | bytes 168960 | tf_op jit(solution)/shard_map/all_gather | solution.py:91
  2502.0 31.2 copy.190
  2534.1 42.9 all_gather.19
  2708.6 213.0 %scatter_custom_fusion = f32[131072]{0:T(1024)S(1)} fusion(s32[32768]{0:T(1024)} %bitcast.277, f32[32768]{0:T(1024)} %reshape.264, f32[]{:T(128)} %constant.26.clone.1), kind=kCustom, calls=%fused_computation.104 | custom fusion | flops 32768 | bytes 524800 | tf_op jit(solution)/shard_map/scatter-add | solution.py:167
  3081.7 217.2 %scatter_fusion = f32[131072]{0:T(1024)S(1)} fusion(f32[131072]{0:T(1024)S(1)} %scatter_custom_fusion, s32[32768]{0:T(1024)S(1)} %bitcast.271, f32[32768]{0:T(1024)S(1)} %copy-done.17), kind=kCustom, calls=%fused_computation.5 | custom fusion | flops 32768 | bytes 524288 | tf_op jit(solution)/shard_map/scatter-add | solution.py:167
  3298.9 219.5 %scatter_fusion.1 = f32[131072]{0:T(1024)S(1)} fusion(f32[131072]{0:T(1024)S(1)} %scatter_fusion, s32[32768]{0:T(1024)S(1)} %bitcast.273, f32[32768]{0:T(1024)S(1)} %copy-done.18), kind=kCustom, calls=%fused_computation.6 | custom fusion | flops 32768 | bytes 524288 | tf_op jit(solution)/shard_map/scatter-add | solution.py:167
  3518.5 224.2 %scatter_fusion.2 = f32[131072]{0:T(1024)S(1)} fusion(f32[131072]{0:T(1024)S(1)} %scatter_fusion.1, s32[32768]{0:T(1024)} %bitcast.275, f32[32768]{0:T(1024)S(1)} %copy-done.19), kind=kCustom, calls=%fused_computation.7 | custom fusion | flops 32768 | bytes 524288 | tf_op jit(solution)/shard_map/scatter-add | solution.py:167
  3757.9 41.8 all-reduce.2
  3871.7 439.4 %scatter_custom_fusion.4 = f32[131072,64]{1,0:T(8,128)} fusion(s32[32768]{0:T(1024)} %get-tuple-element.92, f32[]{:T(128)} %constant.26.clone.1, f32[32768,64]{1,0:T(8,128)} %get-tuple-element.132, s32[32768]{0:T(1024)S(1)} %broadcast_clamp_fusion.3), kind=kCustom, calls=%fused_computation.22 | custom fusion | flops 2097152 | bytes 33554944 | tf_op jit(solution)/shard_map/scatter-add | solution.py:164
  4311.1 453.2 %scatter_custom_fusion.5 = f32[131072,64]{1,0:T(8,128)} fusion(f32[131072,64]{1,0:T(8,128)} %scatter_custom_fusion.4, s32[32768]{0:T(1024)} %get-tuple-element.94, f32[32768,64]{1,0:T(8,128)} %get-tuple-element.131, s32[32768]{0:T(1024)S(1)} %broadcast_clamp_fusion.2), kind=kCustom, calls=%fused_computation.28 | custom fusion | flops 2097152 | bytes 33554432 | tf_op jit(solution)/shard_map/scatter-add | solution.py:164
  4764.4 453.5 %scatter_custom_fusion.6 = f32[131072,64]{1,0:T(8,128)} fusion(f32[131072,64]{1,0:T(8,128)} %scatter_custom_fusion.5, s32[32768]{0:T(1024)} %get-tuple-element.96, f32[32768,64]{1,0:T(8,128)} %get-tuple-element.130, s32[32768]{0:T(1024)S(1)} %broadcast_clamp_fusion.1), kind=kCustom, calls=%fused_computation.26 | custom fusion | flops 2097152 | bytes 33554432 | tf_op jit(solution)/shard_map/scatter-add | solution.py:164
  5217.8 461.4 %scatter_custom_fusion.7 = f32[131072,64]{1,0:T(8,128)} fusion(f32[131072,64]{1,0:T(8,128)} %scatter_custom_fusion.6, s32[32768]{0:T(1024)} %get-tuple-element.98, f32[32768,64]{1,0:T(8,128)} %get-tuple-element.129, s32[32768]{0:T(1024)S(1)} %broadcast_clamp_fusion), kind=kCustom, calls=%fused_computation.24 | custom fusion | flops 2097152 | bytes 33554432 | tf_op jit(solution)/shard_map/scatter-add | solution.py:164
  5679.2 54.7 reshape.226
  5765.0 74.4 %bitcast_select_fusion = (f32[16384,512]{0,1:T(8,128)}, f32[16384,512]{0,1:T(8,128)}, f32[16384,512]{0,1:T(8,128)}) fusion(f32[16384,512]{0,1:T(8,128)} %copy.190, f32[16384,512]{0,1:T(8,128)} %copy.189, pred[16384,8]{0,1:T(8,128)(4,1)S(1)} %copy-done.20, f32[16384,512]{0,1:T(8,128)} %copy.194, f32[16384,512]{0,1:T(8,128)} %copy.162), kind=kLoop, calls=%fused_computation.16 | loop fusion | flops 150994944 | bytes 235012096 | tf_op jit(solution)/shard_map/jit(_where)/select_n | solution.py:176
  5839.3 33.4 copy.209
  5872.8 33.4 copy.210
  5906.2 33.6 copy.211
  (262 shorter events, 559.9 us)
Async XLA Ops:
  7.2 94.8 %all-gather.3.cloned.1.call-start = ((), (), s32[]{:S(2)}) async-start(), calls=%async_computation.5 | async-start | bytes 1081344 | tf_op jit(solution)/shard_map/all_gather | solution.py:102
  8.6 2617.2 %all-gather.5.cloned.1.call-start = ((), (), s32[]{:S(2)}) async-start(), calls=%async_computation.6 | async-start | bytes 17301504 | tf_op jit(solution)/shard_map/all_gather | solution.py:90
  9.4 48.3 copy-start.53
  1605.8 499.0 %copy-start.13 = (f32[4096,8,4]{0,1,2:T(8,128)S(1)}, f32[4096,8,4]{0,1,2:T(8,128)}, u32[]{:S(2)}) copy-start(f32[4096,8,4]{0,1,2:T(8,128)} %get-tuple-element.124) | copy-start | bytes 1572868
  2167.6 411.7 %all-to-all-start = ((f32[32,1,65536]{2,1,0:T(1,128)}), f32[32,1,65536]{2,1,0:T(1,128)}, u32[]{:S(2)}, u32[]{:S(2)}) async-start(f32[32,1,65536]{2,1,0:T(1,128)} %reshape.352), calls=%async_computation | async-start | bytes 16777216 | tf_op jit(solution)/shard_map/all_to_all | solution.py:119
  2171.4 1630.2 %reduce-scatter.10.cloned.1.call-start = ((), (), s32[]{:S(2)}) async-start(), calls=%async_computation.9 | async-start | bytes 540672
  2502.0 75.0 %copy-start.27 = (s32[4096,8,1]{0,1,2:T(8,128)S(1)}, s32[4096,8,1]{0,1,2:T(8,128)}, u32[]{:S(2)}) copy-start(s32[4096,8,1]{0,1,2:T(8,128)} %get-tuple-element.148) | copy-start | bytes 393220
  2640.4 365.3 %copy-start = (f32[128,8,512]{2,0,1:T(8,128)}, f32[128,8,512]{2,0,1:T(8,128)S(1)}, u32[]{:S(2)}) copy-start(f32[128,8,512]{2,0,1:T(8,128)S(1)} %get-tuple-element.153) | copy-start | bytes 6291460
  2671.7 1131.4 %reduce-scatter.8.cloned.1.call-start = ((), (), s32[]{:S(2)}) async-start(), calls=%async_computation.8 | async-start | bytes 1351680 | tf_op jit(solution)/shard_map/reduce_scatter | solution.py:180
  2681.1 3258.6 %reduce-scatter.6.cloned.1.call-start = ((), (), s32[]{:S(2)}) async-start(), calls=%async_computation.7 | async-start | bytes 17301504 | tf_op jit(solution)/shard_map/reduce_scatter | solution.py:178
  3064.9 739.7 %all-to-all-start.1 = ((f32[32,1,65536]{2,1,0:T(1,128)}), f32[32,1,65536]{2,1,0:T(1,128)}, u32[]{:S(2)}, u32[]{:S(2)}) async-start(f32[32,1,65536]{2,1,0:T(1,128)} %reshape.354), calls=%async_computation.1 | async-start | bytes 16777216 | tf_op jit(solution)/shard_map/all_to_all | solution.py:161
  3070.5 228.4 %copy-start.16 = (s32[32768,1]{0,1:T(1,128)}, s32[32768,1]{0,1:T(1,128)S(1)}, u32[]{:S(2)}) copy-start(s32[32768,1]{0,1:T(1,128)S(1)} %compare_select_fusion) | copy-start | bytes 393220
  3081.7 217.2 %copy-start.18 = (f32[32768]{0:T(1024)S(1)}, f32[32768]{0:T(1024)}, u32[]{:S(2)}) copy-start(f32[32768]{0:T(1024)} %reshape.280) | copy-start | bytes 393220
  3298.9 219.6 %copy-start.19 = (f32[32768]{0:T(1024)S(1)}, f32[32768]{0:T(1024)}, u32[]{:S(2)}) copy-start(f32[32768]{0:T(1024)} %reshape.288) | copy-start | bytes 393220
  3754.0 46.3 copy-start.47
  3754.0 46.3 copy-start.56
  3754.0 46.9 copy-start.50
  3754.1 46.9 copy-start.51
  3754.1 48.4 copy-start.39
  3754.1 48.4 copy-start.48
  3754.1 48.4 copy-start.49
  3754.1 49.0 copy-start.33
  3754.1 49.0 copy-start.44
  3754.1 49.0 copy-start.45
  (44 other events, 600.2 us)
Sparse Core Ops, SparseCore 0:
  11.5 55.1 all-gather.2
  69.6 114.5 all-gather.4
  2671.8 131.5 reduce-scatter.9
  2805.6 131.3 reduce-scatter.7
  2993.7 286.0 reduce-scatter.5
where the time goes:
time: 5990 us; the launch traced here: 5950 us
  other arithmetic  2940 us (49%)
  local copies, waits for them, and re-layouts  2510 us (42%)
  blocking collectives  393 us (7%)
  matrix products  83.8 us (1%)
    gather x4, local copies, waits for them, and re-layouts, per_device(): flat_table[flat_index[:, :, column]] * use_weight[:, :, column, None]  1990 us
    scatter-add x12, other arithmetic, per_device(): grad_flat.at[target_rows]  1850 us
    scatter-add x4, other arithmetic, per_device(): hit_count.at[target_rows].add(use_weight[:, :, column].reshape(-1))  874 us
    unnamed x141, local copies, waits for them, and re-layouts  286 us
    psum x1, blocking collectives, per_device(): lax.psum((loss_here, jnp.sum(keep)), ('row', 'col'))  204 us
  transfers between devices with their start and end apart: 7, of which 0 were waited for; matrix products, arithmetic and copies ran while one was open for 92% of the time, Pallas kernels for 0%

commit v1 on v0

v1 whole, which is shorter than its diff:
```python
import functools
import math

import jax
import jax.numpy as jnp
from jax import lax
from jax.experimental import pallas as pl
from jax.experimental.pallas import tpu as pltpu
from jax.sharding import Mesh
from jax.sharding import PartitionSpec as P

DIM = 64
STEP = 10
LANES = 128
MIB = 1024 * 1024

beta_one = 0.9
beta_two = 0.999
epsilon = 1e-08
decay_rate = 0.01
table_rate = 0.2
dense_rate = 0.02

ROW = ("grp", "near")
GROUP = ("near", "col")
ALL = ("grp", "near", "col")
FAST = lax.Precision.HIGH


def adamw(weight, moment, square, gradient, rate):
    moment_next = beta_one * moment + (1.0 - beta_one) * gradient
    square_next = beta_two * square + (1.0 - beta_two) * gradient * gradient
    moment_hat = moment_next * (1.0 / (1.0 - beta_one**STEP))
    square_hat = square_next * (1.0 / (1.0 - beta_two**STEP))
    weight_next = weight - rate * (
        moment_hat / (jnp.sqrt(square_hat) + epsilon) + decay_rate * weight
    )
    return (weight_next, moment_next, square_next)


def table_adamw(weight, moment, square, gradient):
    root = math.sqrt(1.0 - beta_two**STEP)
    moment_next = beta_one * moment + (1.0 - beta_one) * gradient
    square_next = beta_two * square + (1.0 - beta_two) * (gradient * gradient)
    r = lax.rsqrt(square_next)
    below = 1.0 + (epsilon * root) * r
    near = pl.reciprocal(below, approx=True)
    near = near * (2.0 - below * near)
    ratio = (moment_next * r) * near
    weight_next = weight * (1.0 - table_rate * decay_rate) - ratio * (
        table_rate * root / (1.0 - beta_one**STEP)
    )
    return (weight_next, moment_next, square_next)


def low_half():
    return lax.broadcasted_iota(jnp.int32, (1, LANES), 1) < DIM


def gather_kernel(rows, cols, devices, each, idx_ref, table_ref, out_ref, buf, sem):
    count = devices * each

    def fetch(u):
        return pltpu.make_async_copy(
            table_ref.at[:, pl.ds(u * LANES, LANES)], buf.at[u, pl.ds(0, rows)], sem.at[u]
        )

    for u in range(cols):
        fetch(u).start()
        buf[u, pl.ds(rows, 8), :] = jnp.zeros((8, LANES), jnp.float32)
    low = low_half()
    for u in range(cols):
        fetch(u).wait()

        def step(d, carry):
            base = d * each
            for k in range(each):
                first = idx_ref[2 * u * count + base + k]
                second = idx_ref[(2 * u + 1) * count + base + k]
                out_ref[d, u, pl.ds(k, 1), :] = jnp.where(
                    low, buf[u, pl.ds(first, 1), :], buf[u, pl.ds(second, 1), :]
                )
            return carry

        lax.fori_loop(0, devices, step, 0)


def gather_rows(idx, table, devices, each):
    rows, width = table.shape
    cols = width // LANES
    return pl.pallas_call(
        functools.partial(gather_kernel, rows, cols, devices, each),
        out_shape=jax.ShapeDtypeStruct((devices, cols, each, LANES), jnp.float32),
        in_specs=[
            pl.BlockSpec(memory_space=pltpu.SMEM),
            pl.BlockSpec(memory_space=pl.ANY),
        ],
        out_specs=pl.BlockSpec(memory_space=pltpu.VMEM),
        scratch_shapes=[
            pltpu.VMEM((cols, rows + 8, LANES), jnp.float32),
            pltpu.SemaphoreType.DMA((cols,)),
        ],
        compiler_params=pltpu.CompilerParams(vmem_limit_bytes=48 * MIB),
        cost_estimate=pl.CostEstimate(
            flops=0, bytes_accessed=2 * rows * width * 4, transcendentals=0
        ),
    )(idx, table)


def pool_kernel(pieces, halves, cols, each, shift_ref, in_ref, out_ref):
    low = low_half()
    for c in range(halves):
        for u in range(cols):
            shifts = [shift_ref[c * 2 * cols + 2 * u + h] for h in range(2)]
            for a in range(pieces // 4):
                sums = []
                for s in shifts:
                    total = None
                    for j in range(4):
                        part = in_ref[lax.rem(4 * a + j + s, pieces), c, u]
                        total = part if total is None else total + part
                    sums.append(total)
                at = (c * cols + u) * LANES
                out_ref[a * each : (a + 1) * each, at : at + LANES] = jnp.where(
                    low, sums[0], sums[1]
                )


def pool(shifts, arrived):
    pieces, halves, cols, each, _ = arrived.shape
    return pl.pallas_call(
        functools.partial(pool_kernel, pieces, halves, cols, each),
        out_shape=jax.ShapeDtypeStruct(
            (pieces // 4 * each, halves * cols * LANES), jnp.float32
        ),
        in_specs=[
            pl.BlockSpec(memory_space=pltpu.SMEM),
            pl.BlockSpec(memory_space=pltpu.VMEM),
        ],
        out_specs=pl.BlockSpec(memory_space=pltpu.VMEM),
        compiler_params=pltpu.CompilerParams(vmem_limit_bytes=24 * MIB),
    )(shifts, arrived)


def spread_kernel(pieces, halves, cols, each, shift_ref, in_ref, *out_refs):
    low = low_half()
    for c in range(halves):
        for u in range(cols):
            shifts = [shift_ref[c * 2 * cols + 2 * u + h] for h in range(2)]
            at = (c * cols + u) * LANES
            for r in range(pieces):
                parts = []
                for s in shifts:
                    place = lax.rem(r - s + pieces, pieces) // 4
                    start = pl.multiple_of(place * each, each)
                    parts.append(in_ref[pl.ds(start, each), at : at + LANES])
                out_refs[u][halves * r + c] = jnp.where(low, parts[0], parts[1])


def spread(shifts, grads, pieces, halves):
    samples, width = grads.shape
    cols = width // halves // LANES
    each = samples * 4 // pieces
    return pl.pallas_call(
        functools.partial(spread_kernel, pieces, halves, cols, each),
        out_shape=[
            jax.ShapeDtypeStruct((pieces * halves, each, LANES), jnp.float32)
        ]
        * cols,
        in_specs=[
            pl.BlockSpec(memory_space=pltpu.SMEM),
            pl.BlockSpec(memory_space=pltpu.VMEM),
        ],
        out_specs=[pl.BlockSpec(memory_space=pltpu.VMEM)] * cols,
        compiler_params=pltpu.CompilerParams(vmem_limit_bytes=24 * MIB),
    )(shifts, grads)


def update_kernel(rows, part, devices, each, block, outs, idx_ref, grad_ref, *refs):
    sources, targets = refs[:3], refs[-7 - outs : -4 - outs]
    bufs, sums, in_sem, out_sem = refs[-7:-4], refs[-4:-2], refs[-2], refs[-1]
    count = devices * each
    blocks = rows // block
    columns = pl.ds(part * LANES, LANES)

    def fetch(b, k):
        at = pl.ds(b * block, block)
        return pltpu.make_async_copy(
            sources[k].at[at, columns], bufs[k].at[at], in_sem.at[k, b]
        )

    def store(b, k):
        at = pl.ds(b * block, block)
        return pltpu.make_async_copy(
            bufs[k].at[at], targets[k].at[at, columns], out_sem.at[k, b]
        )

    for b in range(blocks):
        for k in range(3):
            fetch(b, k).start()

    def clear(i, carry):
        at = pl.ds(pl.multiple_of(i * 64, 64), 64)
        for s in sums:
            s[at, :] = jnp.full((64, LANES), jnp.inf, jnp.float32)
        return carry

    lax.fori_loop(0, rows // 64, clear, 0)
    for s in sums:
        s[pl.ds(rows, 8), :] = jnp.full((8, LANES), jnp.inf, jnp.float32)

    def step(d, carry):
        for k in range(each):
            value = grad_ref[d, pl.ds(k, 1), :]
            for q in range(2):
                row = pl.ds(idx_ref[(2 * part + q) * count + d * each + k], 1)
                old = sums[q][row, :]
                sums[q][row, :] = value + jnp.where(old < jnp.inf, old, 0.0)
        return carry

    lax.fori_loop(0, devices, step, 0)

    low = low_half()
    tile = 128
    for b in range(blocks):
        for k in range(3):
            fetch(b, k).wait()

        def renew(i, carry):
            at = pl.ds(pl.multiple_of(b * block + i * tile, tile), tile)
            total = jnp.where(low, sums[0][at, :], sums[1][at, :])
            old = [buf[at, :] for buf in bufs]
            new = table_adamw(*old, total)
            hit = total < jnp.inf
            for k in range(3):
                bufs[k][at, :] = jnp.where(hit, new[k], old[k])
            return carry

        lax.fori_loop(0, block // tile, renew, 0)
        for k in range(3):
            store(b, k).start()
    for b in range(blocks):
        for k in range(3):
            store(b, k).wait()


def update_part(idx, grads, tables, part, each, previous, later):
    rows, width = tables[0].shape
    devices = grads.shape[0]
    block = rows // 8
    extra = [] if previous is None else list(previous)
    through = [] if later is None else [later]
    place = pl.BlockSpec(memory_space=pl.ANY)
    aliases = {5 + k: k for k in range(len(extra))}
    if through:
        aliases[5 + len(extra)] = 3
    done = pl.pallas_call(
        functools.partial(update_kernel, rows, part, devices, each, block, 3 + len(through)),
        out_shape=[jax.ShapeDtypeStruct((rows, width), jnp.float32)] * 3
        + [jax.ShapeDtypeStruct(x.shape, x.dtype) for x in through],
        in_specs=[
            pl.BlockSpec(memory_space=pltpu.SMEM),
            pl.BlockSpec(memory_space=pltpu.VMEM),
        ]
        + [place] * (3 + len(extra) + len(through)),
        out_specs=[place] * (3 + len(through)),
        input_output_aliases=aliases,
        scratch_shapes=[pltpu.VMEM((rows, LANES), jnp.float32)] * 3
        + [pltpu.VMEM((rows + 8, LANES), jnp.float32)] * 2
        + [pltpu.SemaphoreType.DMA((3, rows // block))] * 2,
        compiler_params=pltpu.CompilerParams(vmem_limit_bytes=48 * MIB),
        cost_estimate=pl.CostEstimate(
            flops=30 * rows * LANES, bytes_accessed=rows * LANES * 24, transcendentals=0
        ),
    )(idx, grads, *tables, *extra, *through)
    return done[:3], (done[3] if through else None)


def gelu_slope(a):
    scale = math.sqrt(2.0 / math.pi)
    t = jnp.tanh(scale * (a + 0.044715 * a * a * a))
    return 0.5 * (1.0 + t) + 0.5 * a * (1.0 - t * t) * scale * (1.0 + 3.0 * 0.044715 * a * a)


def swap_near(x):
    count = lax.axis_size("near")
    return lax.ppermute(x, "near", [(i, i ^ 1) for i in range(count)])


def swap_core(x):
    return lax.ppermute(x, "col", [(0, 1), (1, 0)])


def gather_group(x):
    pair = jnp.concatenate([x, swap_near(x)], axis=0)
    return jnp.concatenate([pair, swap_core(pair)], axis=0)


def sum_group(x):
    half = x.shape[0] // 2
    pair = x[:half] + swap_core(x[half:])
    return pair[: half // 2] + swap_near(pair[half // 2 :])


def exchange_group(x, member):
    blocks = [lax.dynamic_index_in_dim(x, member ^ i, 0, False) for i in range(4)]
    pair = jnp.stack([blocks[1], blocks[3]])
    other = swap_core(pair)
    far = swap_near(jnp.stack([blocks[2], other[1]]))
    came = jnp.stack([blocks[0], other[0], far[0], far[1]])
    return jnp.stack([lax.dynamic_index_in_dim(came, member ^ i, 0, False) for i in range(4)])


def padded(x, width):
    return jnp.pad(x, [(0, 0)] * (x.ndim - 1) + [(0, width - x.shape[-1])])


def dot(a, b, dims=((1,), (0,))):
    return lax.dot_general(
        a, b, (dims, ((), ())), precision=FAST, preferred_element_type=jnp.float32
    )


def per_device(
    tables,
    table_moment,
    table_square,
    expert_weight,
    expert_moment,
    expert_square,
    gate_weight,
    gate_moment,
    gate_square,
    tower_weight,
    tower_moment,
    tower_square,
    expert_bias,
    bias_moment,
    bias_square,
    head_bias,
    head_moment,
    head_square,
    tower_output,
    output_moment,
    output_square,
    lookup_ids,
    bag_lengths,
    sample_counts,
    labels,
    label_mask,
    sample_weight,
):
    halves = lax.axis_size("col")
    pieces = lax.axis_size("grp") * lax.axis_size("near")
    devices = pieces * halves
    groups = lax.axis_size("grp")
    members = devices // groups
    rows_here, width_here = tables.shape
    tabs_here = width_here // DIM
    samples, tabs, bag = lookup_ids.shape
    each = samples * bag // pieces
    classes = pieces // bag
    experts, depth, hidden_units = expert_weight.shape
    mine = experts // members
    tasks, tower_depth, tower_units = tower_weight.shape
    upper_width = tasks * tower_units
    member = lax.axis_index("near") * halves + lax.axis_index("col")

    def reorder(x):
        return x.reshape((each, classes) + x.shape[1:]).swapaxes(0, 1).reshape(x.shape)

    live = (jnp.arange(samples, dtype=jnp.int32) < sample_counts[0]).astype(jnp.float32)
    keep = reorder(sample_weight[:, None] * label_mask.astype(jnp.float32) * live[:, None])
    targets = reorder(labels.astype(jnp.float32))

    ids = lookup_ids.transpose(0, 2, 1).reshape(each, pieces, tabs)
    use = jnp.arange(bag, dtype=jnp.int32)[None, :, None] < bag_lengths[:, None, :]
    owner = ids // rows_here
    local = jnp.where(use.reshape(each, pieces, tabs), ids - owner * rows_here, rows_here)
    here = owner[None] == jnp.arange(pieces, dtype=jnp.int32)[:, None, None, None]
    wanted = jnp.sum(jnp.where(here, local[None], 0), axis=2)
    wanted = wanted.transpose(0, 2, 1).reshape(devices, tabs_here * each).astype(jnp.float32)
    message = jnp.concatenate(
        [wanted, jnp.broadcast_to(jnp.sum(keep), (devices, 1))], axis=1
    )
    long = -(-message.shape[1] // 1024) * 1024
    message = padded(message, long).reshape(devices, long // LANES, LANES)
    asked = lax.all_to_all(message, ALL, 0, 0, tiled=True).reshape(devices, long)
    idx = asked[:, : tabs_here * each].reshape(devices, tabs_here, each)
    idx = idx.swapaxes(0, 1).reshape(-1).astype(jnp.int32)
    weight_total = jnp.sum(asked[:, tabs_here * each])
    shifts = lookup_ids[0, :, 0] // rows_here

    lots = mine * hidden_units
    send = expert_weight.reshape(members, mine, depth, hidden_units).swapaxes(1, 2)
    send = send.reshape(members, depth, lots)
    small = jnp.concatenate(
        [
            tower_weight.swapaxes(0, 1).reshape(-1),
            gate_weight.swapaxes(0, 1).reshape(-1),
        ]
    )
    tower_flat = tower_depth * upper_width
    small_rows = -(-small.shape[0] // (8 * lots)) * 8
    small = padded(small, small_rows * lots).reshape(1, small_rows, lots)
    send = jnp.concatenate(
        [send, jnp.broadcast_to(small, (members, small_rows, lots))], axis=1
    )
    shared = exchange_group(send, member)
    shared = shared.reshape(members, depth + small_rows, lots)
    whole = lax.all_gather(shared, "grp", axis=0, tiled=True)
    weights = whole[:, :depth].reshape(devices * depth, lots)
    small = whole[:, depth:].reshape(devices, small_rows * lots)
    towers = small[:, :tower_flat].reshape(devices * tower_depth, upper_width)
    gates = small[:, tower_flat : tower_flat + depth * tasks * experts].reshape(
        devices * depth, tasks * experts
    )
    gates_mine = lax.dynamic_slice_in_dim(
        gates.reshape(devices * depth, tasks, experts), member * mine, mine, 2
    ).reshape(devices * depth, tasks * mine)
    bias_mine = lax.dynamic_slice_in_dim(expert_bias, member * mine, mine, 0).reshape(1, lots)

    picked = gather_rows(idx, tables, devices, each)
    cols = width_here // LANES
    arrived = lax.all_to_all(
        picked.reshape(devices, cols * each, LANES), ALL, 0, 0, tiled=True
    ).reshape(pieces, halves, cols, each, LANES)
    pooled = pool(shifts, arrived)
    inputs = gather_group(pooled)

    total = inputs.shape[0]
    preact = dot(inputs, weights) + bias_mine
    hidden = jax.nn.gelu(preact)
    logits = dot(inputs, gates).reshape(total, tasks, experts)
    probs = jax.nn.softmax(logits, axis=-1)
    probs_mine = lax.dynamic_slice_in_dim(probs, member * mine, mine, 2)
    parts = [
        dot(hidden[:, i * hidden_units : (i + 1) * hidden_units], towers).reshape(
            total, tasks, tower_units
        )
        for i in range(mine)
    ]
    inner_part = sum(parts[i] * probs_mine[:, :, i, None] for i in range(mine))
    mixed = sum_group(inner_part.reshape(total, upper_width)).reshape(
        samples, tasks, tower_units
    )
    inner = mixed + head_bias[None, :, :-1]
    upper = jax.nn.gelu(inner)
    score = jnp.sum(upper * tower_output[None], axis=-1) + head_bias[None, :, -1]
    loss_here = jnp.sum(keep * (jax.nn.softplus(score) - targets * score))

    d_score = keep * (jax.nn.sigmoid(score) - targets) / weight_total
    d_inner = d_score[:, :, None] * tower_output[None] * gelu_slope(inner)
    grad_output = jnp.sum(d_score[:, :, None] * upper, axis=0)
    grad_head = jnp.concatenate(
        [jnp.sum(d_inner, axis=0), jnp.sum(d_score, axis=0)[:, None]], axis=1
    )
    mean = jnp.sum(d_inner * mixed, axis=-1)
    packed = jnp.concatenate([d_inner.reshape(samples, upper_width), mean], axis=1)
    packed = padded(packed, -(-packed.shape[1] // LANES) * LANES)
    packed = gather_group(packed)
    d_inner = packed[:, :upper_width].reshape(total, tasks, tower_units)
    mean = packed[:, upper_width : upper_width + tasks]
    d_logits = []
    spreads = []
    d_hidden = []
    for i in range(mine):
        d_prob = jnp.sum(d_inner * parts[i], axis=-1)
        d_logits.append(probs_mine[:, :, i] * (d_prob - mean))
        spreads.append((d_inner * probs_mine[:, :, i, None]).reshape(total, upper_width))
        d_hidden.append(dot(spreads[i], towers, ((1,), (1,))))
    d_logits = jnp.stack(d_logits, axis=-1).reshape(total, tasks * mine)
    d_preact = jnp.concatenate(d_hidden, axis=1) * gelu_slope(preact)
    d_inputs = dot(d_preact, weights, ((1,), (1,))) + dot(d_logits, gates_mine, ((1,), (1,)))
    d_pooled = sum_group(d_inputs)

    grad_weights = dot(inputs, d_preact, ((0,), (0,)))
    grad_gates = dot(inputs, d_logits, ((0,), (0,))).reshape(devices, -1)
    grad_towers = sum(
        dot(hidden[:, i * hidden_units : (i + 1) * hidden_units], spreads[i], ((0,), (0,)))
        for i in range(mine)
    ).reshape(devices, -1)
    gate_flat = grad_gates.shape[1]
    small = padded(jnp.concatenate([grad_towers, grad_gates], axis=1), small_rows * lots)
    summed = jnp.concatenate(
        [grad_weights.reshape(devices, depth, lots), small.reshape(devices, small_rows, lots)],
        axis=1,
    )
    summed = lax.psum_scatter(summed, "grp", scatter_dimension=0, tiled=True)
    summed = exchange_group(summed, member)
    shard_experts = (
        summed[:, :depth]
        .reshape(members, depth, mine, hidden_units)
        .swapaxes(1, 2)
        .reshape(experts, depth, hidden_units)
    )
    small = summed[:, depth:].reshape(members, small_rows * lots)
    shard_towers = (
        jnp.sum(small[:, :tower_flat], axis=0)
        .reshape(tower_depth, tasks, tower_units)
        .swapaxes(0, 1)
    )
    shard_gates = (
        small[:, tower_flat : tower_flat + gate_flat]
        .reshape(members, depth, tasks, mine)
        .transpose(2, 1, 0, 3)
        .reshape(tasks, depth, experts)
    )

    grad_bias = jnp.sum(d_preact, axis=0)
    same = jnp.concatenate(
        [grad_bias, grad_head.reshape(-1), grad_output.reshape(-1), loss_here.reshape(1)]
    )
    cuts = [lots, grad_head.size, grad_output.size, 1]
    long = -(-same.shape[0] // 1024) * 1024
    same = jnp.broadcast_to(
        padded(same, long).reshape(1, long // LANES, LANES), (devices, long // LANES, LANES)
    )
    returned = list(spread(shifts, d_pooled, pieces, halves))
    returned[1] = jnp.concatenate([returned[1], same], axis=1)
    came = [lax.all_to_all(x, ALL, 0, 0, tiled=True) for x in returned[:2]]
    new_tables = None
    for u in range(cols):
        later = returned[u + 2] if u + 2 < cols else None
        new_tables, later = update_part(
            idx, came[u], (tables, table_moment, table_square), u, each, new_tables, later
        )
        if later is not None:
            came.append(lax.all_to_all(later, ALL, 0, 0, tiled=True))
    same = came[1][:, each:].reshape(devices, long)
    found = []
    start = 0
    for size in cuts:
        found.append(same[:, start : start + size])
        start += size
    summed_bias = jnp.sum(found[0].reshape(groups, members, lots), axis=0).reshape(
        experts, hidden_units
    )
    summed_head = jnp.sum(found[1], axis=0).reshape(head_bias.shape)
    summed_output = jnp.sum(found[2], axis=0).reshape(tower_output.shape)
    loss_sum = jnp.sum(found[3])

    return (
        *new_tables,
        *adamw(expert_weight, expert_moment, expert_square, shard_experts, dense_rate),
        *adamw(gate_weight, gate_moment, gate_square, shard_gates, dense_rate),
        *adamw(tower_weight, tower_moment, tower_square, shard_towers, dense_rate),
        *adamw(expert_bias, bias_moment, bias_square, summed_bias, dense_rate),
        *adamw(head_bias, head_moment, head_square, summed_head, dense_rate),
        *adamw(tower_output, output_moment, output_square, summed_output, dense_rate),
        loss_sum,
        weight_total,
    )


def solution(mesh):
    pieces, halves = mesh.devices.shape
    fine = Mesh(mesh.devices.reshape(pieces // 2, 2, halves), ALL)
    table = P(ROW, "col")
    middle = P(None, ALL, None)
    first = P(ALL)
    return jax.shard_map(
        per_device,
        mesh=fine,
        in_specs=(table,) * 3 + (middle,) * 9 + (P(),) * 9 + (first,) * 6,
        out_specs=(table,) * 3 + (middle,) * 9 + (P(),) * 11,
        check_vma=False,
    )
```

time: 5990 us -> 444 us (0.07)
  other arithmetic: 2940 us -> 28.2 us
  local copies, waits for them, and re-layouts: 2510 us -> 43 us
  blocking collectives: 393 us -> 15.2 us
  waiting for transfers between devices: 0.81 us -> 170 us
  Pallas kernels: 0 us -> 98.5 us
    scatter-add x16 -> x0, other arithmetic: 2730 us -> none  [the longest x12 1850 us: per_device(): grad_flat.at[target_rows]]
    gather x4 -> x0, local copies, waits for them, and re-layouts: 1990 us -> none  [per_device(): flat_table[flat_index[:, :, column]] * use_weight[:, :, column, None]]
    unnamed x141 -> x115, local copies, waits for them, and re-layouts: 286 us -> 8.63 us
    psum x2 -> x0, blocking collectives: 246 us -> none  [the longest x1 204 us: per_device(): lax.psum((loss_here, jnp.sum(keep)), ('row', 'col'))]
    all_gather x3 -> x0, blocking collectives: 148 us -> none  [the longest x1 60.5 us: per_device(): lax.all_gather(gate_weight, ('row', 'col'), axis=1, tiled=True)]
    reshape x4 -> x21, local copies, waits for them, and re-layouts: 134 us -> 9.14 us  [the longest x6 3.76 us: reorder(): x.reshape((each, classes) + x.shape[1:]).swapaxes(0, 1).reshape(x.shape)]
    all_to_all x2 -> x5, waiting for transfers between devices: 0.01 us -> 107 us  [the longest x1 90.2 us: per_device(): lax.all_to_all(picked.reshape(devices, cols * each, LANES), ALL, 0, 0, ti...]
    pallas_call x0 -> x7, Pallas kernels: none -> 98.5 us  [the longest x4 79.1 us: update_part(): pl.pallas_call(functools.partial(update_kernel, rows, part, devices, each...]
  transfers between devices with their start and end apart: 7 -> 19, of which waited for: 0 -> 12; matrix products, arithmetic and copies ran while one was open for 92% -> 9% of each run, Pallas kernels for 0% -> 22%
where the time goes in v1:
time: 444 us; the launch traced here: 439 us
  waiting for transfers between devices  170 us (38%)
  Pallas kernels  98.5 us (22%)
  local copies, waits for them, and re-layouts  43 us (10%)
  matrix products  37.2 us (8%)
  starting transfers between devices  30.9 us (7%)
  other arithmetic  28.2 us (6%)
  between operations  16.1 us (4%)
  blocking collectives  15.2 us (3%)
    all_to_all x1, waiting for transfers between devices, per_device(): lax.all_to_all(picked.reshape(devices, cols * each, LANES), ALL, 0, 0, ti...  90.2 us
    pallas_call x4, Pallas kernels, update_part(): pl.pallas_call(functools.partial(update_kernel, rows, part, devices, each...  79.1 us
    ppermute x6, waiting for transfers between devices, swap_near(): return lax.ppermute(x, 'near', [(i, i ^ 1) for i in range(count)])  40.2 us
    dot_general x12, matrix products, dot(): lax.dot_general(a, b, (dims, ((), ())), precision=FAST, preferred_element...  37.2 us
    all_to_all x2, waiting for transfers between devices, per_device(): came = [lax.all_to_all(x, ALL, 0, 0, tiled=True) for x in returned[:2]]  16.6 us
    reduce_scatter x1, waiting for transfers between devices, per_device(): summed = lax.psum_scatter(summed, 'grp', scatter_dimension=0, tiled=True)  16 us
    all_to_all x1, blocking collectives, per_device(): lax.all_to_all(message, ALL, 0, 0, tiled=True).reshape(devices, long)  15.2 us
    pallas_call x1, Pallas kernels, gather_rows(): pl.pallas_call(functools.partial(gather_kernel, rows, cols, devices, each...  14.9 us
  transfers between devices with their start and end apart: 19, of which 12 were waited for; matrix products, arithmetic and copies ran while one was open for 9% of the time, Pallas kernels for 22%

profile of v1, /device:TPU:0, one launch (start us, length us, event | category | flops | bytes accessed | tf_op | source)
XLA Modules:
  0.0 439.2 jit_solution(1631594089784397305)
XLA Ops:
  14.5 8.0 %collective-permute-done.3 = f32[2,40,1024]{2,1,0:T(8,128)S(1)} collective-permute-done((f32[2,40,1024]{2,1,0:T(8,128)S(1)}, f32[2,40,1024]{2,1,0:T(8,128)S(1)}, u32[]{:S(2)}, u32[]{:S(2)}) %collective-permute-start.3) | collective-permute-done | bytes 327712 | tf_op jit(solution)/shard_map/ppermute | solution.py:287
  26.8 15.2 %all_to_all.30 = f32[32,8,128]{2,1,0:T(8,128)S(1)} all-to-all(f32[32,8,128]{2,1,0:T(8,128)S(1)} %bitcast.186), channel_id=1, replica_groups=mesh['grp'=8,'near'=2,'col'=2] {'grp','near','col'}, dimensions={0} | all-to-all | bytes 262144 | tf_op jit(solution)/shard_map/all_to_all | solution.py:388
  42.9 14.9 %shard_map.434 = f32[32,4,32,128]{3,2,1,0:T(8,128)} custom-call(s32[8192]{0:T(1024)S(1)} %convert_element_type.49.idx_ref, f32[16384,512]{1,0:T(8,128)} %refs_0_.7), custom_call_target="tpu_custom_call" | custom-call | bytes 67108864 | tf_op jit(solution)/shard_map/pallas_call | solution.py:91
  57.8 5.0 %all-to-all-start.1 = ((f32[32,128,128]{2,1,0:T(8,128)}), f32[32,128,128]{2,1,0:T(8,128)S(1)}, u32[]{:S(2)}, u32[]{:S(2)}) async-start(f32[32,128,128]{2,1,0:T(8,128)} %bitcast.7), calls=%async_computation.1 | async-start | bytes 4194304 | tf_op jit(solution)/shard_map/all_to_all | solution.py:425
  63.4 90.2 %all-to-all-done.1 = f32[32,128,128]{2,1,0:T(8,128)S(1)} async-done(((f32[32,128,128]{2,1,0:T(8,128)}), f32[32,128,128]{2,1,0:T(8,128)S(1)}, u32[]{:S(2)}, u32[]{:S(2)}) %all-to-all-start.1) | async-done | bytes 2097184 | tf_op jit(solution)/shard_map/all_to_all | solution.py:425
  156.4 11.7 %collective-permute-done = f32[128,1024]{1,0:T(8,128)S(1)} collective-permute-done((f32[128,1024]{1,0:T(8,128)S(1)}, f32[128,1024]{1,0:T(8,128)S(1)}, u32[]{:S(2)}, u32[]{:S(2)}) %collective-permute-start) | collective-permute-done | bytes 524320 | tf_op jit(solution)/shard_map/ppermute | solution.py:287
  179.1 7.3 %fusion.6 = (f32[512,1024]{1,0:T(8,128)S(1)}, f32[512,1024]{1,0:T(8,128)}) fusion(f32[1024]{0:T(1024)S(1)} %bitcast.200, f32[1024,1024]{1,0:T(8,128)S(1)} %bitcast.156, f32[256,1024]{1,0:T(8,128)} %collective-permute-done.1, f32[128,1024]{1,0:T(8,128)S(1)} %copy-done.11, f32[128,1024]{1,0:T(8,128)S(1)} %shard_map.435), kind=kOutput, calls=%fused_computation.11 | convolution fusion | flops 3226992640 | bytes 10489856 | tf_op jit(solution)/shard_map/dot_general | solution.py:319
  204.7 6.6 %collective-permute-done.6 = f32[128,384]{0,1:T(8,128)S(1)} collective-permute-done((f32[128,384]{0,1:T(8,128)S(1)}, f32[128,384]{0,1:T(8,128)S(1)}, u32[]{:S(2)}, u32[]{:S(2)}) %collective-permute-start.6) | collective-permute-done | bytes 196640 | tf_op jit(solution)/shard_map/ppermute | solution.py:287
  220.2 4.0 fusion.29
  225.5 3.7 fusion.106
  237.0 5.1 %fusion.30 = f32[1024,1024]{1,0:T(8,128)S(1)} fusion(f32[512,1024]{1,0:T(8,128)S(1)} %get-tuple-element.178, f32[256,1024]{1,0:T(8,128)} %collective-permute-done.1, f32[128,1024]{1,0:T(8,128)S(1)} %copy-done.12, f32[128,1024]{1,0:T(8,128)S(1)} %shard_map.435), kind=kOutput, calls=%fused_computation.90 | convolution fusion | flops 3222274048 | bytes 8388608 | tf_op jit(solution)/shard_map/dot_general | solution.py:319
  249.1 5.6 %constant_dynamic-slice_fusion.8 = f32[1024,5,2]{2,1,0:T(8,128)} fusion(f32[1024,5,8]{2,1,0:T(8,128)} %reshape_reshape.3, s32[]{:T(128)S(6)} %select_n.72), kind=kLoop, calls=%fused_computation.186 | loop fusion | bytes 81924 | tf_op jit(solution)/shard_map/dynamic_slice | solution.py:418
  257.5 5.7 %fusion.108 = f32[512,1024]{1,0:T(8,128)S(1)} fusion(f32[512,1024]{1,0:T(8,128)S(1)} %get-tuple-element.178, f32[1024,1024]{1,0:T(8,128)} %bitcast.157), kind=kOutput, calls=%fused_computation.225 | convolution fusion | flops 3221225472 | bytes 8388608 | tf_op jit(solution)/shard_map/dot_general | solution.py:319
  267.6 13.9 %collective-permute-done.9 = f32[128,1024]{1,0:T(8,128)S(1)} collective-permute-done((f32[128,1024]{1,0:T(8,128)S(1)}, f32[128,1024]{1,0:T(8,128)S(1)}, u32[]{:S(2)}, u32[]{:S(2)}) %collective-permute-start.9) | collective-permute-done | bytes 524320 | tf_op jit(solution)/shard_map/ppermute | solution.py:287
  281.6 3.3 shard_map.436
  291.4 16.0 %all-to-all-done.3.grad_ref = f32[32,32,128]{2,1,0:T(8,128)S(1)} async-done(((f32[32,32,128]{2,1,0:T(8,128)}), f32[32,32,128]{2,1,0:T(8,128)S(1)}, u32[]{:S(2)}, u32[]{:S(2)}) %all-to-all-start.3) | async-done | bytes 524320 | tf_op jit(solution)/shard_map/all_to_all | solution.py:521
  307.4 3.5 all-to-all-start.2
  311.0 20.0 %shard_map.437 = (f32[16384,512]{1,0:T(8,128)}, f32[16384,512]{1,0:T(8,128)}, f32[16384,512]{1,0:T(8,128)}, f32[32,32,128]{2,1,0:T(8,128)}) custom-call(s32[8192]{0:T(1024)S(1)} %convert_element_type.49.idx_ref, f32[32,32,128]{2,1,0:T(8,128)S(1)} %all-to-all-done.3.grad_ref, f32[16384,512]{1,0:T(8,128)} %refs_0_.7, ...), custom_call_target="tpu_custom_call", output_to_operand_aliasing={{3}: (5, {})} | custom-call | flops 62914560 | bytes 50331648 | tf_op jit(solution)/shard_map/pallas_call | solution.py:257
  331.6 5.2 %all-to-all-start.5 = ((f32[32,32,128]{2,1,0:T(8,128)}), f32[32,32,128]{2,1,0:T(8,128)S(1)}, u32[]{:S(2)}, u32[]{:S(2)}) async-start(f32[32,32,128]{2,1,0:T(8,128)} %get-tuple-element.49), calls=%async_computation.5 | async-start | bytes 1048576 | tf_op jit(solution)/shard_map/all_to_all | solution.py:529
  337.3 19.1 %shard_map.438 = (f32[16384,512]{1,0:T(8,128)}, f32[16384,512]{1,0:T(8,128)}, f32[16384,512]{1,0:T(8,128)}, f32[32,32,128]{2,1,0:T(8,128)}) custom-call(s32[8192]{0:T(1024)S(1)} %convert_element_type.49.idx_ref, f32[32,48,128]{2,1,0:T(8,128)S(1)} %all-to-all-done.2.grad_ref, ...), custom_call_target="tpu_custom_call", output_to_operand_aliasing={{0}: (5, {}), {1}: (6, {}), {2}: (7, {}), {3}: (8, {})} | custom-call | flops 62914560 | bytes 50331648 | tf_op jit(solution)/shard_map/pallas_call | solution.py:257
  357.0 16.0 %reduce-scatter.2.cloned.1.call-done = f32[4,40,1024]{2,1,0:T(8,128)} async-done(((f32[32,40,1024]{2,1,0:T(8,128)}), f32[4,40,1024]{2,1,0:T(8,128)}) %reduce-scatter.2.cloned.1.call-update) | async-done | bytes 655376 | tf_op jit(solution)/shard_map/reduce_scatter | solution.py:489
  374.4 3.9 all-to-all-start.4
  382.3 20.0 %shard_map.439 = (f32[16384,512]{1,0:T(8,128)}, f32[16384,512]{1,0:T(8,128)}, f32[16384,512]{1,0:T(8,128)}) custom-call(s32[8192]{0:T(1024)S(1)} %convert_element_type.49.idx_ref, f32[32,32,128]{2,1,0:T(8,128)S(1)} %all-to-all-done.5.grad_ref, f32[16384,512]{1,0:T(8,128)} %refs_0_.7, ...), custom_call_target="tpu_custom_call", output_to_operand_aliasing={{0}: (5, {}), {1}: (6, {}), {2}: (7, {})} | custom-call | flops 62914560 | bytes 50331648 | tf_op jit(solution)/shard_map/pallas_call | solution.py:257
  402.3 20.0 %shard_map.440 = (f32[16384,512]{1,0:T(8,128)}, f32[16384,512]{1,0:T(8,128)}, f32[16384,512]{1,0:T(8,128)}) custom-call(s32[8192]{0:T(1024)S(1)} %convert_element_type.49.idx_ref, f32[32,32,128]{2,1,0:T(8,128)S(1)} %all-to-all-done.4.grad_ref, f32[16384,512]{1,0:T(8,128)} %refs_0_.7, ...), custom_call_target="tpu_custom_call", output_to_operand_aliasing={{0}: (5, {}), {1}: (6, {}), {2}: (7, {})} | custom-call | flops 62914560 | bytes 50331648 | tf_op jit(solution)/shard_map/pallas_call | solution.py:257
  (283 shorter events, 99.1 us)
Async XLA Ops:
  7.2 162.7 %all-gather.2.cloned.1.call-start = ((), (), s32[]{:S(2)}) async-start(), calls=%async_computation.7 | async-start | bytes 5898240 | tf_op jit(solution)/shard_map/all_gather | solution.py:411
  9.7 1.8 collective-permute-start.2
  11.5 10.9 %collective-permute-start.3 = (f32[2,40,1024]{2,1,0:T(8,128)S(1)}, f32[2,40,1024]{2,1,0:T(8,128)S(1)}, u32[]{:S(2)}, u32[]{:S(2)}) collective-permute-start(f32[2,40,1024]{2,1,0:T(8,128)S(1)} %pad_maximum_fusion.12), channel_id=1, source_target_pairs={{0,2},{2,0},{1,3},{3,1},{4,6},{6,4},{5,7},{7,5},{8,10},{10,8},{9,1... | collective-permute-start | bytes 983048 | tf_op jit(solution)/shard_map/ppermute | solution.py:287
  57.8 95.8 %all-to-all-start.1 = ((f32[32,128,128]{2,1,0:T(8,128)}), f32[32,128,128]{2,1,0:T(8,128)S(1)}, u32[]{:S(2)}, u32[]{:S(2)}) async-start(f32[32,128,128]{2,1,0:T(8,128)} %bitcast.7), calls=%async_computation.1 | async-start | bytes 4194304 | tf_op jit(solution)/shard_map/all_to_all | solution.py:425
  62.8 310.2 %reduce-scatter.2.cloned.1.call-start = ((), (), s32[]{:S(2)}) async-start(), calls=%async_computation.8 | async-start | bytes 5898240 | tf_op jit(solution)/shard_map/reduce_scatter | solution.py:489
  154.8 13.2 %collective-permute-start = (f32[128,1024]{1,0:T(8,128)S(1)}, f32[128,1024]{1,0:T(8,128)S(1)}, u32[]{:S(2)}, u32[]{:S(2)}) collective-permute-start(f32[128,1024]{1,0:T(8,128)S(1)} %shard_map.435), channel_id=1, source_target_pairs={{0,2},{2,0},{1,3},{3,1},{4,6},{6,4},{5,7},{7,5},{8,10},{10,8},{9,1... | collective-permute-start | bytes 1572872 | tf_op jit(solution)/shard_map/ppermute | solution.py:287
  169.2 3.3 collective-permute-start.1
  188.8 1.8 collective-permute-start.4
  192.1 8.4 %collective-permute-start.5 = (f32[128,320]{0,1:T(8,128)}, f32[128,320]{0,1:T(8,128)}, u32[]{:S(2)}, u32[]{:S(2)}) collective-permute-start(f32[128,320]{0,1:T(8,128)} %slice.185), channel_id=1, source_target_pairs={{0,2},{2,0},{1,3},{3,1},{4,6},{6,4},{5,7},{7,5},{8,10},{10,8},{9,1... | collective-permute-start | bytes 491528 | tf_op jit(solution)/shard_map/ppermute | solution.py:287
  204.3 7.0 %collective-permute-start.6 = (f32[128,384]{0,1:T(8,128)S(1)}, f32[128,384]{0,1:T(8,128)S(1)}, u32[]{:S(2)}, u32[]{:S(2)}) collective-permute-start(f32[128,384]{0,1:T(8,128)S(1)} %select_maximum_fusion.1), channel_id=1, source_target_pairs={{0,2},{2,0},{1,3},{3,1},{4,6},{6,4},{5,7},{7,5},{8,10},{10,8},{9,1... | collective-permute-start | bytes 589832 | tf_op jit(solution)/shard_map/ppermute | solution.py:287
  211.3 1.8 collective-permute-start.7
  264.5 2.7 collective-permute-start.8
  267.4 22.1 %copy-start.44 = (f32[320]{0:T(512)S(1)}, f32[320]{0:T(512)}, u32[]{:S(2)}) copy-start(f32[320]{0:T(512)} %get-tuple-element.175) | copy-start | bytes 3844
  267.4 22.3 %copy-start.43 = (f32[320]{0:T(512)S(1)}, f32[320]{0:T(512)}, u32[]{:S(2)}) copy-start(f32[320]{0:T(512)} %get-tuple-element.206) | copy-start | bytes 3844
  267.5 14.0 %collective-permute-start.9 = (f32[128,1024]{1,0:T(8,128)S(1)}, f32[128,1024]{1,0:T(8,128)S(1)}, u32[]{:S(2)}, u32[]{:S(2)}) collective-permute-start(f32[128,1024]{1,0:T(8,128)S(1)} %slice.191), channel_id=1, source_target_pairs={{0,2},{2,0},{1,3},{3,1},{4,6},{6,4},{5,7},{7,5},{8,10},{10,8},{9,1... | collective-permute-start | bytes 1572872 | tf_op jit(solution)/shard_map/ppermute | solution.py:287
  284.9 22.5 %all-to-all-start.3 = ((f32[32,32,128]{2,1,0:T(8,128)}), f32[32,32,128]{2,1,0:T(8,128)S(1)}, u32[]{:S(2)}, u32[]{:S(2)}) async-start(f32[32,32,128]{2,1,0:T(8,128)} %get-tuple-element.42), calls=%async_computation.3 | async-start | bytes 1048576 | tf_op jit(solution)/shard_map/all_to_all | solution.py:521
  307.4 24.2 %all-to-all-start.2 = ((f32[32,48,128]{2,1,0:T(8,128)}), f32[32,48,128]{2,1,0:T(8,128)S(1)}, u32[]{:S(2)}, u32[]{:S(2)}) async-start(f32[32,48,128]{2,1,0:T(8,128)} %pad_maximum_fusion.4), calls=%async_computation.2 | async-start | bytes 1572864 | tf_op jit(solution)/shard_map/all_to_all | solution.py:521
  331.6 42.8 %all-to-all-start.5 = ((f32[32,32,128]{2,1,0:T(8,128)}), f32[32,32,128]{2,1,0:T(8,128)S(1)}, u32[]{:S(2)}, u32[]{:S(2)}) async-start(f32[32,32,128]{2,1,0:T(8,128)} %get-tuple-element.49), calls=%async_computation.5 | async-start | bytes 1048576 | tf_op jit(solution)/shard_map/all_to_all | solution.py:529
  357.0 24.7 %copy-start.36 = (f32[8,512]{1,0:T(8,128)S(1)}, f32[8,512]{1,0:T(8,128)}, u32[]{:S(2)}) copy-start(f32[8,512]{1,0:T(8,128)} %param.39) | copy-start | bytes 49156
  357.0 24.7 %copy-start.41 = (f32[8,512]{1,0:T(8,128)S(1)}, f32[8,512]{1,0:T(8,128)}, u32[]{:S(2)}) copy-start(f32[8,512]{1,0:T(8,128)} %param.40) | copy-start | bytes 49156
  357.0 24.7 %copy-start.42 = (f32[8,512]{1,0:T(8,128)S(1)}, f32[8,512]{1,0:T(8,128)}, u32[]{:S(2)}) copy-start(f32[8,512]{1,0:T(8,128)} %param.41) | copy-start | bytes 49156
  374.3 4.7 %collective-permute-start.10 = (f32[2,40,1024]{2,1,0:T(8,128)S(1)}, f32[2,40,1024]{2,1,0:T(8,128)S(1)}, u32[]{:S(2)}, u32[]{:S(2)}) collective-permute-start(f32[2,40,1024]{2,1,0:T(8,128)S(1)} %pad_maximum_fusion.13), channel_id=1, source_target_pairs={{0,1},{1,0},{2,3},{3,2},{4,5},{5,4},{6,7},{7,6},{8,9},{9,8},{10,11... | collective-permute-start | bytes 983048 | tf_op jit(solution)/shard_map/ppermute | solution.py:291
  374.4 28.0 %all-to-all-start.4 = ((f32[32,32,128]{2,1,0:T(8,128)}), f32[32,32,128]{2,1,0:T(8,128)S(1)}, u32[]{:S(2)}, u32[]{:S(2)}) async-start(f32[32,32,128]{2,1,0:T(8,128)} %get-tuple-element.48), calls=%async_computation.4 | async-start | bytes 1048576 | tf_op jit(solution)/shard_map/all_to_all | solution.py:529
  379.1 43.3 %collective-permute-start.11 = (f32[2,40,1024]{2,1,0:T(8,128)S(1)}, f32[2,40,1024]{2,1,0:T(8,128)S(1)}, u32[]{:S(2)}, u32[]{:S(2)}) collective-permute-start(f32[2,40,1024]{2,1,0:T(8,128)S(1)} %pad_maximum_fusion.14), channel_id=1, source_target_pairs={{0,2},{2,0},{1,3},{3,1},{4,6},{6,4},{5,7},{7,5},{8,10},{10,8},{9,1... | collective-permute-start | bytes 983048 | tf_op jit(solution)/shard_map/ppermute | solution.py:287
  (49 other events, 282.9 us)
Sparse Core Ops, SparseCore 0:
  23.6 130.2 all-gather.1
  245.3 127.7 reduce-scatter.1

commit v2 on v1

v2 whole, which is shorter than its diff:
```python
import functools
import math

import jax
import jax.numpy as jnp
from jax import lax
from jax.experimental import pallas as pl
from jax.experimental.pallas import tpu as pltpu
from jax.sharding import Mesh
from jax.sharding import PartitionSpec as P

DIM = 64
STEP = 10
LANES = 128
MIB = 1024 * 1024

beta_one = 0.9
beta_two = 0.999
epsilon = 1e-08
decay_rate = 0.01
table_rate = 0.2
dense_rate = 0.02

ROW = ("hi", "near", "rest")
PEERS = ("hi", "rest")
ALL = ("hi", "near", "rest", "col")
SCALARS = pl.BlockSpec(memory_space=pltpu.SMEM)
WHOLE = pl.BlockSpec(memory_space=pltpu.VMEM)
ANYWHERE = pl.BlockSpec(memory_space=pl.ANY)


def adamw(weight, moment, square, gradient, rate):
    moment_next = beta_one * moment + (1.0 - beta_one) * gradient
    square_next = beta_two * square + (1.0 - beta_two) * gradient * gradient
    moment_hat = moment_next * (1.0 / (1.0 - beta_one**STEP))
    square_hat = square_next * (1.0 / (1.0 - beta_two**STEP))
    weight_next = weight - rate * (
        moment_hat / (jnp.sqrt(square_hat) + epsilon) + decay_rate * weight
    )
    return (weight_next, moment_next, square_next)


def table_adamw(weight, moment, square, gradient):
    root = math.sqrt(1.0 - beta_two**STEP)
    moment_next = beta_one * moment + (1.0 - beta_one) * gradient
    square_next = beta_two * square + (1.0 - beta_two) * (gradient * gradient)
    r = lax.rsqrt(square_next)
    below = 1.0 + (epsilon * root) * r
    near = pl.reciprocal(below, approx=True)
    near = near * (2.0 - below * near)
    ratio = (moment_next * r) * near
    weight_next = weight * (1.0 - table_rate * decay_rate) - ratio * (
        table_rate * root / (1.0 - beta_one**STEP)
    )
    return (weight_next, moment_next, square_next)


def fence(x, after):
    return pl.pallas_call(
        lambda *refs: None,
        out_shape=jax.ShapeDtypeStruct(x.shape, x.dtype),
        in_specs=[ANYWHERE] * (1 + len(after)),
        out_specs=ANYWHERE,
        input_output_aliases={0: 0},
        compiler_params=pltpu.CompilerParams(vmem_limit_bytes=MIB),
        cost_estimate=pl.CostEstimate(flops=0, bytes_accessed=0, transcendentals=0),
    )(x, *after)


def low_half():
    return lax.broadcasted_iota(jnp.int32, (1, LANES), 1) < DIM


def gather_kernel(rows, cols, devices, each, idx_ref, table_ref, out_ref, buf, sem):
    count = devices * each

    def fetch(u):
        return pltpu.make_async_copy(
            table_ref.at[:, pl.ds(u * LANES, LANES)], buf.at[u, pl.ds(0, rows)], sem.at[u]
        )

    for u in range(cols):
        fetch(u).start()
        buf[u, pl.ds(rows, 8), :] = jnp.zeros((8, LANES), jnp.float32)
    low = low_half()
    for u in range(cols):
        fetch(u).wait()

        def step(d, carry):
            base = d * each
            for k in range(each):
                first = idx_ref[2 * u * count + base + k]
                second = idx_ref[(2 * u + 1) * count + base + k]
                out_ref[d, u, pl.ds(k, 1), :] = jnp.where(
                    low, buf[u, pl.ds(first, 1), :], buf[u, pl.ds(second, 1), :]
                )
            return carry

        lax.fori_loop(0, devices, step, 0)


def gather_rows(idx, table, devices, each):
    rows, width = table.shape
    cols = width // LANES
    return pl.pallas_call(
        functools.partial(gather_kernel, rows, cols, devices, each),
        out_shape=jax.ShapeDtypeStruct((devices, cols, each, LANES), jnp.float32),
        in_specs=[SCALARS, ANYWHERE],
        out_specs=WHOLE,
        scratch_shapes=[
            pltpu.VMEM((cols, rows + 8, LANES), jnp.float32),
            pltpu.SemaphoreType.DMA((cols,)),
        ],
        compiler_params=pltpu.CompilerParams(vmem_limit_bytes=35 * MIB),
        cost_estimate=pl.CostEstimate(
            flops=0, bytes_accessed=2 * rows * width * 4, transcendentals=0
        ),
    )(idx, table)


def pool_kernel(pieces, halves, cols, each, place, shift_ref, peer_ref, in_ref, before, out_ref):
    low = low_half()
    stripe, spot = place
    for c in range(halves):
        for u in range(cols):
            shifts = [shift_ref[c * 2 * cols + 2 * u + h] for h in range(2)]
            bags = []
            for a in range(pieces // 4):
                sums = []
                for s in shifts:
                    total = None
                    for j in range(4):
                        part = in_ref[lax.rem(4 * a + j + s, pieces), c, u]
                        total = part if total is None else total + part
                    sums.append(total)
                bags.append(jnp.where(low, sums[0], sums[1]))
            at = (c * cols + u) * LANES
            block = jnp.concatenate(bags, axis=0).T
            for k in range(LANES // stripe):
                to = pl.multiple_of(spot(at // stripe + k, peer_ref[0]) * stripe, stripe)
                out_ref[pl.ds(to, stripe), :] = block[k * stripe : (k + 1) * stripe]


def pool(shifts, peer, place, arrived, before):
    pieces, halves, cols, each, _ = arrived.shape
    return pl.pallas_call(
        functools.partial(pool_kernel, pieces, halves, cols, each, place),
        out_shape=jax.ShapeDtypeStruct(
            (halves * cols * LANES, pieces // 4 * each), jnp.float32
        ),
        in_specs=[SCALARS, SCALARS, WHOLE, ANYWHERE],
        out_specs=WHOLE,
        compiler_params=pltpu.CompilerParams(vmem_limit_bytes=8 * MIB),
    )(shifts, peer, arrived, before)


def spread_kernel(terms, pieces, halves, cols, each, place, shift_ref, peer_ref, *refs):
    low = low_half()
    stripe, spot = place
    in_refs, out_refs, rows = refs[:terms], refs[terms:-1], refs[-1]
    for c in range(halves):
        for u in range(cols):
            shifts = [shift_ref[c * 2 * cols + 2 * u + h] for h in range(2)]
            at = (c * cols + u) * LANES
            block = []
            for k in range(LANES // stripe):
                where = pl.multiple_of(spot(at // stripe + k, peer_ref[0]) * stripe, stripe)
                block.append(sum(ref[pl.ds(where, stripe), :] for ref in in_refs))
            rows[c * cols + u] = jnp.concatenate(block, axis=0).T
            for r in range(pieces):
                parts = []
                for s in shifts:
                    place = lax.rem(r - s + pieces, pieces) // 4
                    start = pl.multiple_of(place * each, each)
                    parts.append(rows[c * cols + u, pl.ds(start, each), :])
                out_refs[u][halves * r + c] = jnp.where(low, parts[0], parts[1])


def spread(shifts, peer, place, terms, pieces, halves):
    width, samples = terms[0].shape
    cols = width // halves // LANES
    each = samples * 4 // pieces
    return pl.pallas_call(
        functools.partial(spread_kernel, len(terms), pieces, halves, cols, each, place),
        out_shape=[
            jax.ShapeDtypeStruct((pieces * halves, each, LANES), jnp.float32)
        ]
        * cols,
        in_specs=[SCALARS, SCALARS] + [WHOLE] * len(terms),
        out_specs=[WHOLE] * cols,
        scratch_shapes=[pltpu.VMEM((width // LANES, samples, LANES), jnp.float32)],
        compiler_params=pltpu.CompilerParams(vmem_limit_bytes=10 * MIB),
    )(shifts, peer, *terms)


def update_kernel(rows, part, devices, each, block, outs, idx_ref, grad_ref, *refs):
    sources, targets = refs[:3], refs[-7 - outs : -4 - outs]
    bufs, sums, in_sem, out_sem = refs[-7:-4], refs[-4:-2], refs[-2], refs[-1]
    count = devices * each
    blocks = rows // block
    columns = pl.ds(part * LANES, LANES)

    def fetch(b, k):
        at = pl.ds(b * block, block)
        return pltpu.make_async_copy(
            sources[k].at[at, columns], bufs[k].at[at], in_sem.at[k, b]
        )

    def store(b, k):
        at = pl.ds(b * block, block)
        return pltpu.make_async_copy(
            bufs[k].at[at], targets[k].at[at, columns], out_sem.at[k, b]
        )

    for b in range(blocks):
        for k in range(3):
            fetch(b, k).start()

    def clear(i, carry):
        at = pl.ds(pl.multiple_of(i * 64, 64), 64)
        for s in sums:
            s[at, :] = jnp.full((64, LANES), jnp.inf, jnp.float32)
        return carry

    lax.fori_loop(0, rows // 64, clear, 0)
    for s in sums:
        s[pl.ds(rows, 8), :] = jnp.full((8, LANES), jnp.inf, jnp.float32)

    def step(d, carry):
        for k in range(each):
            value = grad_ref[d, pl.ds(k, 1), :]
            for q in range(2):
                row = pl.ds(idx_ref[(2 * part + q) * count + d * each + k], 1)
                old = sums[q][row, :]
                sums[q][row, :] = value + jnp.where(old < jnp.inf, old, 0.0)
        return carry

    lax.fori_loop(0, devices, step, 0)

    low = low_half()
    tile = 128
    for b in range(blocks):
        for k in range(3):
            fetch(b, k).wait()

        def renew(i, carry):
            at = pl.ds(pl.multiple_of(b * block + i * tile, tile), tile)
            total = jnp.where(low, sums[0][at, :], sums[1][at, :])
            old = [buf[at, :] for buf in bufs]
            new = table_adamw(*old, total)
            hit = total < jnp.inf
            for k in range(3):
                bufs[k][at, :] = jnp.where(hit, new[k], old[k])
            return carry

        lax.fori_loop(0, block // tile, renew, 0)
        for k in range(3):
            store(b, k).start()
    for b in range(blocks):
        for k in range(3):
            store(b, k).wait()


def update_part(idx, grads, tables, part, each, previous, through, before):
    rows, width = tables[0].shape
    devices = grads.shape[0]
    block = rows // 8
    extra = [] if previous is None else list(previous)
    place = pl.BlockSpec(memory_space=pl.ANY)
    handed = extra + list(through)
    first = 0 if extra else 3
    outs = 3 + len(through)
    done = pl.pallas_call(
        functools.partial(update_kernel, rows, part, devices, each, block, outs),
        out_shape=[jax.ShapeDtypeStruct((rows, width), jnp.float32)] * 3
        + [jax.ShapeDtypeStruct(x.shape, x.dtype) for x in through],
        in_specs=[SCALARS, WHOLE] + [place] * (3 + len(handed) + len(before)),
        out_specs=[place] * outs,
        input_output_aliases={5 + k: first + k for k in range(len(handed))},
        scratch_shapes=[pltpu.VMEM((rows, LANES), jnp.float32)] * 3
        + [pltpu.VMEM((rows + 8, LANES), jnp.float32)] * 2
        + [pltpu.SemaphoreType.DMA((3, rows // block))] * 2,
        compiler_params=pltpu.CompilerParams(vmem_limit_bytes=42 * MIB),
        cost_estimate=pl.CostEstimate(
            flops=30 * rows * LANES, bytes_accessed=rows * LANES * 24, transcendentals=0
        ),
    )(idx, grads, *tables, *handed, *before)
    return done[:3], list(done[3:])


GELU_SCALE = math.sqrt(2.0 / math.pi)


def gelu(a):
    return 0.5 * a * (1.0 + jnp.tanh(GELU_SCALE * (a + 0.044715 * (a * a * a))))


def gelu_slope(a):
    square = a * a
    t = jnp.tanh(GELU_SCALE * a * (1.0 + 0.044715 * square))
    return 0.5 * (1.0 + t) + (0.5 * GELU_SCALE) * a * (1.0 - t * t) * (
        1.0 + (3.0 * 0.044715) * square
    )


def split(x):
    high = x.astype(jnp.bfloat16)
    return high, (x - high.astype(jnp.float32)).astype(jnp.bfloat16)


def product(a, b, flip=False):
    dims = (((1,), (1 if flip else 0,)), ((), ()))

    def one(x, y):
        return lax.dot_general(x, y, dims, preferred_element_type=jnp.float32)

    return one(a[0], b[0]) + (one(a[0], b[1]) + one(a[1], b[0]))


TOWER_LANES = 384
GATE_LANES = 64


def pack_rows(tower, gate, width):
    def eights(x, lanes):
        x = jnp.pad(x, ((0, -x.shape[0] % 8), (0, lanes - x.shape[1])))
        return x.reshape(-1, 8, lanes).swapaxes(0, 1).reshape(8, -1)

    return padded(
        jnp.concatenate([eights(tower, TOWER_LANES), eights(gate, GATE_LANES)], axis=1), width
    )


def unpack_rows(x, tower_shape, gate_shape):
    def rows(x, shape, lanes):
        x = x.reshape(8, -1, lanes).swapaxes(0, 1).reshape(-1, lanes)
        return x[: shape[0], : shape[1]]

    cut = -(-tower_shape[0] // 8) * TOWER_LANES
    end = cut + gate_shape[0] // 8 * GATE_LANES
    return rows(x[:, :cut], tower_shape, TOWER_LANES), rows(x[:, cut:end], gate_shape, GATE_LANES)


def tower_row(order, peer_ref, number, member, tower_depth):
    rest, counted = order
    place = number ^ peer_ref[0] if counted else number
    device = ((place // rest * 2 + member // 2) * rest + place % rest) * 2 + member % 2
    row = device * tower_depth
    return pl.multiple_of(row, tower_depth) if counted else row


def split_kernel(depth, tower_depth, order, pieces, peer_ref, *refs):
    outs = refs[pieces : -3 - pieces]
    piece_refs, (tower, gate, sem) = refs[-3 - pieces : -3], refs[-3:]
    loads = [
        pltpu.make_async_copy(refs[k], piece_refs[k], sem.at[k]) for k in range(pieces)
    ]
    for load in loads:
        load.start()

    def put(k, at, value):
        high, low = split(value)
        outs[k][at] = high
        outs[k + 1][at] = low

    block = 0
    gate_at = -(-tower_depth // 8) * TOWER_LANES
    gate[...] = jnp.zeros(gate.shape, jnp.float32)
    for load, ref in zip(loads, piece_refs):
        load.wait()
        step = min(LANES // depth, ref.shape[0])
        for b in range(0, ref.shape[0], step):
            rows = slice((block + b) * depth, (block + b + step) * depth)
            put(0, (rows, slice(None)), ref[b : b + step, :depth, :].reshape(-1, ref.shape[2]))
        for b in range(ref.shape[0]):
            number, member = (block + b) // 4, (block + b) % 4
            row = tower_row(order, peer_ref, number, member, tower_depth)
            for k in range(0, tower_depth, 8):
                high = min(8, tower_depth)
                at = k // 8 * TOWER_LANES
                tower[pl.ds(row + k, high), :] = ref[
                    b, depth : depth + high, at : at + TOWER_LANES
                ]
            for k in range(0, depth, LANES // GATE_LANES * 8):
                at = gate_at + k // 8 * GATE_LANES
                both = ref[b, depth : depth + 8, at : at + LANES]
                row = (block + b) * depth + k
                gate[row : row + 8, :GATE_LANES] = both[:, :GATE_LANES]
                if k + 8 < depth:
                    gate[row + 8 : row + 16, :GATE_LANES] = both[:, GATE_LANES:]
        block += ref.shape[0]
    for b in range(outs[0].shape[0] // LANES):
        rows = slice(b * LANES, (b + 1) * LANES)
        for k in range(2):
            turned = outs[k][rows, :].astype(jnp.float32).T
            outs[2 + k][:, rows] = turned.astype(jnp.bfloat16)
    width = outs[4].shape[1]
    put(4, Ellipsis, tower[:, :width])
    put(6, Ellipsis, gate[:, :GATE_LANES])
    put(8, Ellipsis, tower[...].T[:width])
    put(10, Ellipsis, gate[...].T[:GATE_LANES])


def split_weights(pieces, peer, order, depth, tower_depth, tower_width):
    lots = pieces[0].shape[2]
    devices = sum(x.shape[0] for x in pieces)
    width = devices * depth
    height = devices * tower_depth
    shapes = [(width, lots), (lots, width), (height, tower_width), (width, GATE_LANES)]
    shapes += [shapes[2][::-1], shapes[3][::-1]]
    return pl.pallas_call(
        functools.partial(split_kernel, depth, tower_depth, order, len(pieces)),
        out_shape=[
            jax.ShapeDtypeStruct(shape, jnp.bfloat16) for shape in shapes for _ in range(2)
        ],
        in_specs=[SCALARS] + [ANYWHERE] * len(pieces),
        out_specs=[WHOLE] * 12,
        scratch_shapes=[pltpu.VMEM(x.shape, x.dtype) for x in pieces]
        + [
            pltpu.VMEM((height, TOWER_LANES), jnp.float32),
            pltpu.VMEM((width, LANES), jnp.float32),
            pltpu.SemaphoreType.DMA((len(pieces),)),
        ],
        compiler_params=pltpu.CompilerParams(vmem_limit_bytes=16 * MIB),
    )(peer, *pieces)


def forward_kernel(dims, member_ref, *refs):
    tasks, experts, mine, hidden_units, tower_units = dims
    x_refs, refs = refs[:2], refs[2:]
    weight, tower, gate = [(refs[2 * k], refs[2 * k + 1]) for k in range(3)]
    bias_ref, pre_ref, prob_ref, upper_ref, part_ref, x_high, x_low, hid_ref = refs[6:]
    for k in range(2):
        at = slice(k * LANES, (k + 1) * LANES)
        x_high[:, at], x_low[:, at] = split(x_refs[k][...])
    lots = pre_ref.shape[0]
    tile = 256

    def rows(i, carry):
        at = pl.ds(pl.multiple_of(i * tile, tile), tile)
        pre = product([w[at, :] for w in weight], [x_high[...], x_low[...]]) + bias_ref[at, :]
        pre_ref[at, :] = pre
        hid_ref[at, :] = gelu(pre)
        return carry

    lax.fori_loop(0, lots // tile, rows, 0)
    logits = product([g[...] for g in gate], [x_high[...], x_low[...]])
    total = logits.shape[1]
    logits = logits[: tasks * experts].reshape(tasks, experts, total)
    grown = jnp.exp(logits - jnp.max(logits, axis=1, keepdims=True))
    probs = grown / jnp.sum(grown, axis=1, keepdims=True)
    prob_ref[...] = probs.reshape(tasks * experts, total)
    which = lax.broadcasted_iota(jnp.int32, probs.shape, 1)
    part = jnp.zeros((tasks, tower_units, total), jnp.float32)
    for i in range(mine):
        own = jnp.sum(
            jnp.where(which == member_ref[0] * mine + i, probs, 0.0), axis=1, keepdims=True
        )
        hidden = hid_ref[i * hidden_units : (i + 1) * hidden_units, :]
        upper = product([t[...] for t in tower], split(hidden))
        upper_ref[i] = upper
        part = part + own * upper.reshape(tasks, tower_units, total)
    part = part.reshape(tasks * tower_units, total)
    part_ref[0] = part[:, :LANES]
    part_ref[1] = part[:, LANES:]


def forward(dims, member, xs, weight, tower, gate, bias):
    tasks, experts, mine, hidden_units, tower_units = dims
    lots = mine * hidden_units
    width = tasks * tower_units
    total = 2 * LANES
    shapes = [
        (lots, total),
        (tasks * experts, total),
        (mine, width, total),
        (2, width, LANES),
    ]
    return pl.pallas_call(
        functools.partial(forward_kernel, dims),
        out_shape=[jax.ShapeDtypeStruct(shape, jnp.float32) for shape in shapes],
        in_specs=[SCALARS] + [WHOLE] * 9,
        out_specs=[WHOLE] * 4,
        scratch_shapes=[pltpu.VMEM((xs[0].shape[0], total), jnp.bfloat16)] * 2
        + [pltpu.VMEM((lots, total), jnp.float32)],
        compiler_params=pltpu.CompilerParams(vmem_limit_bytes=16 * MIB),
        cost_estimate=pl.CostEstimate(
            flops=8 * lots * xs[0].shape[0] * total,
            bytes_accessed=12 * MIB,
            transcendentals=lots * total,
        ),
    )(member, *xs, *weight, *tower, *gate, bias)


def score_kernel(
    tasks, total_ref, first_ref, second_ref, bias_ref, out_ref, last_ref, keep_ref, target_ref,
    packed_ref, grad_out_ref, grad_bias_ref, small_ref,
):
    mixed = first_ref[...] + second_ref[...]
    width, samples = mixed.shape

    def by_task(x):
        return x.reshape(tasks, width // tasks, samples)

    inner = mixed + bias_ref[...]
    upper = gelu(inner)
    keep = keep_ref[...]
    targets = target_ref[...]
    score = jnp.sum(by_task(upper * out_ref[...]), axis=1) + last_ref[...]
    faded = jnp.exp(-jnp.abs(score))
    softplus = jnp.maximum(score, 0.0) + jnp.log1p(faded)
    sigmoid = jnp.where(score >= 0.0, 1.0, faded) / (1.0 + faded)
    d_score = keep * (sigmoid - targets) / total_ref[0]
    wide = jnp.broadcast_to(d_score[:, None, :], by_task(mixed).shape).reshape(width, samples)
    d_inner = wide * out_ref[...] * gelu_slope(inner)
    packed_ref[:width, :] = d_inner
    mean = jnp.sum(by_task(d_inner * mixed), axis=1)
    packed_ref[width:, :] = jnp.concatenate(
        [mean, jnp.zeros((packed_ref.shape[0] - width - tasks, samples), jnp.float32)], axis=0
    )
    grad_out_ref[...] = jnp.sum(wide * upper, axis=1, keepdims=True)
    grad_bias_ref[...] = jnp.sum(d_inner, axis=1, keepdims=True)
    small_ref[0] = jnp.sum(d_score, axis=1, keepdims=True)
    small_ref[1] = jnp.sum(keep * (softplus - targets * score), axis=1, keepdims=True)


def score_step(tasks, weight_total, first, second, bias, out, last, keep, targets):
    width, samples = first.shape
    shapes = [(-(-(width + tasks) // 8) * 8, samples), (width, 1), (width, 1), (2, tasks, 1)]
    return pl.pallas_call(
        functools.partial(score_kernel, tasks),
        out_shape=[jax.ShapeDtypeStruct(shape, jnp.float32) for shape in shapes],
        in_specs=[SCALARS] + [WHOLE] * 7,
        out_specs=[WHOLE] * 4,
        compiler_params=pltpu.CompilerParams(vmem_limit_bytes=8 * MIB),
    )(weight_total, first, second, bias, out, last, keep, targets)


def backward_kernel(dims, member_ref, *refs):
    tasks, experts, mine, hidden_units, tower_units = dims
    width = tasks * tower_units
    packed_refs, refs = refs[:2], refs[2:]
    pre_ref, prob_ref, upper_ref = refs[:3]
    weight, tower, gate = [(refs[3 + 2 * k], refs[4 + 2 * k]) for k in range(3)]
    d_pre_ref, spread_ref, logit_ref, near_ref, far_ref, high_ref, low_ref = refs[9:]
    total = 2 * LANES
    packed = jnp.concatenate([ref[...] for ref in packed_refs], axis=1)
    d_inner = packed[:width].reshape(tasks, tower_units, total)
    mean = packed[width : width + 8].reshape(1, 8, total)[0][:tasks]
    probs = prob_ref[...].reshape(tasks, experts, total)
    which = lax.broadcasted_iota(jnp.int32, probs.shape, 1)
    d_logits = jnp.zeros(probs.shape, jnp.float32)
    for i in range(mine):
        chosen = which == member_ref[0] * mine + i
        own = jnp.sum(jnp.where(chosen, probs, 0.0), axis=1, keepdims=True)
        d_prob = jnp.sum(d_inner * upper_ref[i].reshape(d_inner.shape), axis=1)
        d_logit = own * (d_prob - mean)[:, None, :]
        d_logits = jnp.where(chosen, d_logit, d_logits)
        spreads = (d_inner * own).reshape(width, total)
        spread_ref[i] = spreads
        at = slice(i * hidden_units, (i + 1) * hidden_units)
        d_hidden = product([t[...] for t in tower], split(spreads))
        d_pre = d_hidden * gelu_slope(pre_ref[at, :])
        d_pre_ref[at, :] = d_pre
        high_ref[at, :], low_ref[at, :] = split(d_pre)
    d_logits = d_logits.reshape(tasks * experts, total)
    d_logits = jnp.concatenate(
        [d_logits, jnp.zeros((GATE_LANES - tasks * experts, total), jnp.float32)], axis=0
    )
    logit_ref[...] = d_logits
    d_logits = split(d_logits)
    tile = 256

    def rows(i, carry):
        at = pl.ds(pl.multiple_of(i * tile, tile), tile)
        value = product([w[at, :] for w in weight], [high_ref[...], low_ref[...]])
        value = value + product([g[at, :] for g in gate], d_logits)
        near_ref[at, :] = value[:, :LANES]
        far_ref[at, :] = value[:, LANES:]
        return carry

    lax.fori_loop(0, near_ref.shape[0] // tile, rows, 0)


def backward(dims, member, packed, pre, probs, upper, weight, tower, gate):
    tasks, experts, mine, hidden_units, tower_units = dims
    lots = mine * hidden_units
    depth = weight[0].shape[0]
    total = 2 * LANES
    shapes = [
        (lots, total),
        (mine, tasks * tower_units, total),
        (GATE_LANES, total),
        (depth, LANES),
        (depth, LANES),
    ]
    return pl.pallas_call(
        functools.partial(backward_kernel, dims),
        out_shape=[jax.ShapeDtypeStruct(shape, jnp.float32) for shape in shapes],
        in_specs=[SCALARS] + [WHOLE] * 11,
        out_specs=[WHOLE] * 5,
        scratch_shapes=[pltpu.VMEM((lots, total), jnp.bfloat16)] * 2,
        compiler_params=pltpu.CompilerParams(vmem_limit_bytes=16 * MIB),
        cost_estimate=pl.CostEstimate(
            flops=8 * lots * depth * total, bytes_accessed=12 * MIB, transcendentals=lots * total
        ),
    )(member, *packed, pre, probs, upper, *weight, *tower, *gate)


def gradient_kernel(dims, depth, tower_depth, order, outs, peer_ref, *refs):
    mine, hidden_units = dims
    logits, sources, refs = refs[:2], refs[2:12], refs[13:]
    weight_refs, bias_ref, refs = refs[:outs], refs[outs], refs[outs + 1 :]
    held, (x_high, x_low, d_high, d_low, tower, in_sem) = refs[:10], refs[10:]
    loads = [pltpu.make_async_copy(sources[k], held[k], in_sem.at[k]) for k in range(10)]
    for load in loads:
        load.start()
    lots = d_high.shape[0]
    tile = LANES
    share = tile // depth
    tiles = x_high.shape[0] // tile
    gate_at = -(-tower_depth // 8) * TOWER_LANES
    gate_end = gate_at + depth // 8 * GATE_LANES
    for k in range(4):
        at = slice(k * LANES, (k + 1) * LANES)
        loads[k].wait()
        x_high[:, at], x_low[:, at] = split(held[k][...])
    bias = None
    for k in range(2):
        at = slice(2 * k * LANES, 2 * (k + 1) * LANES)
        loads[4 + k].wait()
        value = held[4 + k][...]
        d_high[:, at], d_low[:, at] = split(value)
        part = jnp.sum(value, axis=1, keepdims=True)
        bias = part if bias is None else bias + part
    bias_ref[...] = bias
    for k in range(6, 10):
        loads[k].wait()

    def parts(i):
        if outs == 1:
            return [(weight_refs[0], (), i * share, share)]
        high, middle, low = i // 4, i // 2 % 2, i % 2
        return [(weight_refs[low], (high, middle), 0, 2), (weight_refs[2 + middle], (high, low), 0, 2)]

    wide = 256

    def columns(n, carry):
        at = pl.ds(pl.multiple_of(n * wide, wide), wide)
        value = product([x_high[...], x_low[...]], [d_high[at, :], d_low[at, :]], True)
        for i in range(tiles):
            row = i * tile
            for ref, where, first, many in parts(i):
                ref[(*where, slice(first, first + many), slice(0, depth), at)] = value[
                    row : row + many * depth
                ].reshape(many, depth, wide)
                row += many * depth
        return carry

    lax.fori_loop(0, lots // wide, columns, 0)
    d_logits = split(jnp.concatenate([ref[...] for ref in logits], axis=1))
    gates = product([x_high[...], x_low[...]], d_logits, True)
    value = None
    for i in range(mine):
        for k in range(2):
            hidden = gelu(held[6 + k][i * hidden_units : (i + 1) * hidden_units, :])
            part = product(split(hidden), split(held[8 + k][i]), True)
            value = part if value is None else value + part
    tower[...] = jnp.concatenate(
        [value, jnp.zeros((value.shape[0], TOWER_LANES - value.shape[1]), jnp.float32)], axis=1
    )
    full = gate_end == lots and tower_depth % 8 == 0
    for i in range(tiles):
        d = i * share
        for ref, where, first, many in parts(i):
            for k in range(first, first + many):
                if not full:
                    ref[(*where, k, slice(depth, depth + 8), slice(None))] = jnp.zeros(
                        (8, lots), jnp.float32
                    )
                row = tower_row(order, peer_ref, d // 4, d % 4, tower_depth)
                for j in range(0, tower_depth, 8):
                    high = min(8, tower_depth)
                    to = j // 8 * TOWER_LANES
                    ref[(*where, k, slice(depth, depth + high), slice(to, to + TOWER_LANES))] = (
                        tower[pl.ds(row + j, high), :]
                    )
                eights = [gates[d * depth + j : d * depth + j + 8] for j in range(0, depth, 8)]
                ref[(*where, k, slice(depth, depth + 8), slice(gate_at, gate_end))] = (
                    jnp.concatenate(eights, axis=1) if len(eights) > 1 else eights[0]
                )
                d += 1


def gradients(dims, devices, depth, tower_depth, order, peer, logits, operands, before):
    mine, hidden_units = dims
    lots = mine * hidden_units
    tall = depth + 8
    counted = order[1]
    shape = (2, 2, 2, tall, lots) if counted else (devices, tall, lots)
    outs = 4 if counted else 1
    return pl.pallas_call(
        functools.partial(gradient_kernel, dims, depth, tower_depth, order, outs),
        out_shape=[jax.ShapeDtypeStruct(shape, jnp.float32)] * outs
        + [jax.ShapeDtypeStruct((lots, 1), jnp.float32)],
        in_specs=[SCALARS, WHOLE, WHOLE] + [ANYWHERE] * 11,
        out_specs=[WHOLE] * (outs + 1),
        scratch_shapes=[pltpu.VMEM(x.shape, x.dtype) for x in operands]
        + [pltpu.VMEM((devices * depth, 4 * LANES), jnp.bfloat16)] * 2
        + [pltpu.VMEM((lots, 4 * LANES), jnp.bfloat16)] * 2
        + [
            pltpu.VMEM((hidden_units, TOWER_LANES), jnp.float32),
            pltpu.SemaphoreType.DMA((10,)),
        ],
        compiler_params=pltpu.CompilerParams(vmem_limit_bytes=28 * MIB),
        cost_estimate=pl.CostEstimate(
            flops=16 * lots * devices * depth * LANES,
            bytes_accessed=16 * MIB,
            transcendentals=0,
        ),
    )(peer, *logits, *operands, before)


def swap_near(x):
    count = lax.axis_size("near")
    return lax.ppermute(x, "near", [(i, i ^ 1) for i in range(count)])


def swap_core(x):
    return lax.ppermute(x, "col", [(0, 1), (1, 0)])


def exchange_cores(x, member):
    blocks = [lax.dynamic_index_in_dim(x, member ^ i, 0, False) for i in range(4)]
    return blocks, swap_core(jnp.stack([blocks[1], blocks[3]]))


def exchange_chips(state, member, after=0):
    blocks, other = state
    far = swap_near(jnp.stack([blocks[2], other[1]]))
    came = jnp.stack([blocks[0], other[0], far[0], far[1]])
    member = member + after
    return jnp.stack([lax.dynamic_index_in_dim(came, member ^ i, 0, False) for i in range(4)])


def swap_peer(x, bit):
    if bit == 4:
        return lax.ppermute(x, "hi", [(0, 1), (1, 0)])
    return lax.ppermute(x, "rest", [(i, i ^ bit) for i in range(lax.axis_size("rest"))])


def near_peers(x):
    return [swap_peer(x, bit) for bit in (1, 2, 4)]


def gather_peers(x, one, two, top):
    cut = x.shape[0] // 2

    def plane(own, one, two):
        far = [swap_peer(two[:cut], 1), swap_peer(one[cut:], 2)]
        return [own, one, two] + far

    return plane(x, one, two) + plane(top, swap_peer(top, 1), swap_peer(top, 2))


def both_sums(x, far, axis):
    return [
        lax.index_in_dim(x, i, axis, False) + lax.index_in_dim(far, i, axis, False)
        for i in range(2)
    ]


def padded(x, width):
    return jnp.pad(x, [(0, 0)] * (x.ndim - 1) + [(0, width - x.shape[-1])])


def per_device(
    tables,
    table_moment,
    table_square,
    expert_weight,
    expert_moment,
    expert_square,
    gate_weight,
    gate_moment,
    gate_square,
    tower_weight,
    tower_moment,
    tower_square,
    expert_bias,
    bias_moment,
    bias_square,
    head_bias,
    head_moment,
    head_square,
    tower_output,
    output_moment,
    output_square,
    lookup_ids,
    bag_lengths,
    sample_counts,
    labels,
    label_mask,
    sample_weight,
):
    halves = lax.axis_size("col")
    rest = lax.axis_size("rest")
    pieces = 4 * rest
    devices = pieces * halves
    groups = 2 * rest
    members = devices // groups
    rows_here, width_here = tables.shape
    tabs_here = width_here // DIM
    samples, tabs, bag = lookup_ids.shape
    each = samples * bag // pieces
    classes = pieces // bag
    experts, depth, hidden_units = expert_weight.shape
    mine = experts // members
    tasks, tower_depth, tower_units = tower_weight.shape
    upper_width = tasks * tower_units
    member = lax.axis_index("near") * halves + lax.axis_index("col")
    counted = groups == 8
    peer = lax.axis_index("hi") * rest + lax.axis_index("rest") if counted else jnp.int32(0)
    peer_at = peer.astype(jnp.int32).reshape(1)
    depth = expert_weight.shape[1]

    def spot(stripe, own):
        high, near, low = stripe // (2 * rest), stripe // rest % 2, stripe % rest
        return ((high * rest + low) ^ own) * 2 + near

    place = (halves * depth, spot)

    order = (rest, counted)

    def reorder(x):
        return x.reshape((each, classes) + x.shape[1:]).swapaxes(0, 1).reshape(x.shape)

    live = (jnp.arange(samples, dtype=jnp.int32) < sample_counts[0]).astype(jnp.float32)
    keep = reorder(sample_weight[:, None] * label_mask.astype(jnp.float32) * live[:, None])
    targets = reorder(labels.astype(jnp.float32))

    ids = lookup_ids.transpose(0, 2, 1).reshape(each, pieces, tabs)
    use = jnp.arange(bag, dtype=jnp.int32)[None, :, None] < bag_lengths[:, None, :]
    owner = ids // rows_here
    local = jnp.where(use.reshape(each, pieces, tabs), ids - owner * rows_here, rows_here)
    here = owner[None] == jnp.arange(pieces, dtype=jnp.int32)[:, None, None, None]
    wanted = jnp.sum(jnp.where(here, local[None], 0), axis=2)
    wanted = wanted.transpose(0, 2, 1).reshape(devices, tabs_here * each).astype(jnp.float32)
    message = jnp.concatenate(
        [wanted, jnp.broadcast_to(jnp.sum(keep), (devices, 1))], axis=1
    )
    wide = -(-message.shape[1] // 1024) * 1024
    message = padded(message, wide).reshape(devices, wide // LANES, LANES)
    shifts = lookup_ids[0, :, 0] // rows_here

    asked = lax.all_to_all(message, ALL, 0, 0, tiled=True).reshape(devices, wide)
    idx = asked[:, : tabs_here * each].reshape(devices, tabs_here, each)
    idx = idx.swapaxes(0, 1).reshape(-1).astype(jnp.int32)
    weight_total = jnp.sum(asked[:, tabs_here * each])

    lots = mine * hidden_units
    send = expert_weight.reshape(members, mine, depth, hidden_units).swapaxes(1, 2)
    send = send.reshape(members, depth, lots)
    small = pack_rows(
        tower_weight.swapaxes(0, 1).reshape(tower_depth, upper_width),
        gate_weight.swapaxes(0, 1).reshape(depth, tasks * experts),
        lots,
    )
    send = jnp.concatenate(
        [send, jnp.broadcast_to(small[None], (members,) + small.shape)], axis=1
    )
    ready = jnp.minimum(idx[0], 0)
    shared = exchange_chips(exchange_cores(send, member), member, ready)
    if counted:
        round_one = near_peers(shared)
        parts = gather_peers(shared, *round_one)
    else:
        round_one = [shared]
        parts = [lax.all_gather(shared, PEERS, axis=0, tiled=True)]
    bias_mine = lax.dynamic_slice_in_dim(expert_bias, member * mine, mine, 0).reshape(lots, 1)

    picked = fence(gather_rows(idx, tables, devices, each), round_one)
    cols = width_here // LANES
    arrived = lax.all_to_all(
        picked.reshape(devices, cols * each, LANES), ALL, 0, 0, tiled=True
    ).reshape(pieces, halves, cols, each, LANES)
    split_parts = split_weights(
        parts, peer_at, order, depth, tower_depth, upper_width
    )
    weight_pair, weight_turned, tower_pair, gate_pair, tower_turned, gate_turned = [
        split_parts[2 * k : 2 * k + 2] for k in range(6)
    ]
    mine_x = pool(shifts, peer_at, place, arrived, split_parts[0])
    near_x = swap_near(mine_x)
    halves_x = [(mine_x, swap_core(mine_x)), (near_x, swap_core(near_x))]

    dims = (tasks, experts, mine, hidden_units, tower_units)
    member_at = member.astype(jnp.int32).reshape(1)
    runs = [
        forward(dims, member_at, x, weight_turned, tower_turned, gate_turned, bias_mine)
        for x in halves_x
    ]
    part_own, part_near = runs[0][3], runs[1][3]
    first = part_own[0] + swap_core(part_own[1])
    second = swap_near(part_near[0] + swap_core(part_near[1]))
    packed, grad_output, grad_head, few = score_step(
        tasks,
        weight_total.reshape(1),
        first,
        second,
        head_bias[:, :-1].reshape(upper_width, 1),
        tower_output.reshape(upper_width, 1),
        head_bias[:, -1:],
        keep.T,
        targets.T,
    )

    near_packed = swap_near(packed)
    halves_packed = [(packed, swap_core(packed)), (near_packed, swap_core(near_packed))]

    def half_back(k, packed):
        run = runs[k]
        return backward(
            dims,
            member_at,
            packed,
            run[0],
            run[1],
            run[2],
            weight_pair,
            tower_pair,
            gate_pair,
        )

    back_near = half_back(1, halves_packed[1])
    (near_in, far_in) = back_near[3:]
    leaving = near_in + swap_core(far_in)
    beyond = swap_near(leaving)
    back = [half_back(0, (fence(packed, [leaving]), halves_packed[0][1])), back_near]
    d_terms = [back[0][3], swap_core(back[0][4]), beyond]

    returned = list(spread(shifts, peer_at, place, d_terms, pieces, halves))

    *sums, grad_bias = gradients(
        (mine, hidden_units),
        devices,
        depth,
        tower_depth,
        order,
        peer_at,
        [x[2] for x in back],
        [
            *halves_x[0],
            *halves_x[1],
            *[x[0] for x in back],
            *[x[0] for x in runs],
            *[x[1] for x in back],
        ],
        returned[0],
    )

    grad_head = jnp.concatenate([grad_head.reshape(tasks, tower_units), few[0]], axis=1)
    same = jnp.concatenate(
        [
            grad_bias.reshape(-1),
            grad_head.reshape(-1),
            grad_output.reshape(-1),
            jnp.sum(few[1]).reshape(1),
        ]
    )
    cuts = [lots, grad_head.size, grad_output.size, 1]
    long = -(-same.shape[0] // 1024) * 1024
    same = jnp.broadcast_to(
        padded(same, long).reshape(1, long // LANES, LANES), (devices, long // LANES, LANES)
    )
    returned[1] = jnp.concatenate([returned[1], same], axis=1)
    came = [lax.all_to_all(x, ALL, 0, 0, tiled=True) for x in returned[:2]]
    new_tables = None
    before = []
    if counted:
        kept = [sums[0], sums[2]]
        far = [swap_peer(sums[1], 1), swap_peer(sums[3], 2)]
    else:
        kept = []
    for u in range(cols):
        later = returned[u + 2 : u + 3]
        new_tables, handed = update_part(
            idx,
            came[u],
            (tables, table_moment, table_square),
            u,
            each,
            new_tables,
            kept + later,
            before,
        )
        kept = handed[: len(kept)]
        if later:
            came.append(lax.all_to_all(handed[-1], ALL, 0, 0, tiled=True))
        if counted and u == 0:
            a, b = [both_sums(x, y, 1) for x, y in zip(kept, far)]
            kept, before = [a[0], b[0]], [a[1], b[1]]
            far = [swap_peer(a[1], 2), swap_peer(b[1], 1)]
        if counted and u == 1:
            a, b = [both_sums(x, y, 0) for x, y in zip(kept, far)]
            kept, leaves = [[jnp.concatenate([x, y], axis=0)] for x, y in zip(a, b)]
            before = leaves
            far = [swap_peer(leaves[0], 4)]
        if counted and u == 2:
            state = exchange_cores(kept[0] + far[0], member)
            kept, before = [], [state[1]]
    if not counted:
        summed = lax.psum_scatter(sums[0], PEERS, scatter_dimension=0, tiled=True)
        state = exchange_cores(summed, member)
    summed = exchange_chips(state, member)
    shard_experts = (
        summed[:, :depth]
        .reshape(members, depth, mine, hidden_units)
        .swapaxes(1, 2)
        .reshape(experts, depth, hidden_units)
    )
    shard_towers, shard_gates = unpack_rows(
        jnp.sum(summed[:, depth:], axis=0),
        (tower_depth, upper_width),
        (depth, tasks * experts),
    )
    shard_towers = shard_towers.reshape(tower_depth, tasks, tower_units).swapaxes(0, 1)
    shard_gates = shard_gates.reshape(depth, tasks, experts).swapaxes(0, 1)
    same = came[1][:, each:].reshape(devices, long)
    found = []
    start = 0
    for size in cuts:
        found.append(same[:, start : start + size])
        start += size
    summed_bias = jnp.sum(found[0].reshape(2, 2, rest, halves, lots), axis=(0, 2)).reshape(
        experts, hidden_units
    )
    summed_head = jnp.sum(found[1], axis=0).reshape(head_bias.shape)
    summed_output = jnp.sum(found[2], axis=0).reshape(tower_output.shape)
    loss_sum = jnp.sum(found[3])

    return (
        *new_tables,
        *adamw(expert_weight, expert_moment, expert_square, shard_experts, dense_rate),
        *adamw(gate_weight, gate_moment, gate_square, shard_gates, dense_rate),
        *adamw(tower_weight, tower_moment, tower_square, shard_towers, dense_rate),
        *adamw(expert_bias, bias_moment, bias_square, summed_bias, dense_rate),
        *adamw(head_bias, head_moment, head_square, summed_head, dense_rate),
        *adamw(tower_output, output_moment, output_square, summed_output, dense_rate),
        loss_sum,
        weight_total,
    )


def solution(mesh):
    pieces, halves = mesh.devices.shape
    fine = Mesh(mesh.devices.reshape(2, 2, pieces // 4, halves), ALL)
    table = P(ROW, "col")
    middle = P(None, ALL, None)
    first = P(ALL)
    return jax.shard_map(
        per_device,
        mesh=fine,
        in_specs=(table,) * 3 + (middle,) * 9 + (P(),) * 9 + (first,) * 6,
        out_specs=(table,) * 3 + (middle,) * 9 + (P(),) * 11,
        check_vma=False,
    )
```

time: 444 us -> 385 us (0.87)
  waiting for transfers between devices: 170 us -> 117 us
  matrix products: 37.2 us -> 0 us
  Pallas kernels: 98.5 us -> 131 us
  starting transfers between devices: 30.9 us -> 59.6 us
  blocking collectives: 15.2 us -> 0 us
  between operations: 16.1 us -> 3.19 us
  local copies, waits for them, and re-layouts: 43 us -> 51.2 us
  other arithmetic: 28.2 us -> 21.4 us
    all_to_all x1, waiting for transfers between devices: 90.2 us -> 0.01 us  [per_device(): lax.all_to_all(picked.reshape(devices, cols * each, LANES), ALL, 0, 0, ti...]
    ppermute x0 -> x14, waiting for transfers between devices: none -> 69.1 us  [the longest x12 48.2 us: swap_peer(): lax.ppermute(x, 'rest', [(i, i ^ bit) for i in range(lax.axis_size('rest'...]
    dot_general x12 -> x0, matrix products: 37.2 us -> none  [dot(): lax.dot_general(a, b, (dims, ((), ())), precision=FAST, preferred_element...]
    pallas_call x2 -> x11, Pallas kernels: 4.49 us -> 36.5 us  [the longest x2 8.84 us: backward(): pl.pallas_call(functools.partial(backward_kernel, dims), out_shape=[jax.S...]
    unnamed x115 -> x168, local copies, waits for them, and re-layouts: 8.63 us -> 39.2 us
    ppermute x0 -> x14, starting transfers between devices: none -> 20.8 us  [the longest x12 15.9 us: swap_peer(): lax.ppermute(x, 'rest', [(i, i ^ bit) for i in range(lax.axis_size('rest'...]
    all_to_all x2, waiting for transfers between devices: 16.6 us -> 0.01 us  [per_device(): came = [lax.all_to_all(x, ALL, 0, 0, tiled=True) for x in returned[:2]]]
    reduce_scatter x1 -> x0, waiting for transfers between devices: 16 us -> none  [per_device(): summed = lax.psum_scatter(summed, 'grp', scatter_dimension=0, tiled=True)]
  transfers between devices with their start and end apart: 19 -> 36, of which waited for: 12 -> 19; matrix products, arithmetic and copies ran while one was open for 9% -> 8% of each run, Pallas kernels for 22% -> 29%
where the time goes in v2:
time: 385 us; the launch traced here: 384 us
  Pallas kernels  131 us (34%)
  waiting for transfers between devices  117 us (30%)
  starting transfers between devices  59.6 us (15%)
  local copies, waits for them, and re-layouts  51.2 us (13%)
  other arithmetic  21.4 us (6%)
    pallas_call x4, Pallas kernels, update_part(): pl.pallas_call(functools.partial(update_kernel, rows, part, devices, each...  79.9 us
    ppermute x12, waiting for transfers between devices, swap_peer(): lax.ppermute(x, 'rest', [(i, i ^ bit) for i in range(lax.axis_size('rest'...  48.2 us
    unnamed x168, local copies, waits for them, and re-layouts  39.2 us
    ppermute x6, waiting for transfers between devices, swap_near(): return lax.ppermute(x, 'near', [(i, i ^ 1) for i in range(count)])  35.3 us
    ppermute x2, waiting for transfers between devices, swap_peer(): return lax.ppermute(x, 'hi', [(0, 1), (1, 0)])  21 us
    ppermute x12, starting transfers between devices, swap_peer(): lax.ppermute(x, 'rest', [(i, i ^ bit) for i in range(lax.axis_size('rest'...  15.9 us
    pallas_call x1, Pallas kernels, gather_rows(): pl.pallas_call(functools.partial(gather_kernel, rows, cols, devices, each...  14.8 us
    pallas_call x2, Pallas kernels, backward(): pl.pallas_call(functools.partial(backward_kernel, dims), out_shape=[jax.S...  8.84 us
  transfers between devices with their start and end apart: 36, of which 19 were waited for; matrix products, arithmetic and copies ran while one was open for 8% of the time, Pallas kernels for 29%

profile of v2, /device:TPU:0, one launch (start us, length us, event | category | flops | bytes accessed | tf_op | source)
XLA Modules:
  0.0 383.7 jit_solution(10376315292144035720)
XLA Ops:
  7.5 7.0 %all-to-all-start = ((f32[32,8,128]{2,1,0:T(8,128)}), f32[32,8,128]{2,1,0:T(8,128)S(1)}, u32[]{:S(2)}, u32[]{:S(2)}) async-start(f32[32,8,128]{2,1,0:T(8,128)} %bitcast.58), calls=%async_computation | async-start | bytes 262144 | tf_op jit(solution)/shard_map/all_to_all | solution.py:856
  16.4 6.4 %all-to-all-done = f32[32,8,128]{2,1,0:T(8,128)S(1)} async-done(((f32[32,8,128]{2,1,0:T(8,128)}), f32[32,8,128]{2,1,0:T(8,128)S(1)}, u32[]{:S(2)}, u32[]{:S(2)}) %all-to-all-start) | async-done | bytes 131104 | tf_op jit(solution)/shard_map/all_to_all | solution.py:856
  32.1 14.8 %shard_map.434.refs_0_ = f32[32,4,32,128]{3,2,1,0:T(8,128)} custom-call(s32[8192]{0:T(1024)S(1)} %convert_element_type.47.idx_ref, f32[16384,512]{1,0:T(8,128)} %refs_0_.7), custom_call_target="tpu_custom_call" | custom-call | bytes 67108864 | tf_op jit(solution)/shard_map/pallas_call | solution.py:105
  46.9 11.0 %collective-permute-done.4.refs_3_.refs_5_ = f32[4,40,1024]{2,1,0:T(8,128)S(1)} collective-permute-done((f32[4,40,1024]{2,1,0:T(8,128)S(1)}, f32[4,40,1024]{2,1,0:T(8,128)S(1)}, u32[]{:S(2)}, u32[]{:S(2)}) %collective-permute-start.4) | collective-permute-done | bytes 655392 | tf_op jit(solution)/shard_map/ppermute | solution.py:748
  58.8 4.9 %all-to-all-start.1 = ((f32[32,128,128]{2,1,0:T(8,128)}), f32[32,128,128]{2,1,0:T(8,128)S(1)}, u32[]{:S(2)}, u32[]{:S(2)}) async-start(f32[32,128,128]{2,1,0:T(8,128)} %bitcast.20), calls=%async_computation.1 | async-start | bytes 4194304 | tf_op jit(solution)/shard_map/all_to_all | solution.py:884
  68.0 32.7 %collective-permute-done.7.refs_6_ = f32[4,40,1024]{2,1,0:T(8,128)} collective-permute-done((f32[4,40,1024]{2,1,0:T(8,128)}, f32[4,40,1024]{2,1,0:T(8,128)}, u32[]{:S(2)}, u32[]{:S(2)}) %collective-permute-start.7) | collective-permute-done | bytes 655392 | tf_op jit(solution)/shard_map/ppermute | solution.py:749
  105.2 5.2 %collective-permute-done.5.refs_3_ = f32[2,40,1024]{2,1,0:T(8,128)S(1)} collective-permute-done((f32[2,40,1024]{2,1,0:T(8,128)S(1)}, f32[2,40,1024]{2,1,0:T(8,128)S(1)}, u32[]{:S(2)}, u32[]{:S(2)}) %collective-permute-start.5) | collective-permute-done | bytes 327712 | tf_op jit(solution)/shard_map/ppermute | solution.py:749
  110.4 6.5 %collective-permute-done.10.refs_9_ = f32[2,40,1024]{2,1,0:T(8,128)S(1)} collective-permute-done((f32[2,40,1024]{2,1,0:T(8,128)S(1)}, f32[2,40,1024]{2,1,0:T(8,128)S(1)}, u32[]{:S(2)}, u32[]{:S(2)}) %collective-permute-start.10) | collective-permute-done | bytes 327712 | tf_op jit(solution)/shard_map/ppermute | solution.py:749
  117.0 4.8 %shard_map.436 = (bf16[1024,1024]{1,0:T(8,128)(2,1)S(1)}, bf16[1024,1024]{1,0:T(8,128)(2,1)S(1)}, bf16[1024,1024]{1,0:T(8,128)(2,1)S(1)}, bf16[1024,1024]{1,0:T(...) custom-call(s32[1]{0:T(128)} %bitcast.6.peer_ref, ...), custom_call_target="tpu_custom_call" | custom-call | tf_op jit(solution)/shard_map/pallas_call | solution.py:411
  137.2 12.0 %collective-permute-done.13.refs_0_.refs_4_ = f32[1024,128]{1,0:T(8,128)S(1)} collective-permute-done((f32[1024,128]{1,0:T(8,128)S(1)}, f32[1024,128]{1,0:T(8,128)S(1)}, u32[]{:S(2)}, u32[]{:S(2)}) %collective-permute-start.13) | collective-permute-done | bytes 524320 | tf_op jit(solution)/shard_map/ppermute | solution.py:726
  165.3 5.0 %shard_map.439 = (f32[1024,256]{1,0:T(8,128)S(1)}, f32[40,256]{1,0:T(8,128)S(1)}, f32[2,320,256]{2,1,0:T(8,128)S(1)}, f32[2,320,128]{2,1,0:T(8,128)S(1)}) custom-call(s32[1]{0:T(128)} %bitcast.7.member_ref, f32[1024,128]{1,0:T(8,128)S(1)} %collective-permute-done.13.refs_0_.refs_4_, f32[1024,128]{1,0:T(8,128)} %collective-permute-done.14.refs_1_.refs_5_, ...), custom_call_target="tpu_custom_call" | custom-call | flops 2147483648 | bytes 12582912 | tf_op jit(solution)/shard_map/pallas_call | solution.py:479
  173.5 5.0 %collective-permute-done.16.second_ref = f32[320,128]{1,0:T(8,128)S(1)} collective-permute-done((f32[320,128]{1,0:T(8,128)S(1)}, f32[320,128]{1,0:T(8,128)S(1)}, u32[]{:S(2)}, u32[]{:S(2)}) %collective-permute-start.16) | collective-permute-done | bytes 163872 | tf_op jit(solution)/shard_map/ppermute | solution.py:726
  181.0 4.3 %collective-permute-done.17.refs_0_ = f32[328,128]{1,0:T(8,128)S(1)} collective-permute-done((f32[328,128]{1,0:T(8,128)S(1)}, f32[328,128]{1,0:T(8,128)S(1)}, u32[]{:S(2)}, u32[]{:S(2)}) %collective-permute-start.17) | collective-permute-done | bytes 167968 | tf_op jit(solution)/shard_map/ppermute | solution.py:726
  186.7 4.5 %shard_map.441 = (f32[1024,256]{1,0:T(8,128)S(1)}, f32[2,320,256]{2,1,0:T(8,128)S(1)}, f32[64,256]{1,0:T(8,128)S(1)}, f32[1024,128]{1,0:T(8,128)S(1)}, f32[1024,128]{1,0:T(8,128)S(1)}) custom-call(s32[1]{0:T(128)} %bitcast.7.member_ref, f32[328,128]{1,0:T(8,128)S(1)} %collective-permute-done.17.refs_0_, f32[328,128]{1,0:T(8,128)S(1)} %collective-permute-done.18.refs_1_, ...), custom_call_target="tpu_custom_call" | custom-call | flops 2147483648 | bytes 12582912 | tf_op jit(solution)/shard_map/pallas_call | solution.py:597
  194.4 4.3 %shard_map.443 = (f32[1024,256]{1,0:T(8,128)S(1)}, f32[2,320,256]{2,1,0:T(8,128)S(1)}, f32[64,256]{1,0:T(8,128)S(1)}, f32[1024,128]{1,0:T(8,128)S(1)}, f32[1024,128]{1,0:T(8,128)S(1)}) custom-call(s32[1]{0:T(128)} %bitcast.7.member_ref, f32[328,128]{1,0:T(8,128)S(1)} %shard_map.442.refs_0_, f32[328,128]{1,0:T(8,128)S(1)} %collective-permute-done.20.refs_1_, ...), custom_call_target="tpu_custom_call" | custom-call | flops 2147483648 | bytes 12582912 | tf_op jit(solution)/shard_map/pallas_call | solution.py:597
  202.5 12.4 %collective-permute-done.22.refs_2_ = f32[1024,128]{1,0:T(8,128)S(1)} collective-permute-done((f32[1024,128]{1,0:T(8,128)S(1)}, f32[1024,128]{1,0:T(8,128)S(1)}, u32[]{:S(2)}, u32[]{:S(2)}) %collective-permute-start.22) | collective-permute-done | bytes 524320 | tf_op jit(solution)/shard_map/ppermute | solution.py:726
  219.0 5.0 %all-to-all-start.3 = ((f32[32,32,128]{2,1,0:T(8,128)}), f32[32,32,128]{2,1,0:T(8,128)S(1)}, u32[]{:S(2)}, u32[]{:S(2)}) async-start(f32[32,32,128]{2,1,0:T(8,128)} %get-tuple-element.117.refs_12_), calls=%async_computation.3 | async-start | bytes 1048576 | tf_op jit(solution)/shard_map/all_to_all | solution.py:977
  234.2 8.7 %shard_map.445 = (f32[2,2,2,40,1024]{4,3,2,1,0:T(8,128)S(1)}, f32[2,2,2,40,1024]{4,3,2,1,0:T(8,128)S(1)}, f32[2,2,2,40,1024]{4,3,2,1,0:T(8,128)S(1)}, f32[2,2,2,40,1024]{4,3,2,1,0:T(8,128)S(1)}, f32[1024,1]{1,0:T(8,128)S(1)}) custom-call(s32[1]{0:T(128)} %bitcast.6.peer_ref, f32[64,256]{1,0:T(8,128)S(1)} %get-tuple-element.111.refs_0_, ...), custom_call_target="tpu_custom_call" | custom-call | flops 2147483648 | bytes 16777216 | tf_op jit(solution)/shard_map/pallas_call | solution.py:702
  258.5 20.0 %shard_map.446 = (f32[16384,512]{1,0:T(8,128)}, f32[16384,512]{1,0:T(8,128)}, f32[16384,512]{1,0:T(8,128)}, f32[2,2,2,40,1024]{4,3,2,1,0:T(8,128)S(1)}, f32[2,2,...) custom-call(s32[8192]{0:T(1024)S(1)} %convert_element_type.47.idx_re, ...), custom_call_target="tpu_custom_call", output_to_operand_aliasing={{3}: (5, {}), {4}: (6, {}), {5}: (7, {})} | custom-call | flops 62914560 | bytes 50331648 | tf_op jit(solution)/shard_map/pallas_call | solution.py:273
  290.3 4.4 %all-to-all-start.5 = ((f32[32,32,128]{2,1,0:T(8,128)}), f32[32,32,128]{2,1,0:T(8,128)}, u32[]{:S(2)}, u32[]{:S(2)}) async-start(f32[32,32,128]{2,1,0:T(8,128)} %get-tuple-element.134), calls=%async_computation.5 | async-start | bytes 1048576 | tf_op jit(solution)/shard_map/all_to_all | solution.py:999
  294.7 20.0 %shard_map.447 = (f32[16384,512]{1,0:T(8,128)}, f32[16384,512]{1,0:T(8,128)}, f32[16384,512]{1,0:T(8,128)}, f32[2,2,40,1024]{3,2,1,0:T(8,128)S(1)}, f32[2,2,40,1...) custom-call(s32[8192]{0:T(1024)S(1)} %convert_element_type.47.idx_re, ...), custom_call_target="tpu_custom_call", output_to_operand_aliasing={{0}: (5, {}), {1}: (6, {}), {2}: (7, {}), {3}: (8, {}), {4}... | custom-call | flops 62914560 | bytes 50331648 | tf_op jit(solution)/shard_map/pallas_call | solution.py:273
  324.4 20.0 %shard_map.448 = (f32[16384,512]{1,0:T(8,128)}, f32[16384,512]{1,0:T(8,128)}, f32[16384,512]{1,0:T(8,128)}, f32[4,40,1024]{2,1,0:T(8,128)S(1)}) custom-call(s32[8192]{0:T(1024)S(1)} %convert_element_type.47.idx_ref, f32[32,32,128]{2,1,0:T(8,128)} %all-to-all-done.5.grad_ref, ...), custom_call_target="tpu_custom_call", output_to_operand_aliasing={{0}: (5, {}), {1}: (6, {}), {2}: (7, {}), {3}: (8, {})} | custom-call | flops 62914560 | bytes 50331648 | tf_op jit(solution)/shard_map/pallas_call | solution.py:273
  344.4 10.0 %collective-permute-done.27 = f32[4,40,1024]{2,1,0:T(8,128)} collective-permute-done((f32[4,40,1024]{2,1,0:T(8,128)S(1)}, f32[4,40,1024]{2,1,0:T(8,128)}, u32[]{:S(2)}, u32[]{:S(2)}) %collective-permute-start.27) | collective-permute-done | bytes 655392 | tf_op jit(solution)/shard_map/ppermute | solution.py:748
  360.0 19.9 %shard_map.449 = (f32[16384,512]{1,0:T(8,128)}, f32[16384,512]{1,0:T(8,128)}, f32[16384,512]{1,0:T(8,128)}) custom-call(s32[8192]{0:T(1024)S(1)} %convert_element_type.47.idx_ref, f32[32,32,128]{2,1,0:T(8,128)S(1)} %all-to-all-done.4.grad_ref, f32[16384,512]{1,0:T(8,128)} %refs_0_.7, ...), custom_call_target="tpu_custom_call", output_to_operand_aliasing={{0}: (5, {}), {1}: (6, {}), {2}: (7, {})} | custom-call | flops 62914560 | bytes 50331648 | tf_op jit(solution)/shard_map/pallas_call | solution.py:273
  (341 shorter events, 131.8 us)
Async XLA Ops:
  7.5 15.2 %all-to-all-start = ((f32[32,8,128]{2,1,0:T(8,128)}), f32[32,8,128]{2,1,0:T(8,128)S(1)}, u32[]{:S(2)}, u32[]{:S(2)}) async-start(f32[32,8,128]{2,1,0:T(8,128)} %bitcast.58), calls=%async_computation | async-start | bytes 262144 | tf_op jit(solution)/shard_map/all_to_all | solution.py:856
  26.7 31.2 %collective-permute-start.4 = (f32[4,40,1024]{2,1,0:T(8,128)S(1)}, f32[4,40,1024]{2,1,0:T(8,128)S(1)}, u32[]{:S(2)}, u32[]{:S(2)}) collective-permute-start(f32[4,40,1024]{2,1,0:T(8,128)S(1)} %pad_maximum_fusion.2.refs_0_), channel_id=1, source_target_pairs={{0,16},{16,0},{1,17},{17,1},{2,18},{18,2},{3,19},{19,3},{4,20},{20... | collective-permute-start | bytes 1966088 | tf_op jit(solution)/shard_map/ppermute | solution.py:748
  29.2 28.8 %collective-permute-start.3 = (f32[4,40,1024]{2,1,0:T(8,128)S(1)}, f32[4,40,1024]{2,1,0:T(8,128)S(1)}, u32[]{:S(2)}, u32[]{:S(2)}) collective-permute-start(f32[4,40,1024]{2,1,0:T(8,128)S(1)} %pad_maximum_fusion.2.refs_0_), channel_id=1, source_target_pairs={{0,4},{2,6},{4,0},{6,2},{1,5},{3,7},{5,1},{7,3},{8,12},{10,14},{12... | collective-permute-start | bytes 1966088 | tf_op jit(solution)/shard_map/ppermute | solution.py:749
  30.7 27.3 %collective-permute-start.2 = (f32[4,40,1024]{2,1,0:T(8,128)S(1)}, f32[4,40,1024]{2,1,0:T(8,128)S(1)}, u32[]{:S(2)}, u32[]{:S(2)}) collective-permute-start(f32[4,40,1024]{2,1,0:T(8,128)S(1)} %pad_maximum_fusion.2.refs_0_), channel_id=1, source_target_pairs={{0,2},{2,0},{4,6},{6,4},{1,3},{3,1},{5,7},{7,5},{8,10},{10,8},{12,... | collective-permute-start | bytes 1966088 | tf_op jit(solution)/shard_map/ppermute | solution.py:749
  58.8 74.1 %all-to-all-start.1 = ((f32[32,128,128]{2,1,0:T(8,128)}), f32[32,128,128]{2,1,0:T(8,128)S(1)}, u32[]{:S(2)}, u32[]{:S(2)}) async-start(f32[32,128,128]{2,1,0:T(8,128)} %bitcast.20), calls=%async_computation.1 | async-start | bytes 4194304 | tf_op jit(solution)/shard_map/all_to_all | solution.py:884
  63.7 37.0 %collective-permute-start.7 = (f32[4,40,1024]{2,1,0:T(8,128)}, f32[4,40,1024]{2,1,0:T(8,128)}, u32[]{:S(2)}, u32[]{:S(2)}) collective-permute-start(f32[4,40,1024]{2,1,0:T(8,128)} %copy-done), channel_id=1, source_target_pairs={{0,2},{2,0},{4,6},{6,4},{1,3},{3,1},{5,7},{7,5},{8,10},{10,8},{12,... | collective-permute-start | bytes 1966088 | tf_op jit(solution)/shard_map/ppermute | solution.py:749
  65.4 37.1 %collective-permute-start.8 = (f32[4,40,1024]{2,1,0:T(8,128)}, f32[4,40,1024]{2,1,0:T(8,128)}, u32[]{:S(2)}, u32[]{:S(2)}) collective-permute-start(f32[4,40,1024]{2,1,0:T(8,128)} %copy-done), channel_id=1, source_target_pairs={{0,4},{2,6},{4,0},{6,2},{1,5},{3,7},{5,1},{7,3},{8,12},{10,14},{12... | collective-permute-start | bytes 1966088 | tf_op jit(solution)/shard_map/ppermute | solution.py:749
  66.9 43.5 %collective-permute-start.5 = (f32[2,40,1024]{2,1,0:T(8,128)S(1)}, f32[2,40,1024]{2,1,0:T(8,128)S(1)}, u32[]{:S(2)}, u32[]{:S(2)}) collective-permute-start(f32[2,40,1024]{2,1,0:T(8,128)S(1)} %slice.206), channel_id=1, source_target_pairs={{0,2},{2,0},{4,6},{6,4},{1,3},{3,1},{5,7},{7,5},{8,10},{10,8},{12,... | collective-permute-start | bytes 983048 | tf_op jit(solution)/shard_map/ppermute | solution.py:749
  67.5 42.9 %collective-permute-start.6 = (f32[2,40,1024]{2,1,0:T(8,128)S(1)}, f32[2,40,1024]{2,1,0:T(8,128)S(1)}, u32[]{:S(2)}, u32[]{:S(2)}) collective-permute-start(f32[2,40,1024]{2,1,0:T(8,128)S(1)} %slice.207), channel_id=1, source_target_pairs={{0,4},{2,6},{4,0},{6,2},{1,5},{3,7},{5,1},{7,3},{8,12},{10,14},{12... | collective-permute-start | bytes 983048 | tf_op jit(solution)/shard_map/ppermute | solution.py:749
  101.7 15.3 %collective-permute-start.10 = (f32[2,40,1024]{2,1,0:T(8,128)S(1)}, f32[2,40,1024]{2,1,0:T(8,128)S(1)}, u32[]{:S(2)}, u32[]{:S(2)}) collective-permute-start(f32[2,40,1024]{2,1,0:T(8,128)S(1)} %slice.209), channel_id=1, source_target_pairs={{0,4},{2,6},{4,0},{6,2},{1,5},{3,7},{5,1},{7,3},{8,12},{10,14},{12... | collective-permute-start | bytes 983048 | tf_op jit(solution)/shard_map/ppermute | solution.py:749
  135.7 13.5 %collective-permute-start.13 = (f32[1024,128]{1,0:T(8,128)S(1)}, f32[1024,128]{1,0:T(8,128)S(1)}, u32[]{:S(2)}, u32[]{:S(2)}) collective-permute-start(f32[1024,128]{1,0:T(8,128)S(1)} %shard_map.437.refs_0_.refs_2_), channel_id=1, source_target_pairs={{0,8},{8,0},{1,9},{9,1},{2,10},{10,2},{3,11},{11,3},{4,12},{12,4},... | collective-permute-start | bytes 1572872 | tf_op jit(solution)/shard_map/ppermute | solution.py:726
  137.2 16.2 %collective-permute-start.11 = (f32[1024,128]{1,0:T(8,128)S(1)}, f32[1024,128]{1,0:T(8,128)S(1)}, u32[]{:S(2)}, u32[]{:S(2)}) collective-permute-start(f32[1024,128]{1,0:T(8,128)S(1)} %shard_map.437.refs_0_.refs_2_), channel_id=1, source_target_pairs={{0,1},{1,0},{2,3},{3,2},{4,5},{5,4},{6,7},{7,6},{8,9},{9,8},{10,11... | collective-permute-start | bytes 1572872 | tf_op jit(solution)/shard_map/ppermute | solution.py:730
  149.2 16.0 %collective-permute-start.14 = (f32[1024,128]{1,0:T(8,128)S(1)}, f32[1024,128]{1,0:T(8,128)}, u32[]{:S(2)}, u32[]{:S(2)}) collective-permute-start(f32[1024,128]{1,0:T(8,128)S(1)} %collective-permute-done.13.refs_0_.refs_4_), channel_id=1, source_target_pairs={{0,1},{1,0},{2,3},{3,2},{4,5},{5,4},{6,7},{7,6},{8,9},{9,8},{10,11... | collective-permute-start | bytes 1572872 | tf_op jit(solution)/shard_map/ppermute | solution.py:730
  200.7 14.2 %collective-permute-start.22 = (f32[1024,128]{1,0:T(8,128)S(1)}, f32[1024,128]{1,0:T(8,128)S(1)}, u32[]{:S(2)}, u32[]{:S(2)}) collective-permute-start(f32[1024,128]{1,0:T(8,128)S(1)} %add.224.refs_1_), channel_id=1, source_target_pairs={{0,8},{8,0},{1,9},{9,1},{2,10},{10,2},{3,11},{11,3},{4,12},{12,4},... | collective-permute-start | bytes 1572872 | tf_op jit(solution)/shard_map/ppermute | solution.py:726
  219.0 35.7 %all-to-all-start.3 = ((f32[32,32,128]{2,1,0:T(8,128)}), f32[32,32,128]{2,1,0:T(8,128)S(1)}, u32[]{:S(2)}, u32[]{:S(2)}) async-start(f32[32,32,128]{2,1,0:T(8,128)} %get-tuple-element.117.refs_12_), calls=%async_computation.3 | async-start | bytes 1048576 | tf_op jit(solution)/shard_map/all_to_all | solution.py:977
  244.1 38.2 %collective-permute-start.23 = (f32[2,2,2,40,1024]{4,3,2,0,1:T(8,128)}, f32[2,2,2,40,1024]{4,3,2,0,1:T(8,128)}, u32[]{:S(2)}, u32[]{:S(2)}) collective-permute-start(f32[2,2,2,40,1024]{4,3,2,0,1:T(8,128)} %copy.184), channel_id=1, source_target_pairs={{0,2},{2,0},{4,6},{6,4},{1,3},{3,1},{5,7},{7,5},{8,10},{10,8},{12,... | collective-permute-start | bytes 3932168 | tf_op jit(solution)/shard_map/ppermute | solution.py:749
  247.1 39.3 %collective-permute-start.24 = (f32[2,2,2,40,1024]{4,3,2,0,1:T(8,128)}, f32[2,2,2,40,1024]{4,3,2,0,1:T(8,128)}, u32[]{:S(2)}, u32[]{:S(2)}) collective-permute-start(f32[2,2,2,40,1024]{4,3,2,0,1:T(8,128)} %copy.186), channel_id=1, source_target_pairs={{0,4},{2,6},{4,0},{6,2},{1,5},{3,7},{5,1},{7,3},{8,12},{10,14},{12... | collective-permute-start | bytes 3932168 | tf_op jit(solution)/shard_map/ppermute | solution.py:749
  254.7 35.6 %all-to-all-start.2 = ((f32[32,48,128]{2,1,0:T(8,128)}), f32[32,48,128]{2,1,0:T(8,128)}, u32[]{:S(2)}, u32[]{:S(2)}) async-start(f32[32,48,128]{2,1,0:T(8,128)} %pad_maximum_fusion), calls=%async_computation.2 | async-start | bytes 1572864 | tf_op jit(solution)/shard_map/all_to_all | solution.py:977
  284.7 30.0 %collective-permute-start.25 = (f32[2,2,40,1024]{3,2,1,0:T(8,128)}, f32[2,2,40,1024]{3,2,1,0:T(8,128)}, u32[]{:S(2)}, u32[]{:S(2)}) collective-permute-start(f32[2,2,40,1024]{3,2,1,0:T(8,128)} %get-tuple-element.238.refs_9_), channel_id=1, source_target_pairs={{0,4},{2,6},{4,0},{6,2},{1,5},{3,7},{5,1},{7,3},{8,12},{10,14},{12... | collective-permute-start | bytes 1966088 | tf_op jit(solution)/shard_map/ppermute | solution.py:749
  288.8 27.1 %collective-permute-start.26 = (f32[2,2,40,1024]{3,2,1,0:T(8,128)}, f32[2,2,40,1024]{3,2,1,0:T(8,128)S(1)}, u32[]{:S(2)}, u32[]{:S(2)}) collective-permute-start(f32[2,2,40,1024]{3,2,1,0:T(8,128)} %get-tuple-element.236.refs_10_), channel_id=1, source_target_pairs={{0,2},{2,0},{4,6},{6,4},{1,3},{3,1},{5,7},{7,5},{8,10},{10,8},{12,... | collective-permute-start | bytes 1966088 | tf_op jit(solution)/shard_map/ppermute | solution.py:749
  290.3 30.4 %all-to-all-start.5 = ((f32[32,32,128]{2,1,0:T(8,128)}), f32[32,32,128]{2,1,0:T(8,128)}, u32[]{:S(2)}, u32[]{:S(2)}) async-start(f32[32,32,128]{2,1,0:T(8,128)} %get-tuple-element.134), calls=%async_computation.5 | async-start | bytes 1048576 | tf_op jit(solution)/shard_map/all_to_all | solution.py:999
  316.1 38.3 %collective-permute-start.27 = (f32[4,40,1024]{2,1,0:T(8,128)S(1)}, f32[4,40,1024]{2,1,0:T(8,128)}, u32[]{:S(2)}, u32[]{:S(2)}) collective-permute-start(f32[4,40,1024]{2,1,0:T(8,128)S(1)} %pad_maximum_fusion.4.refs_7_), channel_id=1, source_target_pairs={{0,16},{16,0},{1,17},{17,1},{2,18},{18,2},{3,19},{19,3},{4,20},{20... | collective-permute-start | bytes 1966088 | tf_op jit(solution)/shard_map/ppermute | solution.py:748
  320.6 39.4 %all-to-all-start.4 = ((f32[32,32,128]{2,1,0:T(8,128)}), f32[32,32,128]{2,1,0:T(8,128)S(1)}, u32[]{:S(2)}, u32[]{:S(2)}) async-start(f32[32,32,128]{2,1,0:T(8,128)} %get-tuple-element.133), calls=%async_computation.4 | async-start | bytes 1048576 | tf_op jit(solution)/shard_map/all_to_all | solution.py:999
  357.5 22.5 %collective-permute-start.29 = (f32[2,40,1024]{2,1,0:T(8,128)S(1)}, f32[2,40,1024]{2,1,0:T(8,128)S(1)}, u32[]{:S(2)}, u32[]{:S(2)}) collective-permute-start(f32[2,40,1024]{2,1,0:T(8,128)S(1)} %pad_maximum_fusion.11), channel_id=1, source_target_pairs={{0,8},{8,0},{1,9},{9,1},{2,10},{10,2},{3,11},{11,3},{4,12},{12,4},... | collective-permute-start | bytes 983048 | tf_op jit(solution)/shard_map/ppermute | solution.py:726
  (92 other events, 599.2 us)

commit v3 on v2

--- a/solution.py
+++ b/solution.py
@@ -13,6 +13,7 @@
 STEP = 10
 LANES = 128
 MIB = 1024 * 1024
+ROOM = 60 * MIB
 
 beta_one = 0.9
 beta_two = 0.999
@@ -27,6 +28,7 @@
 SCALARS = pl.BlockSpec(memory_space=pltpu.SMEM)
 WHOLE = pl.BlockSpec(memory_space=pltpu.VMEM)
 ANYWHERE = pl.BlockSpec(memory_space=pl.ANY)
+FAR = pl.BlockSpec(memory_space=pltpu.HBM)
 
 
 def adamw(weight, moment, square, gradient, rate):
@@ -111,14 +113,15 @@
             pltpu.VMEM((cols, rows + 8, LANES), jnp.float32),
             pltpu.SemaphoreType.DMA((cols,)),
         ],
-        compiler_params=pltpu.CompilerParams(vmem_limit_bytes=35 * MIB),
+        compiler_params=pltpu.CompilerParams(vmem_limit_bytes=ROOM),
         cost_estimate=pl.CostEstimate(
             flops=0, bytes_accessed=2 * rows * width * 4, transcendentals=0
         ),
     )(idx, table)
 
 
-def pool_kernel(pieces, halves, cols, each, place, shift_ref, peer_ref, in_ref, before, out_ref):
+def pool_kernel(pieces, halves, cols, each, place, shift_ref, peer_ref, in_ref, *refs):
+    out_ref = refs[-1]
     low = low_half()
     stripe, spot = place
     for c in range(halves):
@@ -148,49 +151,49 @@
         out_shape=jax.ShapeDtypeStruct(
             (halves * cols * LANES, pieces // 4 * each), jnp.float32
         ),
-        in_specs=[SCALARS, SCALARS, WHOLE, ANYWHERE],
+        in_specs=[SCALARS, SCALARS, WHOLE] + [ANYWHERE] * len(before),
         out_specs=WHOLE,
-        compiler_params=pltpu.CompilerParams(vmem_limit_bytes=8 * MIB),
-    )(shifts, peer, arrived, before)
-
-
-def spread_kernel(terms, pieces, halves, cols, each, place, shift_ref, peer_ref, *refs):
+        compiler_params=pltpu.CompilerParams(vmem_limit_bytes=ROOM),
+    )(shifts, peer, arrived, *before)
+
+
+def spread_kernel(terms, pieces, halves, cols, first, starts, each, shift_ref, *refs):
     low = low_half()
-    stripe, spot = place
     in_refs, out_refs, rows = refs[:terms], refs[terms:-1], refs[-1]
+    many = len(out_refs)
     for c in range(halves):
-        for u in range(cols):
-            shifts = [shift_ref[c * 2 * cols + 2 * u + h] for h in range(2)]
-            at = (c * cols + u) * LANES
-            block = []
-            for k in range(LANES // stripe):
-                where = pl.multiple_of(spot(at // stripe + k, peer_ref[0]) * stripe, stripe)
-                block.append(sum(ref[pl.ds(where, stripe), :] for ref in in_refs))
-            rows[c * cols + u] = jnp.concatenate(block, axis=0).T
+        for u in range(many):
+            shifts = [shift_ref[c * 2 * cols + 2 * (first + u) + h] for h in range(2)]
+            block = 0.0
+            for ref, start in zip(in_refs, starts):
+                at = start[c] + u * LANES
+                block = block + ref[at : at + LANES, :]
+            rows[c * many + u] = block.T
             for r in range(pieces):
                 parts = []
                 for s in shifts:
                     place = lax.rem(r - s + pieces, pieces) // 4
                     start = pl.multiple_of(place * each, each)
-                    parts.append(rows[c * cols + u, pl.ds(start, each), :])
+                    parts.append(rows[c * many + u, pl.ds(start, each), :])
                 out_refs[u][halves * r + c] = jnp.where(low, parts[0], parts[1])
 
 
-def spread(shifts, peer, place, terms, pieces, halves):
-    width, samples = terms[0].shape
-    cols = width // halves // LANES
+def spread(shifts, terms, starts, pieces, halves, cols, first, many):
+    samples = terms[0].shape[1]
     each = samples * 4 // pieces
     return pl.pallas_call(
-        functools.partial(spread_kernel, len(terms), pieces, halves, cols, each, place),
+        functools.partial(
+            spread_kernel, len(terms), pieces, halves, cols, first, starts, each
+        ),
         out_shape=[
             jax.ShapeDtypeStruct((pieces * halves, each, LANES), jnp.float32)
         ]
-        * cols,
-        in_specs=[SCALARS, SCALARS] + [WHOLE] * len(terms),
-        out_specs=[WHOLE] * cols,
-        scratch_shapes=[pltpu.VMEM((width // LANES, samples, LANES), jnp.float32)],
+        * many,
+        in_specs=[SCALARS] + [WHOLE] * len(terms),
+        out_specs=[WHOLE] * many,
+        scratch_shapes=[pltpu.VMEM((halves * many, samples, LANES), jnp.float32)],
         compiler_params=pltpu.CompilerParams(vmem_limit_bytes=10 * MIB),
-    )(shifts, peer, *terms)
+    )(shifts, *terms)
 
 
 def update_kernel(rows, part, devices, each, block, outs, idx_ref, grad_ref, *refs):
@@ -280,7 +283,7 @@
         scratch_shapes=[pltpu.VMEM((rows, LANES), jnp.float32)] * 3
         + [pltpu.VMEM((rows + 8, LANES), jnp.float32)] * 2
         + [pltpu.SemaphoreType.DMA((3, rows // block))] * 2,
-        compiler_params=pltpu.CompilerParams(vmem_limit_bytes=42 * MIB),
+        compiler_params=pltpu.CompilerParams(vmem_limit_bytes=ROOM),
         cost_estimate=pl.CostEstimate(
             flops=30 * rows * LANES, bytes_accessed=rows * LANES * 24, transcendentals=0
         ),
@@ -350,13 +353,14 @@
 
 
 def split_kernel(depth, tower_depth, order, pieces, peer_ref, *refs):
-    outs = refs[pieces : -3 - pieces]
-    piece_refs, (tower, gate, sem) = refs[-3 - pieces : -3], refs[-3:]
+    sources, far, refs = refs[:pieces], refs[pieces : pieces + 12], refs[pieces + 12 :]
+    piece_refs, outs, (tower, gate, sem, out_sem) = refs[:pieces], refs[pieces:-4], refs[-4:]
     loads = [
-        pltpu.make_async_copy(refs[k], piece_refs[k], sem.at[k]) for k in range(pieces)
+        pltpu.make_async_copy(sources[k], piece_refs[k], sem.at[k]) for k in range(pieces)
     ]
     for load in loads:
         load.start()
+    stores = [pltpu.make_async_copy(outs[k], far[k], out_sem.at[k]) for k in range(12)]
 
     def put(k, at, value):
         high, low = split(value)
@@ -389,6 +393,8 @@
                 if k + 8 < depth:
                     gate[row + 8 : row + 16, :GATE_LANES] = both[:, GATE_LANES:]
         block += ref.shape[0]
+    for k in range(2):
+        stores[k].start()
     for b in range(outs[0].shape[0] // LANES):
         rows = slice(b * LANES, (b + 1) * LANES)
         for k in range(2):
@@ -399,6 +405,10 @@
     put(6, Ellipsis, gate[:, :GATE_LANES])
     put(8, Ellipsis, tower[...].T[:width])
     put(10, Ellipsis, gate[...].T[:GATE_LANES])
+    for k in range(2, 12):
+        stores[k].start()
+    for store in stores:
+        store.wait()
 
 
 def split_weights(pieces, peer, order, depth, tower_depth, tower_width):
@@ -408,43 +418,91 @@
     height = devices * tower_depth
     shapes = [(width, lots), (lots, width), (height, tower_width), (width, GATE_LANES)]
     shapes += [shapes[2][::-1], shapes[3][::-1]]
+    shapes = [shape for shape in shapes for _ in range(2)]
     return pl.pallas_call(
         functools.partial(split_kernel, depth, tower_depth, order, len(pieces)),
-        out_shape=[
-            jax.ShapeDtypeStruct(shape, jnp.bfloat16) for shape in shapes for _ in range(2)
-        ],
+        out_shape=[jax.ShapeDtypeStruct(shape, jnp.bfloat16) for shape in shapes],
         in_specs=[SCALARS] + [ANYWHERE] * len(pieces),
-        out_specs=[WHOLE] * 12,
+        out_specs=[FAR] * 12,
         scratch_shapes=[pltpu.VMEM(x.shape, x.dtype) for x in pieces]
+        + [pltpu.VMEM(shape, jnp.bfloat16) for shape in shapes]
         + [
             pltpu.VMEM((height, TOWER_LANES), jnp.float32),
             pltpu.VMEM((width, LANES), jnp.float32),
             pltpu.SemaphoreType.DMA((len(pieces),)),
+            pltpu.SemaphoreType.DMA((12,)),
         ],
-        compiler_params=pltpu.CompilerParams(vmem_limit_bytes=16 * MIB),
+        compiler_params=pltpu.CompilerParams(vmem_limit_bytes=ROOM),
     )(peer, *pieces)
 
 
 def forward_kernel(dims, member_ref, *refs):
     tasks, experts, mine, hidden_units, tower_units = dims
-    x_refs, refs = refs[:2], refs[2:]
-    weight, tower, gate = [(refs[2 * k], refs[2 * k + 1]) for k in range(3)]
-    bias_ref, pre_ref, prob_ref, upper_ref, part_ref, x_high, x_low, hid_ref = refs[6:]
+    x_refs, weight_far, late_far = refs[:2], refs[2:4], refs[4:9]
+    pre_far, upper_far, x_far, hid_far, (prob_ref, part_ref) = (
+        refs[9],
+        refs[10],
+        refs[11:13],
+        refs[13:15],
+        refs[15:17],
+    )
+    weight, pre, upper, x, hid, late, (in_sem, out_sem, late_sem) = (
+        refs[17:19],
+        refs[19],
+        refs[20],
+        refs[21:23],
+        refs[23:25],
+        refs[25:30],
+        refs[30:],
+    )
+    tower_high, tower_low, gate_high, gate_low, bias_ref = late
+    lates = [pltpu.make_async_copy(late_far[k], late[k], late_sem.at[k]) for k in range(5)]
+    lates[4].start()
+    lots = pre.shape[0]
+    tile = 256
+
+    def load(i, k):
+        at = pl.ds(i * tile, tile)
+        return pltpu.make_async_copy(weight_far[k].at[at], weight[k].at[at], in_sem.at[i, k])
+
+    for i in range(lots // tile):
+        for k in range(2):
+            load(i, k).start()
+    for k in range(4):
+        lates[k].start()
+    stores = [
+        pltpu.make_async_copy(a, b, out_sem.at[k])
+        for k, (a, b) in enumerate(zip([*x, upper], [*x_far, upper_far]))
+    ]
+
+    def tile_stores(at):
+        return [
+            pltpu.make_async_copy(a.at[at], b.at[at], out_sem.at[3 + k])
+            for k, (a, b) in enumerate(zip([pre, *hid], [pre_far, *hid_far]))
+        ]
+
     for k in range(2):
         at = slice(k * LANES, (k + 1) * LANES)
-        x_high[:, at], x_low[:, at] = split(x_refs[k][...])
-    lots = pre_ref.shape[0]
-    tile = 256
+        x[0][:, at], x[1][:, at] = split(x_refs[k][...])
+    for k in range(2):
+        stores[k].start()
+    lates[4].wait()
 
     def rows(i, carry):
         at = pl.ds(pl.multiple_of(i * tile, tile), tile)
-        pre = product([w[at, :] for w in weight], [x_high[...], x_low[...]]) + bias_ref[at, :]
-        pre_ref[at, :] = pre
-        hid_ref[at, :] = gelu(pre)
+        for k in range(2):
+            load(i, k).wait()
+        value = product([w[at, :] for w in weight], [x[0][...], x[1][...]]) + bias_ref[at, :]
+        pre[at, :] = value
+        hid[0][at, :], hid[1][at, :] = split(gelu(value))
+        for store in tile_stores(at):
+            store.start()
         return carry
 
     lax.fori_loop(0, lots // tile, rows, 0)
-    logits = product([g[...] for g in gate], [x_high[...], x_low[...]])
+    for k in range(4):
+        lates[k].wait()
+    logits = product([gate_high[...], gate_low[...]], [x[0][...], x[1][...]])
     total = logits.shape[1]
     logits = logits[: tasks * experts].reshape(tasks, experts, total)
     grown = jnp.exp(logits - jnp.max(logits, axis=1, keepdims=True))
@@ -456,13 +514,16 @@
         own = jnp.sum(
             jnp.where(which == member_ref[0] * mine + i, probs, 0.0), axis=1, keepdims=True
         )
-        hidden = hid_ref[i * hidden_units : (i + 1) * hidden_units, :]
-        upper = product([t[...] for t in tower], split(hidden))
-        upper_ref[i] = upper
-        part = part + own * upper.reshape(tasks, tower_units, total)
+        at = slice(i * hidden_units, (i + 1) * hidden_units)
+        value = product([tower_high[...], tower_low[...]], [h[at, :] for h in hid])
+        upper[i] = value
+        part = part + own * value.reshape(tasks, tower_units, total)
+    stores[2].start()
     part = part.reshape(tasks * tower_units, total)
     part_ref[0] = part[:, :LANES]
     part_ref[1] = part[:, LANES:]
+    for store in stores + tile_stores(slice(None)):
+        store.wait()
 
 
 def forward(dims, member, xs, weight, tower, gate, bias):
@@ -470,24 +531,32 @@
     lots = mine * hidden_units
     width = tasks * tower_units
     total = 2 * LANES
-    shapes = [
-        (lots, total),
-        (tasks * experts, total),
-        (mine, width, total),
-        (2, width, LANES),
+    deep = xs[0].shape[0]
+    far = [
+        ((lots, total), jnp.float32),
+        ((mine, width, total), jnp.float32),
+        ((deep, total), jnp.bfloat16),
+        ((deep, total), jnp.bfloat16),
+        ((lots, total), jnp.bfloat16),
+        ((lots, total), jnp.bfloat16),
     ]
+    near = [((tasks * experts, total), jnp.float32), ((2, width, LANES), jnp.float32)]
     return pl.pallas_call(
         functools.partial(forward_kernel, dims),
-        out_shape=[jax.ShapeDtypeStruct(shape, jnp.float32) for shape in shapes],
-        in_specs=[SCALARS] + [WHOLE] * 9,
-        out_specs=[WHOLE] * 4,
-        scratch_shapes=[pltpu.VMEM((xs[0].shape[0], total), jnp.bfloat16)] * 2
-        + [pltpu.VMEM((lots, total), jnp.float32)],
-        compiler_params=pltpu.CompilerParams(vmem_limit_bytes=16 * MIB),
+        out_shape=[jax.ShapeDtypeStruct(*x) for x in far + near],
+        in_specs=[SCALARS, WHOLE, WHOLE] + [FAR] * 7,
+        out_specs=[FAR] * 6 + [WHOLE] * 2,
+        scratch_shapes=[pltpu.VMEM(weight[0].shape, jnp.bfloat16)] * 2
+        + [pltpu.VMEM(*x) for x in far]
+        + [pltpu.VMEM(v.shape, v.dtype) for v in (*tower, *gate, bias)]
+        + [
+            pltpu.SemaphoreType.DMA((lots // 256, 2)),
+            pltpu.SemaphoreType.DMA((6,)),
+            pltpu.SemaphoreType.DMA((5,)),
+        ],
+        compiler_params=pltpu.CompilerParams(vmem_limit_bytes=ROOM),
         cost_estimate=pl.CostEstimate(
-            flops=8 * lots * xs[0].shape[0] * total,
-            bytes_accessed=12 * MIB,
-            transcendentals=lots * total,
+            flops=8 * lots * deep * total, bytes_accessed=12 * MIB, transcendentals=lots * total
         ),
     )(member, *xs, *weight, *tower, *gate, bias)
 
@@ -536,13 +605,35 @@
     )(weight_total, first, second, bias, out, last, keep, targets)
 
 
-def backward_kernel(dims, member_ref, *refs):
+def backward_kernel(dims, place, member_ref, peer_ref, *refs):
     tasks, experts, mine, hidden_units, tower_units = dims
+    stripe, spot = place
     width = tasks * tower_units
-    packed_refs, refs = refs[:2], refs[2:]
-    pre_ref, prob_ref, upper_ref = refs[:3]
-    weight, tower, gate = [(refs[3 + 2 * k], refs[4 + 2 * k]) for k in range(3)]
-    d_pre_ref, spread_ref, logit_ref, near_ref, far_ref, high_ref, low_ref = refs[9:]
+    packed_refs, prob_ref, (tower_high, tower_low, gate_high, gate_low), far_in = (
+        refs[:2],
+        refs[2],
+        refs[3:7],
+        refs[7:11],
+    )
+    far_out, (logit_ref, near_ref, far_ref), refs = refs[11:15], refs[15:18], refs[18:]
+    pre, upper, weight, d_pre, spreads, (in_sem, out_sem) = (
+        refs[0],
+        refs[1],
+        refs[2:4],
+        refs[4:6],
+        refs[6:8],
+        refs[8:],
+    )
+    loads = [
+        pltpu.make_async_copy(a, b, in_sem.at[k])
+        for k, (a, b) in enumerate(zip(far_in, [upper, pre, *weight]))
+    ]
+    for load in loads:
+        load.start()
+    stores = [
+        pltpu.make_async_copy(a, b, out_sem.at[k])
+        for k, (a, b) in enumerate(zip([*d_pre, *spreads], far_out))
+    ]
     total = 2 * LANES
     packed = jnp.concatenate([ref[...] for ref in packed_refs], axis=1)
     d_inner = packed[:width].reshape(tasks, tower_units, total)
@@ -550,104 +641,121 @@
     probs = prob_ref[...].reshape(tasks, experts, total)
     which = lax.broadcasted_iota(jnp.int32, probs.shape, 1)
     d_logits = jnp.zeros(probs.shape, jnp.float32)
+    loads[0].wait()
     for i in range(mine):
         chosen = which == member_ref[0] * mine + i
         own = jnp.sum(jnp.where(chosen, probs, 0.0), axis=1, keepdims=True)
-        d_prob = jnp.sum(d_inner * upper_ref[i].reshape(d_inner.shape), axis=1)
+        d_prob = jnp.sum(d_inner * upper[i].reshape(d_inner.shape), axis=1)
         d_logit = own * (d_prob - mean)[:, None, :]
         d_logits = jnp.where(chosen, d_logit, d_logits)
-        spreads = (d_inner * own).reshape(width, total)
-        spread_ref[i] = spreads
+        value = split((d_inner * own).reshape(width, total))
+        spreads[0][i], spreads[1][i] = value
+        if i == 0:
+            loads[1].wait()
         at = slice(i * hidden_units, (i + 1) * hidden_units)
-        d_hidden = product([t[...] for t in tower], split(spreads))
-        d_pre = d_hidden * gelu_slope(pre_ref[at, :])
-        d_pre_ref[at, :] = d_pre
-        high_ref[at, :], low_ref[at, :] = split(d_pre)
+        d_hidden = product([tower_high[...], tower_low[...]], value)
+        value = d_hidden * gelu_slope(pre[at, :])
+        d_pre[0][at, :], d_pre[1][at, :] = split(value)
+    for store in stores:
+        store.start()
     d_logits = d_logits.reshape(tasks * experts, total)
     d_logits = jnp.concatenate(
         [d_logits, jnp.zeros((GATE_LANES - tasks * experts, total), jnp.float32)], axis=0
     )
     logit_ref[...] = d_logits
     d_logits = split(d_logits)
+    for k in range(2, 4):
+        loads[k].wait()
     tile = 256
 
     def rows(i, carry):
         at = pl.ds(pl.multiple_of(i * tile, tile), tile)
-        value = product([w[at, :] for w in weight], [high_ref[...], low_ref[...]])
-        value = value + product([g[at, :] for g in gate], d_logits)
-        near_ref[at, :] = value[:, :LANES]
-        far_ref[at, :] = value[:, LANES:]
+        value = product([w[at, :] for w in weight], [d_pre[0][...], d_pre[1][...]])
+        value = value + product([gate_high[at, :], gate_low[at, :]], d_logits)
+        for k in range(tile // stripe):
+            to = pl.ds(
+                pl.multiple_of(spot(i * (tile // stripe) + k, peer_ref[0]) * stripe, stripe),
+                stripe,
+            )
+            near_ref[to, :] = value[k * stripe : (k + 1) * stripe, :LANES]
+            far_ref[to, :] = value[k * stripe : (k + 1) * stripe, LANES:]
         return carry
 
     lax.fori_loop(0, near_ref.shape[0] // tile, rows, 0)
-
-
-def backward(dims, member, packed, pre, probs, upper, weight, tower, gate):
+    for store in stores:
+        store.wait()
+
+
+def backward(dims, place, member, peer, packed, pre, probs, upper, weight, tower, gate):
     tasks, experts, mine, hidden_units, tower_units = dims
     lots = mine * hidden_units
+    width = tasks * tower_units
     depth = weight[0].shape[0]
     total = 2 * LANES
-    shapes = [
-        (lots, total),
-        (mine, tasks * tower_units, total),
-        (GATE_LANES, total),
-        (depth, LANES),
-        (depth, LANES),
+    far = [((lots, total), jnp.bfloat16)] * 2 + [((mine, width, total), jnp.bfloat16)] * 2
+    near = [
+        ((GATE_LANES, total), jnp.float32),
+        ((depth, LANES), jnp.float32),
+        ((depth, LANES), jnp.float32),
     ]
     return pl.pallas_call(
-        functools.partial(backward_kernel, dims),
-        out_shape=[jax.ShapeDtypeStruct(shape, jnp.float32) for shape in shapes],
-        in_specs=[SCALARS] + [WHOLE] * 11,
-        out_specs=[WHOLE] * 5,
-        scratch_shapes=[pltpu.VMEM((lots, total), jnp.bfloat16)] * 2,
-        compiler_params=pltpu.CompilerParams(vmem_limit_bytes=16 * MIB),
+        functools.partial(backward_kernel, dims, place),
+        out_shape=[jax.ShapeDtypeStruct(*x) for x in far + near],
+        in_specs=[SCALARS, SCALARS] + [WHOLE] * 7 + [FAR] * 4,
+        out_specs=[FAR] * 4 + [WHOLE] * 3,
+        scratch_shapes=[pltpu.VMEM(pre.shape, jnp.float32), pltpu.VMEM(upper.shape, jnp.float32)]
+        + [pltpu.VMEM(weight[0].shape, jnp.bfloat16)] * 2
+        + [pltpu.VMEM(*x) for x in far]
+        + [pltpu.SemaphoreType.DMA((4,))] * 2,
+        compiler_params=pltpu.CompilerParams(vmem_limit_bytes=ROOM),
         cost_estimate=pl.CostEstimate(
             flops=8 * lots * depth * total, bytes_accessed=12 * MIB, transcendentals=lots * total
         ),
-    )(member, *packed, pre, probs, upper, *weight, *tower, *gate)
-
-
-def gradient_kernel(dims, depth, tower_depth, order, outs, peer_ref, *refs):
+    )(member, peer, *packed, probs, *tower, *gate, upper, pre, *weight)
+
+
+def gradient_kernel(dims, depth, tower_depth, order, outs, befores, peer_ref, *refs):
     mine, hidden_units = dims
-    logits, sources, refs = refs[:2], refs[2:12], refs[13:]
+    logits, sources, refs = refs[:2], refs[2:18], refs[18 + befores :]
     weight_refs, bias_ref, refs = refs[:outs], refs[outs], refs[outs + 1 :]
-    held, (x_high, x_low, d_high, d_low, tower, in_sem) = refs[:10], refs[10:]
-    loads = [pltpu.make_async_copy(sources[k], held[k], in_sem.at[k]) for k in range(10)]
+    x, d_pre, hid, spreads, (tower, in_sem) = refs[:2], refs[2:4], refs[4:6], refs[6:8], refs[8:]
+    half = 2 * LANES
+    places = [
+        pair[k].at[(Ellipsis, pl.ds(h * half, half))] if pair is not spreads else pair[k].at[h]
+        for pair in (x, d_pre, hid, spreads)
+        for h in range(2)
+        for k in range(2)
+    ]
+    loads = [pltpu.make_async_copy(sources[k], places[k], in_sem.at[k]) for k in range(16)]
     for load in loads:
         load.start()
-    lots = d_high.shape[0]
+    lots = d_pre[0].shape[0]
     tile = LANES
     share = tile // depth
-    tiles = x_high.shape[0] // tile
+    tiles = x[0].shape[0] // tile
     gate_at = -(-tower_depth // 8) * TOWER_LANES
     gate_end = gate_at + depth // 8 * GATE_LANES
-    for k in range(4):
-        at = slice(k * LANES, (k + 1) * LANES)
-        loads[k].wait()
-        x_high[:, at], x_low[:, at] = split(held[k][...])
-    bias = None
-    for k in range(2):
-        at = slice(2 * k * LANES, 2 * (k + 1) * LANES)
-        loads[4 + k].wait()
-        value = held[4 + k][...]
-        d_high[:, at], d_low[:, at] = split(value)
-        part = jnp.sum(value, axis=1, keepdims=True)
-        bias = part if bias is None else bias + part
-    bias_ref[...] = bias
-    for k in range(6, 10):
-        loads[k].wait()
+    for load in loads[:8]:
+        load.wait()
 
     def parts(i):
         if outs == 1:
             return [(weight_refs[0], (), i * share, share)]
         high, middle, low = i // 4, i // 2 % 2, i % 2
-        return [(weight_refs[low], (high, middle), 0, 2), (weight_refs[2 + middle], (high, low), 0, 2)]
+        return [(weight_refs[low], (middle, high), 0, 2), (weight_refs[2 + middle], (low, high), 0, 2)]
 
     wide = 256
 
     def columns(n, carry):
         at = pl.ds(pl.multiple_of(n * wide, wide), wide)
-        value = product([x_high[...], x_low[...]], [d_high[at, :], d_low[at, :]], True)
+        value = product([x[0][...], x[1][...]], [d[at, :] for d in d_pre], True)
+        ones = jnp.ones((8, x[0].shape[1]), jnp.bfloat16)
+        bias_ref[:, at] = sum(
+            lax.dot_general(
+                ones, d[at, :], (((1,), (1,)), ((), ())), preferred_element_type=jnp.float32
+            )
+            for d in d_pre
+        )
         for i in range(tiles):
             row = i * tile
             for ref, where, first, many in parts(i):
@@ -659,12 +767,14 @@
 
     lax.fori_loop(0, lots // wide, columns, 0)
     d_logits = split(jnp.concatenate([ref[...] for ref in logits], axis=1))
-    gates = product([x_high[...], x_low[...]], d_logits, True)
+    gates = product([x[0][...], x[1][...]], d_logits, True)
+    for load in loads[8:]:
+        load.wait()
     value = None
     for i in range(mine):
         for k in range(2):
-            hidden = gelu(held[6 + k][i * hidden_units : (i + 1) * hidden_units, :])
-            part = product(split(hidden), split(held[8 + k][i]), True)
+            at = (slice(i * hidden_units, (i + 1) * hidden_units), slice(k * half, (k + 1) * half))
+            part = product([h[at] for h in hid], [p[k, i] for p in spreads], True)
             value = part if value is None else value + part
     tower[...] = jnp.concatenate(
         [value, jnp.zeros((value.shape[0], TOWER_LANES - value.shape[1]), jnp.float32)], axis=1
@@ -699,26 +809,28 @@
     counted = order[1]
     shape = (2, 2, 2, tall, lots) if counted else (devices, tall, lots)
     outs = 4 if counted else 1
+    total = 4 * LANES
+    held = [(devices * depth, total), (lots, total), (lots, total), (2,) + operands[-1].shape]
     return pl.pallas_call(
-        functools.partial(gradient_kernel, dims, depth, tower_depth, order, outs),
+        functools.partial(
+            gradient_kernel, dims, depth, tower_depth, order, outs, len(before)
+        ),
         out_shape=[jax.ShapeDtypeStruct(shape, jnp.float32)] * outs
-        + [jax.ShapeDtypeStruct((lots, 1), jnp.float32)],
-        in_specs=[SCALARS, WHOLE, WHOLE] + [ANYWHERE] * 11,
+        + [jax.ShapeDtypeStruct((8, lots), jnp.float32)],
+        in_specs=[SCALARS, WHOLE, WHOLE] + [FAR] * 16 + [ANYWHERE] * len(before),
         out_specs=[WHOLE] * (outs + 1),
-        scratch_shapes=[pltpu.VMEM(x.shape, x.dtype) for x in operands]
-        + [pltpu.VMEM((devices * depth, 4 * LANES), jnp.bfloat16)] * 2
-        + [pltpu.VMEM((lots, 4 * LANES), jnp.bfloat16)] * 2
+        scratch_shapes=[pltpu.VMEM(x, jnp.bfloat16) for x in held for _ in range(2)]
         + [
             pltpu.VMEM((hidden_units, TOWER_LANES), jnp.float32),
-            pltpu.SemaphoreType.DMA((10,)),
+            pltpu.SemaphoreType.DMA((16,)),
         ],
-        compiler_params=pltpu.CompilerParams(vmem_limit_bytes=28 * MIB),
+        compiler_params=pltpu.CompilerParams(vmem_limit_bytes=ROOM),
         cost_estimate=pl.CostEstimate(
             flops=16 * lots * devices * depth * LANES,
             bytes_accessed=16 * MIB,
             transcendentals=0,
         ),
-    )(peer, *logits, *operands, before)
+    )(peer, *logits, *operands, *before)
 
 
 def swap_near(x):
@@ -735,10 +847,22 @@
     return blocks, swap_core(jnp.stack([blocks[1], blocks[3]]))
 
 
-def exchange_chips(state, member, after=0):
+def exchange_chips(state, member):
     blocks, other = state
     far = swap_near(jnp.stack([blocks[2], other[1]]))
     came = jnp.stack([blocks[0], other[0], far[0], far[1]])
+    return jnp.stack([lax.dynamic_index_in_dim(came, member ^ i, 0, False) for i in range(4)])
+
+
+def exchange_group(x, member, after):
+    blocks = [lax.dynamic_index_in_dim(x, member ^ i, 0, False) for i in range(4)]
+    came = [
+        blocks[0],
+        swap_core(blocks[1]),
+        swap_near(blocks[2]),
+        lax.ppermute(blocks[3], ("near", "col"), [(i, i ^ 3) for i in range(4)]),
+    ]
+    came = jnp.stack(came)
     member = member + after
     return jnp.stack([lax.dynamic_index_in_dim(came, member ^ i, 0, False) for i in range(4)])
 
@@ -753,14 +877,9 @@
     return [swap_peer(x, bit) for bit in (1, 2, 4)]
 
 
-def gather_peers(x, one, two, top):
-    cut = x.shape[0] // 2
-
-    def plane(own, one, two):
-        far = [swap_peer(two[:cut], 1), swap_peer(one[cut:], 2)]
-        return [own, one, two] + far
-
-    return plane(x, one, two) + plane(top, swap_peer(top, 1), swap_peer(top, 2))
+def gather_plane(own, one, two):
+    cut = own.shape[0] // 2
+    return [own, one, two, swap_peer(two[:cut], 1), swap_peer(one[cut:], 2)]
 
 
 def both_sums(x, far, axis):
@@ -828,7 +947,12 @@
         high, near, low = stripe // (2 * rest), stripe // rest % 2, stripe % rest
         return ((high * rest + low) ^ own) * 2 + near
 
+    def natural(stripe, own):
+        number, near = (stripe // 2) ^ own, stripe % 2
+        return (number // rest * 2 + near) * rest + number % rest
+
     place = (halves * depth, spot)
+    place_back = (halves * depth, natural)
 
     order = (rest, counted)
 
@@ -853,11 +977,6 @@
     message = padded(message, wide).reshape(devices, wide // LANES, LANES)
     shifts = lookup_ids[0, :, 0] // rows_here
 
-    asked = lax.all_to_all(message, ALL, 0, 0, tiled=True).reshape(devices, wide)
-    idx = asked[:, : tabs_here * each].reshape(devices, tabs_here, each)
-    idx = idx.swapaxes(0, 1).reshape(-1).astype(jnp.int32)
-    weight_total = jnp.sum(asked[:, tabs_here * each])
-
     lots = mine * hidden_units
     send = expert_weight.reshape(members, mine, depth, hidden_units).swapaxes(1, 2)
     send = send.reshape(members, depth, lots)
@@ -869,17 +988,23 @@
     send = jnp.concatenate(
         [send, jnp.broadcast_to(small[None], (members,) + small.shape)], axis=1
     )
-    ready = jnp.minimum(idx[0], 0)
-    shared = exchange_chips(exchange_cores(send, member), member, ready)
+    asked = lax.all_to_all(message, ALL, 0, 0, tiled=True).reshape(devices, wide)
+    idx = asked[:, : tabs_here * each].reshape(devices, tabs_here, each)
+    idx = idx.swapaxes(0, 1).reshape(-1).astype(jnp.int32)
+    weight_total = jnp.sum(asked[:, tabs_here * each])
+
+    shared = exchange_group(send, member, jnp.minimum(idx[0], 0))
     if counted:
-        round_one = near_peers(shared)
-        parts = gather_peers(shared, *round_one)
+        one, two, top = near_peers(shared)
+        parts = gather_plane(shared, one, two)
+        early = [one, two, top]
+        parts += gather_plane(top, swap_peer(top, 1), swap_peer(top, 2))
     else:
-        round_one = [shared]
+        early = [shared]
         parts = [lax.all_gather(shared, PEERS, axis=0, tiled=True)]
     bias_mine = lax.dynamic_slice_in_dim(expert_bias, member * mine, mine, 0).reshape(lots, 1)
 
-    picked = fence(gather_rows(idx, tables, devices, each), round_one)
+    picked = fence(gather_rows(idx, tables, devices, each), early)
     cols = width_here // LANES
     arrived = lax.all_to_all(
         picked.reshape(devices, cols * each, LANES), ALL, 0, 0, tiled=True
@@ -890,17 +1015,22 @@
     weight_pair, weight_turned, tower_pair, gate_pair, tower_turned, gate_turned = [
         split_parts[2 * k : 2 * k + 2] for k in range(6)
     ]
-    mine_x = pool(shifts, peer_at, place, arrived, split_parts[0])
+    mine_x = pool(shifts, peer_at, place, arrived, parts)
     near_x = swap_near(mine_x)
-    halves_x = [(mine_x, swap_core(mine_x)), (near_x, swap_core(near_x))]
+    halves_x = [(mine_x, swap_core(mine_x))]
 
     dims = (tasks, experts, mine, hidden_units, tower_units)
     member_at = member.astype(jnp.int32).reshape(1)
-    runs = [
-        forward(dims, member_at, x, weight_turned, tower_turned, gate_turned, bias_mine)
-        for x in halves_x
-    ]
-    part_own, part_near = runs[0][3], runs[1][3]
+    def half_forward(x):
+        return forward(
+            dims, member_at, x, weight_turned, tower_turned, gate_turned, bias_mine
+        )
+
+    runs = [half_forward(halves_x[0])]
+    near_x = fence(near_x, [runs[0][7]])
+    halves_x.append((near_x, swap_core(near_x)))
+    runs.append(half_forward(halves_x[1]))
+    part_own, part_near = runs[0][7], runs[1][7]
     first = part_own[0] + swap_core(part_own[1])
     second = swap_near(part_near[0] + swap_core(part_near[1]))
     packed, grad_output, grad_head, few = score_step(
@@ -915,31 +1045,61 @@
         targets.T,
     )
 
-    near_packed = swap_near(packed)
-    halves_packed = [(packed, swap_core(packed)), (near_packed, swap_core(near_packed))]
+    core_packed = swap_core(packed)
+    halves_packed = [(packed, core_packed), (swap_near(packed), swap_near(core_packed))]
 
     def half_back(k, packed):
         run = runs[k]
         return backward(
             dims,
+            place_back,
             member_at,
+            peer_at,
             packed,
             run[0],
+            run[6],
             run[1],
-            run[2],
             weight_pair,
             tower_pair,
             gate_pair,
         )
 
-    back_near = half_back(1, halves_packed[1])
-    (near_in, far_in) = back_near[3:]
+    back = [half_back(0, halves_packed[0])]
+    near_first, near_second = halves_packed[1]
+    back.append(half_back(1, (fence(near_first, [back[0][4]]), near_second)))
+    near_in, far_in = back[1][5:]
     leaving = near_in + swap_core(far_in)
-    beyond = swap_near(leaving)
-    back = [half_back(0, (fence(packed, [leaving]), halves_packed[0][1])), back_near]
-    d_terms = [back[0][3], swap_core(back[0][4]), beyond]
-
-    returned = list(spread(shifts, peer_at, place, d_terms, pieces, halves))
+
+    half_width = width_here
+    ahead = jnp.concatenate(
+        [leaving[c * half_width : c * half_width + LANES] for c in range(halves)], axis=0
+    )
+    others = jnp.concatenate(
+        [leaving[c * half_width + LANES : (c + 1) * half_width] for c in range(halves)], axis=0
+    )
+    ahead = swap_near(ahead)
+    others = swap_near(others)
+    terms = [back[0][5], swap_core(back[0][6])]
+
+    def starts(first, stride):
+        whole = tuple(c * half_width + first for c in range(halves))
+        return (whole, whole, tuple(c * stride for c in range(halves)))
+
+    returned = list(
+        spread(shifts, terms + [ahead], starts(0, LANES), pieces, halves, cols, 0, 1)
+    )
+    returned += list(
+        spread(
+            shifts,
+            terms + [fence(others, returned)],
+            starts(LANES, half_width - LANES),
+            pieces,
+            halves,
+            cols,
+            1,
+            cols - 1,
+        )
+    )
 
     *sums, grad_bias = gradients(
         (mine, hidden_units),
@@ -948,21 +1108,18 @@
         tower_depth,
         order,
         peer_at,
-        [x[2] for x in back],
-        [
-            *halves_x[0],
-            *halves_x[1],
-            *[x[0] for x in back],
-            *[x[0] for x in runs],
-            *[x[1] for x in back],
-        ],
-        returned[0],
+        [x[4] for x in back],
+        [x[k] for x in runs for k in (2, 3)]
+        + [x[k] for x in back for k in (0, 1)]
+        + [x[k] for x in runs for k in (4, 5)]
+        + [x[k] for x in back for k in (2, 3)],
+        [returned[0], others],
     )
 
     grad_head = jnp.concatenate([grad_head.reshape(tasks, tower_units), few[0]], axis=1)
     same = jnp.concatenate(
         [
-            grad_bias.reshape(-1),
+            grad_bias[0],
             grad_head.reshape(-1),
             grad_output.reshape(-1),
             jnp.sum(few[1]).reshape(1),
@@ -983,7 +1140,7 @@
     else:
         kept = []
     for u in range(cols):
-        later = returned[u + 2 : u + 3]
+        later = returned[2:] if u == 0 else []
         new_tables, handed = update_part(
             idx,
             came[u],
@@ -996,9 +1153,11 @@
         )
         kept = handed[: len(kept)]
         if later:
-            came.append(lax.all_to_all(handed[-1], ALL, 0, 0, tiled=True))
+            came += [
+                lax.all_to_all(x, ALL, 0, 0, tiled=True) for x in handed[len(handed) - len(later) :]
+            ]
         if counted and u == 0:
-            a, b = [both_sums(x, y, 1) for x, y in zip(kept, far)]
+            a, b = [both_sums(x, y, 0) for x, y in zip(kept, far)]
             kept, before = [a[0], b[0]], [a[1], b[1]]
             far = [swap_peer(a[1], 2), swap_peer(b[1], 1)]
         if counted and u == 1:

time: 385 us -> 369 us (0.958)
  Pallas kernels: 131 us -> 160 us
  local copies, waits for them, and re-layouts: 51.2 us -> 25 us
  waiting for transfers between devices: 117 us -> 103 us
  starting transfers between devices: 59.6 us -> 54.1 us
    unnamed x168 -> x140, local copies, waits for them, and re-layouts: 39.2 us -> 16.7 us
    ppermute x6 -> x8, waiting for transfers between devices: 35.3 us -> 17.7 us  [swap_near(): return lax.ppermute(x, 'near', [(i, i ^ 1) for i in range(count)])]
    pallas_call x2, Pallas kernels: 8.58 us -> 16.9 us  [forward(): pl.pallas_call(functools.partial(forward_kernel, dims), out_shape=[jax.Sh...]
    pallas_call x2, Pallas kernels: 8.84 us -> 16.5 us  [backward(): pl.pallas_call(functools.partial(backward_kernel, dims, place), out_shape...]
    pallas_call x1, Pallas kernels: 8.66 us -> 14.4 us  [gradients(): pl.pallas_call(functools.partial(gradient_kernel, dims, depth, tower_dept...]
    ppermute x6 -> x8, starting transfers between devices: 8 us -> 6.31 us  [swap_near(): return lax.ppermute(x, 'near', [(i, i ^ 1) for i in range(count)])]
  transfers between devices with their start and end apart: 36 -> 38, of which waited for: 19 -> 15; matrix products, arithmetic and copies ran while one was open for 8% -> 7% of each run, Pallas kernels for 29% -> 38%
where the time goes in v3:
time: 369 us; the launch traced here: 368 us
  Pallas kernels  160 us (43%)
  waiting for transfers between devices  103 us (28%)
  starting transfers between devices  54.1 us (15%)
  local copies, waits for them, and re-layouts  25 us (7%)
  other arithmetic  22.3 us (6%)
    pallas_call x4, Pallas kernels, update_part(): pl.pallas_call(functools.partial(update_kernel, rows, part, devices, each...  80.7 us
    ppermute x12, waiting for transfers between devices, swap_peer(): lax.ppermute(x, 'rest', [(i, i ^ bit) for i in range(lax.axis_size('rest'...  47.3 us
    ppermute x2, waiting for transfers between devices, swap_peer(): return lax.ppermute(x, 'hi', [(0, 1), (1, 0)])  24.7 us
    ppermute x8, waiting for transfers between devices, swap_near(): return lax.ppermute(x, 'near', [(i, i ^ 1) for i in range(count)])  17.7 us
    pallas_call x2, Pallas kernels, forward(): pl.pallas_call(functools.partial(forward_kernel, dims), out_shape=[jax.Sh...  16.9 us
    unnamed x140, local copies, waits for them, and re-layouts  16.7 us
    pallas_call x2, Pallas kernels, backward(): pl.pallas_call(functools.partial(backward_kernel, dims, place), out_shape...  16.5 us
    pallas_call x1, Pallas kernels, gather_rows(): pl.pallas_call(functools.partial(gather_kernel, rows, cols, devices, each...  14.9 us
  transfers between devices with their start and end apart: 38, of which 15 were waited for; matrix products, arithmetic and copies ran while one was open for 7% of the time, Pallas kernels for 38%

profile of v3, /device:TPU:0, one launch (start us, length us, event | category | flops | bytes accessed | tf_op | source)
XLA Modules:
  0.0 367.7 jit_solution(8039166372954884414)
XLA Ops:
  10.2 6.0 %all-to-all-start = ((f32[32,8,128]{2,1,0:T(8,128)}), f32[32,8,128]{2,1,0:T(8,128)S(1)}, u32[]{:S(2)}, u32[]{:S(2)}) async-start(f32[32,8,128]{2,1,0:T(8,128)} %bitcast.65), calls=%async_computation | async-start | bytes 262144 | tf_op jit(solution)/shard_map/all_to_all | solution.py:991
  16.3 8.1 %all-to-all-done = f32[32,8,128]{2,1,0:T(8,128)S(1)} async-done(((f32[32,8,128]{2,1,0:T(8,128)}), f32[32,8,128]{2,1,0:T(8,128)S(1)}, u32[]{:S(2)}, u32[]{:S(2)}) %all-to-all-start) | async-done | bytes 131104 | tf_op jit(solution)/shard_map/all_to_all | solution.py:991
  28.1 14.9 %shard_map.434.refs_0_ = f32[32,4,32,128]{3,2,1,0:T(8,128)} custom-call(s32[8192]{0:T(1024)} %copy-done.35, f32[16384,512]{1,0:T(8,128)} %refs_0_.7), custom_call_target="tpu_custom_call" | custom-call | bytes 67108864 | tf_op jit(solution)/shard_map/pallas_call | solution.py:107
  43.1 15.4 %collective-permute-done.5.refs_3_.refs_5_ = f32[4,40,1024]{2,1,0:T(8,128)S(1)} collective-permute-done((f32[4,40,1024]{2,1,0:T(8,128)S(1)}, f32[4,40,1024]{2,1,0:T(8,128)S(1)}, u32[]{:S(2)}, u32[]{:S(2)}) %collective-permute-start.5) | collective-permute-done | bytes 655392 | tf_op jit(solution)/shard_map/ppermute | solution.py:872
  69.6 31.6 %collective-permute-done.9.refs_7_ = f32[4,40,1024]{2,1,0:T(8,128)S(1)} collective-permute-done((f32[4,40,1024]{2,1,0:T(8,128)S(1)}, f32[4,40,1024]{2,1,0:T(8,128)S(1)}, u32[]{:S(2)}, u32[]{:S(2)}) %collective-permute-start.9) | collective-permute-done | bytes 655392 | tf_op jit(solution)/shard_map/ppermute | solution.py:873
  104.4 7.3 %collective-permute-done.6.refs_3_ = f32[2,40,1024]{2,1,0:T(8,128)S(1)} collective-permute-done((f32[2,40,1024]{2,1,0:T(8,128)S(1)}, f32[2,40,1024]{2,1,0:T(8,128)S(1)}, u32[]{:S(2)}, u32[]{:S(2)}) %collective-permute-start.6) | collective-permute-done | bytes 327712 | tf_op jit(solution)/shard_map/ppermute | solution.py:873
  111.7 6.5 %collective-permute-done.10.refs_8_ = f32[2,40,1024]{2,1,0:T(8,128)S(1)} collective-permute-done((f32[2,40,1024]{2,1,0:T(8,128)S(1)}, f32[2,40,1024]{2,1,0:T(8,128)S(1)}, u32[]{:S(2)}, u32[]{:S(2)}) %collective-permute-start.10) | collective-permute-done | bytes 327712 | tf_op jit(solution)/shard_map/ppermute | solution.py:873
  125.5 7.8 %shard_map.437 = (bf16[1024,1024]{1,0:T(8,128)(2,1)}, bf16[1024,1024]{1,0:T(8,128)(2,1)}, bf16[1024,1024]{1,0:T(8,128)(2,1)}, bf16[1024,1024]{1,0:T(8,128)(2,1)}...) custom-call(s32[1]{0:T(128)} %bitcast.7.peer_ref, ...), custom_call_target="tpu_custom_call" | custom-call | tf_op jit(solution)/shard_map/pallas_call | solution.py:422
  134.1 8.5 %shard_map.438 = (f32[1024,256]{1,0:T(8,128)}, f32[2,320,256]{2,1,0:T(8,128)}, bf16[1024,256]{1,0:T(8,128)(2,1)}, bf16[1024,256]{1,0:T(8,128)(2,1)}, bf16[1024,2...) custom-call(s32[1]{0:T(128)} %bitcast.6.member_ref, ...), custom_call_target="tpu_custom_call" | custom-call | flops 2147483648 | bytes 12582912 | tf_op jit(solution)/shard_map/pallas_call | solution.py:544
  146.3 8.4 %shard_map.440 = (f32[1024,256]{1,0:T(8,128)}, f32[2,320,256]{2,1,0:T(8,128)}, bf16[1024,256]{1,0:T(8,128)(2,1)}, bf16[1024,256]{1,0:T(8,128)(2,1)}, bf16[1024,2...) custom-call(s32[1]{0:T(128)} %bitcast.6.member_ref, ...), custom_call_target="tpu_custom_call" | custom-call | flops 2147483648 | bytes 12582912 | tf_op jit(solution)/shard_map/pallas_call | solution.py:544
  158.6 5.8 %collective-permute-done.17.second_ref = f32[320,128]{1,0:T(8,128)S(1)} collective-permute-done((f32[320,128]{1,0:T(8,128)S(1)}, f32[320,128]{1,0:T(8,128)S(1)}, u32[]{:S(2)}, u32[]{:S(2)}) %collective-permute-start.17) | collective-permute-done | bytes 163872 | tf_op jit(solution)/shard_map/ppermute | solution.py:838
  167.6 8.3 %shard_map.442 = (bf16[1024,256]{1,0:T(8,128)(2,1)}, bf16[1024,256]{1,0:T(8,128)(2,1)}, bf16[2,320,256]{2,1,0:T(8,128)(2,1)}, bf16[2,320,256]{2,1,0:T(8,128)(2,1...) custom-call(s32[1]{0:T(128)} %bitcast.6.member_ref, s32[1]{0:T(128)} %bitcast.7.peer_ref, ...), custom_call_target="tpu_custom_call" | custom-call | flops 2147483648 | bytes 12582912 | tf_op jit(solution)/shard_map/pallas_call | solution.py:701
  178.1 8.2 %shard_map.444 = (bf16[1024,256]{1,0:T(8,128)(2,1)}, bf16[1024,256]{1,0:T(8,128)(2,1)}, bf16[2,320,256]{2,1,0:T(8,128)(2,1)}, bf16[2,320,256]{2,1,0:T(8,128)(2,1...) custom-call(s32[1]{0:T(128)} %bitcast.6.member_ref, s32[1]{0:T(128)} %bitcast.7.peer_ref, ...), custom_call_target="tpu_custom_call" | custom-call | flops 2147483648 | bytes 12582912 | tf_op jit(solution)/shard_map/pallas_call | solution.py:701
  191.9 11.8 %collective-permute-done.23.refs_2_ = f32[256,128]{1,0:T(8,128)S(1)} collective-permute-done((f32[256,128]{1,0:T(8,128)S(1)}, f32[256,128]{1,0:T(8,128)S(1)}, u32[]{:S(2)}, u32[]{:S(2)}) %collective-permute-start.23) | collective-permute-done | bytes 131104 | tf_op jit(solution)/shard_map/ppermute | solution.py:838
  205.5 4.5 %all-to-all-start.2 = ((f32[32,32,128]{2,1,0:T(8,128)}), f32[32,32,128]{2,1,0:T(8,128)S(1)}, u32[]{:S(2)}, u32[]{:S(2)}) async-start(f32[32,32,128]{2,1,0:T(8,128)} %shard_map.445.refs_18_.refs_1_), calls=%async_computation.2 | async-start | bytes 1048576 | tf_op jit(solution)/shard_map/all_to_all | solution.py:1134
  210.8 14.4 %shard_map.446 = (f32[2,2,2,40,1024]{4,3,2,1,0:T(8,128)}, f32[2,2,2,40,1024]{4,3,2,1,0:T(8,128)}, f32[2,2,2,40,1024]{4,3,2,1,0:T(8,128)}, f32[2,2,2,40,1024]{4,3,2,1,0:T(8,128)}, f32[8,1024]{1,0:T(8,128)}) custom-call(s32[1]{0:T(128)} %bitcast.7.peer_ref, f32[64,256]{1,0:T(8,128)} %get-tuple-element.116.refs_1_.refs_0_, ...), custom_call_target="tpu_custom_call" | custom-call | flops 2147483648 | bytes 16777216 | tf_op jit(solution)/shard_map/pallas_call | solution.py:814
  237.6 3.7 %all-to-all-start.5 = ((f32[32,48,128]{2,1,0:T(8,128)}), f32[32,48,128]{2,1,0:T(8,128)S(1)}, u32[]{:S(2)}, u32[]{:S(2)}) async-start(f32[32,48,128]{2,1,0:T(8,128)} %pad_maximum_fusion), calls=%async_computation.5 | async-start | bytes 1572864 | tf_op jit(solution)/shard_map/all_to_all | solution.py:1134
  241.3 20.2 %shard_map.449 = (f32[16384,512]{1,0:T(8,128)}, f32[16384,512]{1,0:T(8,128)}, f32[16384,512]{1,0:T(8,128)}, f32[2,2,2,40,1024]{4,3,2,1,0:T(8,128)}, f32[2,2,2,40...) custom-call(s32[8192]{0:T(1024)} %copy-done.35, ...), custom_call_target="tpu_custom_call", output_to_operand_aliasing={{3}: (5, {}), {4}: (6, {}), {5}: (7, {}), {6}: (8, {})} | custom-call | flops 62914560 | bytes 50331648 | tf_op jit(solution)/shard_map/pallas_call | solution.py:276
  271.8 3.7 %all-to-all-start.4 = ((f32[32,32,128]{2,1,0:T(8,128)}), f32[32,32,128]{2,1,0:T(8,128)S(1)}, u32[]{:S(2)}, u32[]{:S(2)}) async-start(f32[32,32,128]{2,1,0:T(8,128)} %get-tuple-element.144), calls=%async_computation.4 | async-start | bytes 1048576 | tf_op jit(solution)/shard_map/all_to_all | solution.py:1157
  275.6 20.2 %shard_map.450 = (f32[16384,512]{1,0:T(8,128)}, f32[16384,512]{1,0:T(8,128)}, f32[16384,512]{1,0:T(8,128)}, f32[2,2,40,1024]{3,2,1,0:T(8,128)}, f32[2,2,40,1024]{3,2,1,0:T(8,128)}) custom-call(s32[8192]{0:T(1024)} %copy-done.35, f32[32,48,128]{2,1,0:T(8,128)} %copy-done.20, ...), custom_call_target="tpu_custom_call", output_to_operand_aliasing={{0}: (5, {}), {1}: (6, {}), {2}: (7, {}), {3}: (8, {}), {4}... | custom-call | flops 62914560 | bytes 50331648 | tf_op jit(solution)/shard_map/pallas_call | solution.py:276
  303.0 4.0 %all-to-all-start.3 = ((f32[32,32,128]{2,1,0:T(8,128)}), f32[32,32,128]{2,1,0:T(8,128)S(1)}, u32[]{:S(2)}, u32[]{:S(2)}) async-start(f32[32,32,128]{2,1,0:T(8,128)} %get-tuple-element.143), calls=%async_computation.3 | async-start | bytes 1048576 | tf_op jit(solution)/shard_map/all_to_all | solution.py:1157
  307.0 20.1 %shard_map.451 = (f32[16384,512]{1,0:T(8,128)}, f32[16384,512]{1,0:T(8,128)}, f32[16384,512]{1,0:T(8,128)}, f32[4,40,1024]{2,1,0:T(8,128)}) custom-call(s32[8192]{0:T(1024)} %copy-done.35, f32[32,32,128]{2,1,0:T(8,128)} %copy-done.27, f32[16384,512]{1,0:T(8,128)} %refs_0_.7, ...), custom_call_target="tpu_custom_call", output_to_operand_aliasing={{0}: (5, {}), {1}: (6, {}), {2}: (7, {}), {3}: (8, {})} | custom-call | flops 62914560 | bytes 50331648 | tf_op jit(solution)/shard_map/pallas_call | solution.py:276
  327.2 9.4 %collective-permute-done.29 = f32[4,40,1024]{2,1,0:T(8,128)S(1)} collective-permute-done((f32[4,40,1024]{2,1,0:T(8,128)S(1)}, f32[4,40,1024]{2,1,0:T(8,128)S(1)}, u32[]{:S(2)}, u32[]{:S(2)}) %collective-permute-start.29) | collective-permute-done | bytes 655392 | tf_op jit(solution)/shard_map/ppermute | solution.py:872
  343.3 20.1 %shard_map.452 = (f32[16384,512]{1,0:T(8,128)}, f32[16384,512]{1,0:T(8,128)}, f32[16384,512]{1,0:T(8,128)}) custom-call(s32[8192]{0:T(1024)} %copy-done.35, f32[32,32,128]{2,1,0:T(8,128)} %copy-done.28, f32[16384,512]{1,0:T(8,128)} %refs_0_.7, f32[16384,512]{1,0:T(8,128)} %refs_1_.7, ...), custom_call_target="tpu_custom_call", output_to_operand_aliasing={{0}: (5, {}), {1}: (6, {}), {2}: (7, {})} | custom-call | flops 62914560 | bytes 50331648 | tf_op jit(solution)/shard_map/pallas_call | solution.py:276
  (320 shorter events, 95.5 us)
Async XLA Ops:
  3.1 13.2 %collective-permute-start.2 = (f32[40,1024]{1,0:T(8,128)S(1)}, f32[40,1024]{1,0:T(8,128)S(1)}, u32[]{:S(2)}, u32[]{:S(2)}) collective-permute-start(f32[40,1024]{1,0:T(8,128)S(1)} %get-tuple-element.283), channel_id=1, source_target_pairs={{0,9},{1,8},{8,1},{9,0},{2,11},{3,10},{10,3},{11,2},{4,13},{5,12},... | collective-permute-start | bytes 491528 | tf_op jit(solution)/shard_map/ppermute | solution.py:863
  10.2 14.3 %all-to-all-start = ((f32[32,8,128]{2,1,0:T(8,128)}), f32[32,8,128]{2,1,0:T(8,128)S(1)}, u32[]{:S(2)}, u32[]{:S(2)}) async-start(f32[32,8,128]{2,1,0:T(8,128)} %bitcast.65), calls=%async_computation | async-start | bytes 262144 | tf_op jit(solution)/shard_map/all_to_all | solution.py:991
  26.1 17.0 %collective-permute-start.3 = (f32[4,40,1024]{2,1,0:T(8,128)S(1)}, f32[4,40,1024]{2,1,0:T(8,128)S(1)}, u32[]{:S(2)}, u32[]{:S(2)}) collective-permute-start(f32[4,40,1024]{2,1,0:T(8,128)S(1)} %pad_maximum_fusion.2.refs_0_), channel_id=1, source_target_pairs={{0,2},{2,0},{4,6},{6,4},{1,3},{3,1},{5,7},{7,5},{8,10},{10,8},{12,... | collective-permute-start | bytes 1966088 | tf_op jit(solution)/shard_map/ppermute | solution.py:873
  26.6 16.5 %collective-permute-start.4 = (f32[4,40,1024]{2,1,0:T(8,128)S(1)}, f32[4,40,1024]{2,1,0:T(8,128)S(1)}, u32[]{:S(2)}, u32[]{:S(2)}) collective-permute-start(f32[4,40,1024]{2,1,0:T(8,128)S(1)} %pad_maximum_fusion.2.refs_0_), channel_id=1, source_target_pairs={{0,4},{2,6},{4,0},{6,2},{1,5},{3,7},{5,1},{7,3},{8,12},{10,14},{12... | collective-permute-start | bytes 1966088 | tf_op jit(solution)/shard_map/ppermute | solution.py:873
  27.6 30.9 %collective-permute-start.5 = (f32[4,40,1024]{2,1,0:T(8,128)S(1)}, f32[4,40,1024]{2,1,0:T(8,128)S(1)}, u32[]{:S(2)}, u32[]{:S(2)}) collective-permute-start(f32[4,40,1024]{2,1,0:T(8,128)S(1)} %pad_maximum_fusion.2.refs_0_), channel_id=1, source_target_pairs={{0,16},{16,0},{1,17},{17,1},{2,18},{18,2},{3,19},{19,3},{4,20},{20... | collective-permute-start | bytes 1966088 | tf_op jit(solution)/shard_map/ppermute | solution.py:872
  61.6 56.7 %all-to-all-start.1 = ((f32[32,128,128]{2,1,0:T(8,128)}), f32[32,128,128]{2,1,0:T(8,128)}, u32[]{:S(2)}, u32[]{:S(2)}) async-start(f32[32,128,128]{2,1,0:T(8,128)} %bitcast.151), calls=%async_computation.1 | async-start | bytes 4194304 | tf_op jit(solution)/shard_map/all_to_all | solution.py:1009
  65.3 35.9 %collective-permute-start.9 = (f32[4,40,1024]{2,1,0:T(8,128)S(1)}, f32[4,40,1024]{2,1,0:T(8,128)S(1)}, u32[]{:S(2)}, u32[]{:S(2)}) collective-permute-start(f32[4,40,1024]{2,1,0:T(8,128)S(1)} %collective-permute-done.5.refs_3_.refs_5_), channel_id=1, source_target_pairs={{0,4},{2,6},{4,0},{6,2},{1,5},{3,7},{5,1},{7,3},{8,12},{10,14},{12... | collective-permute-start | bytes 1966088 | tf_op jit(solution)/shard_map/ppermute | solution.py:873
  66.8 36.4 %collective-permute-start.8 = (f32[4,40,1024]{2,1,0:T(8,128)S(1)}, f32[4,40,1024]{2,1,0:T(8,128)S(1)}, u32[]{:S(2)}, u32[]{:S(2)}) collective-permute-start(f32[4,40,1024]{2,1,0:T(8,128)S(1)} %collective-permute-done.5.refs_3_.refs_5_), channel_id=1, source_target_pairs={{0,2},{2,0},{4,6},{6,4},{1,3},{3,1},{5,7},{7,5},{8,10},{10,8},{12,... | collective-permute-start | bytes 1966088 | tf_op jit(solution)/shard_map/ppermute | solution.py:873
  68.3 43.4 %collective-permute-start.6 = (f32[2,40,1024]{2,1,0:T(8,128)S(1)}, f32[2,40,1024]{2,1,0:T(8,128)S(1)}, u32[]{:S(2)}, u32[]{:S(2)}) collective-permute-start(f32[2,40,1024]{2,1,0:T(8,128)S(1)} %slice.213), channel_id=1, source_target_pairs={{0,2},{2,0},{4,6},{6,4},{1,3},{3,1},{5,7},{7,5},{8,10},{10,8},{12,... | collective-permute-start | bytes 983048 | tf_op jit(solution)/shard_map/ppermute | solution.py:873
  68.9 42.8 %collective-permute-start.7 = (f32[2,40,1024]{2,1,0:T(8,128)S(1)}, f32[2,40,1024]{2,1,0:T(8,128)S(1)}, u32[]{:S(2)}, u32[]{:S(2)}) collective-permute-start(f32[2,40,1024]{2,1,0:T(8,128)S(1)} %slice.214), channel_id=1, source_target_pairs={{0,4},{2,6},{4,0},{6,2},{1,5},{3,7},{5,1},{7,3},{8,12},{10,14},{12... | collective-permute-start | bytes 983048 | tf_op jit(solution)/shard_map/ppermute | solution.py:873
  101.2 17.0 %collective-permute-start.10 = (f32[2,40,1024]{2,1,0:T(8,128)S(1)}, f32[2,40,1024]{2,1,0:T(8,128)S(1)}, u32[]{:S(2)}, u32[]{:S(2)}) collective-permute-start(f32[2,40,1024]{2,1,0:T(8,128)S(1)} %slice.215), channel_id=1, source_target_pairs={{0,2},{2,0},{4,6},{6,4},{1,3},{3,1},{5,7},{7,5},{8,10},{10,8},{12,... | collective-permute-start | bytes 983048 | tf_op jit(solution)/shard_map/ppermute | solution.py:873
  103.2 15.1 %collective-permute-start.11 = (f32[2,40,1024]{2,1,0:T(8,128)S(1)}, f32[2,40,1024]{2,1,0:T(8,128)S(1)}, u32[]{:S(2)}, u32[]{:S(2)}) collective-permute-start(f32[2,40,1024]{2,1,0:T(8,128)S(1)} %slice.216), channel_id=1, source_target_pairs={{0,4},{2,6},{4,0},{6,2},{1,5},{3,7},{5,1},{7,3},{8,12},{10,14},{12... | collective-permute-start | bytes 983048 | tf_op jit(solution)/shard_map/ppermute | solution.py:873
  122.2 20.4 %collective-permute-start.14 = (f32[1024,128]{1,0:T(8,128)}, f32[1024,128]{1,0:T(8,128)S(1)}, u32[]{:S(2)}, u32[]{:S(2)}) collective-permute-start(f32[1024,128]{1,0:T(8,128)} %shard_map.436.refs_0_), channel_id=1, source_target_pairs={{0,8},{8,0},{1,9},{9,1},{2,10},{10,2},{3,11},{11,3},{4,12},{12,4},... | collective-permute-start | bytes 1572872 | tf_op jit(solution)/shard_map/ppermute | solution.py:838
  189.7 20.4 %collective-permute-start.24 = (f32[768,128]{1,0:T(8,128)S(1)}, f32[768,128]{1,0:T(8,128)S(1)}, u32[]{:S(2)}, u32[]{:S(2)}) collective-permute-start(f32[768,128]{1,0:T(8,128)S(1)} %pad_maximum_fusion.8), channel_id=1, source_target_pairs={{0,8},{8,0},{1,9},{9,1},{2,10},{10,2},{3,11},{11,3},{4,12},{12,4},... | collective-permute-start | bytes 1179656 | tf_op jit(solution)/shard_map/ppermute | solution.py:838
  205.5 32.1 %all-to-all-start.2 = ((f32[32,32,128]{2,1,0:T(8,128)}), f32[32,32,128]{2,1,0:T(8,128)S(1)}, u32[]{:S(2)}, u32[]{:S(2)}) async-start(f32[32,32,128]{2,1,0:T(8,128)} %shard_map.445.refs_18_.refs_1_), calls=%async_computation.2 | async-start | bytes 1048576 | tf_op jit(solution)/shard_map/all_to_all | solution.py:1134
  225.2 38.2 %collective-permute-start.26 = (f32[2,2,2,40,1024]{4,3,2,1,0:T(8,128)}, f32[2,2,2,40,1024]{4,3,2,1,0:T(8,128)}, u32[]{:S(2)}, u32[]{:S(2)}) collective-permute-start(f32[2,2,2,40,1024]{4,3,2,1,0:T(8,128)} %get-tuple-element.156), channel_id=1, source_target_pairs={{0,4},{2,6},{4,0},{6,2},{1,5},{3,7},{5,1},{7,3},{8,12},{10,14},{12... | collective-permute-start | bytes 3932168 | tf_op jit(solution)/shard_map/ppermute | solution.py:873
  227.2 40.8 %collective-permute-start.25 = (f32[2,2,2,40,1024]{4,3,2,1,0:T(8,128)}, f32[2,2,2,40,1024]{4,3,2,1,0:T(8,128)}, u32[]{:S(2)}, u32[]{:S(2)}) collective-permute-start(f32[2,2,2,40,1024]{4,3,2,1,0:T(8,128)} %get-tuple-element.154), channel_id=1, source_target_pairs={{0,2},{2,0},{4,6},{6,4},{1,3},{3,1},{5,7},{7,5},{8,10},{10,8},{12,... | collective-permute-start | bytes 3932168 | tf_op jit(solution)/shard_map/ppermute | solution.py:873
  237.6 34.2 %all-to-all-start.5 = ((f32[32,48,128]{2,1,0:T(8,128)}), f32[32,48,128]{2,1,0:T(8,128)S(1)}, u32[]{:S(2)}, u32[]{:S(2)}) async-start(f32[32,48,128]{2,1,0:T(8,128)} %pad_maximum_fusion), calls=%async_computation.5 | async-start | bytes 1572864 | tf_op jit(solution)/shard_map/all_to_all | solution.py:1134
  266.1 29.7 %collective-permute-start.28 = (f32[2,2,40,1024]{3,2,1,0:T(8,128)S(1)}, f32[2,2,40,1024]{3,2,1,0:T(8,128)S(1)}, u32[]{:S(2)}, u32[]{:S(2)}) collective-permute-start(f32[2,2,40,1024]{3,2,1,0:T(8,128)S(1)} %get-tuple-element.258.refs_9_), channel_id=1, source_target_pairs={{0,2},{2,0},{4,6},{6,4},{1,3},{3,1},{5,7},{7,5},{8,10},{10,8},{12,... | collective-permute-start | bytes 1966088 | tf_op jit(solution)/shard_map/ppermute | solution.py:873
  270.3 26.7 %collective-permute-start.27 = (f32[2,2,40,1024]{3,2,1,0:T(8,128)S(1)}, f32[2,2,40,1024]{3,2,1,0:T(8,128)}, u32[]{:S(2)}, u32[]{:S(2)}) collective-permute-start(f32[2,2,40,1024]{3,2,1,0:T(8,128)S(1)} %get-tuple-element.260.refs_8_), channel_id=1, source_target_pairs={{0,4},{2,6},{4,0},{6,2},{1,5},{3,7},{5,1},{7,3},{8,12},{10,14},{12... | collective-permute-start | bytes 1966088 | tf_op jit(solution)/shard_map/ppermute | solution.py:873
  271.8 31.2 %all-to-all-start.4 = ((f32[32,32,128]{2,1,0:T(8,128)}), f32[32,32,128]{2,1,0:T(8,128)S(1)}, u32[]{:S(2)}, u32[]{:S(2)}) async-start(f32[32,32,128]{2,1,0:T(8,128)} %get-tuple-element.144), calls=%async_computation.4 | async-start | bytes 1048576 | tf_op jit(solution)/shard_map/all_to_all | solution.py:1157
  298.4 38.2 %collective-permute-start.29 = (f32[4,40,1024]{2,1,0:T(8,128)S(1)}, f32[4,40,1024]{2,1,0:T(8,128)S(1)}, u32[]{:S(2)}, u32[]{:S(2)}) collective-permute-start(f32[4,40,1024]{2,1,0:T(8,128)S(1)} %pad_maximum_fusion.4.refs_7_), channel_id=1, source_target_pairs={{0,16},{16,0},{1,17},{17,1},{2,18},{18,2},{3,19},{19,3},{4,20},{20... | collective-permute-start | bytes 1966088 | tf_op jit(solution)/shard_map/ppermute | solution.py:872
  303.0 39.6 %all-to-all-start.3 = ((f32[32,32,128]{2,1,0:T(8,128)}), f32[32,32,128]{2,1,0:T(8,128)S(1)}, u32[]{:S(2)}, u32[]{:S(2)}) async-start(f32[32,32,128]{2,1,0:T(8,128)} %get-tuple-element.143), calls=%async_computation.3 | async-start | bytes 1048576 | tf_op jit(solution)/shard_map/all_to_all | solution.py:1157
  339.6 23.9 %collective-permute-start.31 = (f32[2,40,1024]{2,1,0:T(8,128)S(1)}, f32[2,40,1024]{2,1,0:T(8,128)S(1)}, u32[]{:S(2)}, u32[]{:S(2)}) collective-permute-start(f32[2,40,1024]{2,1,0:T(8,128)S(1)} %pad_maximum_fusion.10), channel_id=1, source_target_pairs={{0,8},{8,0},{1,9},{9,1},{2,10},{10,2},{3,11},{11,3},{4,12},{12,4},... | collective-permute-start | bytes 983048 | tf_op jit(solution)/shard_map/ppermute | solution.py:838
  (81 other events, 451.3 us)

commit v4 on v3

--- a/solution.py
+++ b/solution.py
@@ -57,14 +57,14 @@
     return (weight_next, moment_next, square_next)
 
 
-def fence(x, after):
+def fence(x, after, room=MIB):
     return pl.pallas_call(
         lambda *refs: None,
         out_shape=jax.ShapeDtypeStruct(x.shape, x.dtype),
         in_specs=[ANYWHERE] * (1 + len(after)),
         out_specs=ANYWHERE,
         input_output_aliases={0: 0},
-        compiler_params=pltpu.CompilerParams(vmem_limit_bytes=MIB),
+        compiler_params=pltpu.CompilerParams(vmem_limit_bytes=room),
         cost_estimate=pl.CostEstimate(flops=0, bytes_accessed=0, transcendentals=0),
     )(x, *after)
 
@@ -73,7 +73,7 @@
     return lax.broadcasted_iota(jnp.int32, (1, LANES), 1) < DIM
 
 
-def gather_kernel(rows, cols, devices, each, idx_ref, table_ref, out_ref, buf, sem):
+def gather_kernel(rows, cols, devices, each, idx_ref, table_ref, far_ref, buf, out_ref, sem, out_sem):
     count = devices * each
 
     def fetch(u):
@@ -99,6 +99,9 @@
             return carry
 
         lax.fori_loop(0, devices, step, 0)
+        pltpu.make_async_copy(out_ref.at[:, u], far_ref.at[:, u], out_sem.at[u]).start()
+    for u in range(cols):
+        pltpu.make_async_copy(out_ref.at[:, u], far_ref.at[:, u], out_sem.at[u]).wait()
 
 
 def gather_rows(idx, table, devices, each):
@@ -108,9 +111,11 @@
         functools.partial(gather_kernel, rows, cols, devices, each),
         out_shape=jax.ShapeDtypeStruct((devices, cols, each, LANES), jnp.float32),
         in_specs=[SCALARS, ANYWHERE],
-        out_specs=WHOLE,
+        out_specs=FAR,
         scratch_shapes=[
             pltpu.VMEM((cols, rows + 8, LANES), jnp.float32),
+            pltpu.VMEM((devices, cols, each, LANES), jnp.float32),
+            pltpu.SemaphoreType.DMA((cols,)),
             pltpu.SemaphoreType.DMA((cols,)),
         ],
         compiler_params=pltpu.CompilerParams(vmem_limit_bytes=ROOM),
@@ -352,88 +357,97 @@
     return pl.multiple_of(row, tower_depth) if counted else row
 
 
-def split_kernel(depth, tower_depth, order, pieces, peer_ref, *refs):
-    sources, far, refs = refs[:pieces], refs[pieces : pieces + 12], refs[pieces + 12 :]
-    piece_refs, outs, (tower, gate, sem, out_sem) = refs[:pieces], refs[pieces:-4], refs[-4:]
-    loads = [
-        pltpu.make_async_copy(sources[k], piece_refs[k], sem.at[k]) for k in range(pieces)
-    ]
+def split_kernel(depth, tower_depth, order, sizes, befores, turn, peer_ref, *refs):
+    pieces = len(sizes)
+    sources, refs = refs[:pieces], refs[pieces + befores :]
+    far, (whole, *outs), (tower, gate, sem, out_sem) = refs[:6], refs[6:13], refs[13:]
+    loads = []
+    ends = []
+    for k in range(pieces):
+        start = sum(sizes[:k])
+        loads.append(
+            pltpu.make_async_copy(sources[k], whole.at[pl.ds(start, sizes[k])], sem.at[k])
+        )
+        ends.append(start + sizes[k])
     for load in loads:
         load.start()
-    stores = [pltpu.make_async_copy(outs[k], far[k], out_sem.at[k]) for k in range(12)]
-
-    def put(k, at, value):
-        high, low = split(value)
-        outs[k][at] = high
-        outs[k + 1][at] = low
-
-    block = 0
     gate_at = -(-tower_depth // 8) * TOWER_LANES
     gate[...] = jnp.zeros(gate.shape, jnp.float32)
-    for load, ref in zip(loads, piece_refs):
-        load.wait()
-        step = min(LANES // depth, ref.shape[0])
-        for b in range(0, ref.shape[0], step):
-            rows = slice((block + b) * depth, (block + b + step) * depth)
-            put(0, (rows, slice(None)), ref[b : b + step, :depth, :].reshape(-1, ref.shape[2]))
-        for b in range(ref.shape[0]):
-            number, member = (block + b) // 4, (block + b) % 4
-            row = tower_row(order, peer_ref, number, member, tower_depth)
+    devices, _, lots = whole.shape
+    share = LANES // depth
+    waited = 0
+    stores = []
+
+    def store(k, at, n):
+        copy = pltpu.make_async_copy(outs[k].at[at], far[k].at[at], out_sem.at[k, n])
+        copy.start()
+        stores.append(copy)
+
+    for n in range(devices // share):
+        while waited < pieces and (waited == 0 or ends[waited - 1] < (n + 1) * share):
+            loads[waited].wait()
+            waited += 1
+        rows = slice(n * LANES, (n + 1) * LANES)
+        block = whole[n * share : (n + 1) * share, :depth, :].reshape(LANES, lots)
+        at = (slice(None), rows) if turn else (rows, slice(None))
+        outs[0][at], outs[1][at] = split(block.T if turn else block)
+        for k in range(2):
+            store(k, at, n)
+        for d in range(n * share, (n + 1) * share):
+            row = tower_row(order, peer_ref, d // 4, d % 4, tower_depth)
             for k in range(0, tower_depth, 8):
                 high = min(8, tower_depth)
                 at = k // 8 * TOWER_LANES
-                tower[pl.ds(row + k, high), :] = ref[
-                    b, depth : depth + high, at : at + TOWER_LANES
+                tower[pl.ds(row + k, high), :] = whole[
+                    d, depth : depth + high, at : at + TOWER_LANES
                 ]
             for k in range(0, depth, LANES // GATE_LANES * 8):
                 at = gate_at + k // 8 * GATE_LANES
-                both = ref[b, depth : depth + 8, at : at + LANES]
-                row = (block + b) * depth + k
+                both = whole[d, depth : depth + 8, at : at + LANES]
+                row = d * depth + k
                 gate[row : row + 8, :GATE_LANES] = both[:, :GATE_LANES]
                 if k + 8 < depth:
                     gate[row + 8 : row + 16, :GATE_LANES] = both[:, GATE_LANES:]
-        block += ref.shape[0]
-    for k in range(2):
-        stores[k].start()
-    for b in range(outs[0].shape[0] // LANES):
-        rows = slice(b * LANES, (b + 1) * LANES)
-        for k in range(2):
-            turned = outs[k][rows, :].astype(jnp.float32).T
-            outs[2 + k][:, rows] = turned.astype(jnp.bfloat16)
-    width = outs[4].shape[1]
-    put(4, Ellipsis, tower[:, :width])
-    put(6, Ellipsis, gate[:, :GATE_LANES])
-    put(8, Ellipsis, tower[...].T[:width])
-    put(10, Ellipsis, gate[...].T[:GATE_LANES])
-    for k in range(2, 12):
-        stores[k].start()
-    for store in stores:
-        store.wait()
-
-
-def split_weights(pieces, peer, order, depth, tower_depth, tower_width):
+    if turn:
+        width = outs[2].shape[0]
+        outs[2][...], outs[3][...] = split(tower[...].T[:width])
+        outs[4][...], outs[5][...] = split(gate[...].T[:GATE_LANES])
+    else:
+        width = outs[2].shape[1]
+        outs[2][...], outs[3][...] = split(tower[:, :width])
+        outs[4][...], outs[5][...] = split(gate[:, :GATE_LANES])
+    for k in range(2, 6):
+        store(k, Ellipsis, 0)
+    for copy in stores:
+        copy.wait()
+
+
+def split_weights(pieces, peer, order, depth, tower_depth, tower_width, turn, before):
     lots = pieces[0].shape[2]
-    devices = sum(x.shape[0] for x in pieces)
+    sizes = tuple(x.shape[0] for x in pieces)
+    devices = sum(sizes)
     width = devices * depth
     height = devices * tower_depth
-    shapes = [(width, lots), (lots, width), (height, tower_width), (width, GATE_LANES)]
-    shapes += [shapes[2][::-1], shapes[3][::-1]]
-    shapes = [shape for shape in shapes for _ in range(2)]
-    return pl.pallas_call(
-        functools.partial(split_kernel, depth, tower_depth, order, len(pieces)),
+    shapes = [(width, lots), (height, tower_width), (width, GATE_LANES)]
+    shapes = [shape[::-1] if turn else shape for shape in shapes for _ in range(2)]
+    done = pl.pallas_call(
+        functools.partial(
+            split_kernel, depth, tower_depth, order, sizes, len(before), turn
+        ),
         out_shape=[jax.ShapeDtypeStruct(shape, jnp.bfloat16) for shape in shapes],
-        in_specs=[SCALARS] + [ANYWHERE] * len(pieces),
-        out_specs=[FAR] * 12,
-        scratch_shapes=[pltpu.VMEM(x.shape, x.dtype) for x in pieces]
+        in_specs=[SCALARS] + [ANYWHERE] * (len(pieces) + len(before)),
+        out_specs=[FAR] * 6,
+        scratch_shapes=[pltpu.VMEM((devices,) + pieces[0].shape[1:], jnp.float32)]
         + [pltpu.VMEM(shape, jnp.bfloat16) for shape in shapes]
         + [
             pltpu.VMEM((height, TOWER_LANES), jnp.float32),
             pltpu.VMEM((width, LANES), jnp.float32),
             pltpu.SemaphoreType.DMA((len(pieces),)),
-            pltpu.SemaphoreType.DMA((12,)),
+            pltpu.SemaphoreType.DMA((6, width // LANES)),
         ],
         compiler_params=pltpu.CompilerParams(vmem_limit_bytes=ROOM),
-    )(peer, *pieces)
+    )(peer, *pieces, *before)
+    return [done[2 * k : 2 * k + 2] for k in range(3)]
 
 
 def forward_kernel(dims, member_ref, *refs):
@@ -563,7 +577,7 @@
 
 def score_kernel(
     tasks, total_ref, first_ref, second_ref, bias_ref, out_ref, last_ref, keep_ref, target_ref,
-    packed_ref, grad_out_ref, grad_bias_ref, small_ref,
+    before, packed_ref, grad_out_ref, grad_bias_ref, small_ref,
 ):
     mixed = first_ref[...] + second_ref[...]
     width, samples = mixed.shape
@@ -593,16 +607,16 @@
     small_ref[1] = jnp.sum(keep * (softplus - targets * score), axis=1, keepdims=True)
 
 
-def score_step(tasks, weight_total, first, second, bias, out, last, keep, targets):
+def score_step(tasks, weight_total, first, second, bias, out, last, keep, targets, before):
     width, samples = first.shape
     shapes = [(-(-(width + tasks) // 8) * 8, samples), (width, 1), (width, 1), (2, tasks, 1)]
     return pl.pallas_call(
         functools.partial(score_kernel, tasks),
         out_shape=[jax.ShapeDtypeStruct(shape, jnp.float32) for shape in shapes],
-        in_specs=[SCALARS] + [WHOLE] * 7,
+        in_specs=[SCALARS] + [WHOLE] * 7 + [ANYWHERE],
         out_specs=[WHOLE] * 4,
         compiler_params=pltpu.CompilerParams(vmem_limit_bytes=8 * MIB),
-    )(weight_total, first, second, bias, out, last, keep, targets)
+    )(weight_total, first, second, bias, out, last, keep, targets, before)
 
 
 def backward_kernel(dims, place, member_ref, peer_ref, *refs):
@@ -718,7 +732,9 @@
     mine, hidden_units = dims
     logits, sources, refs = refs[:2], refs[2:18], refs[18 + befores :]
     weight_refs, bias_ref, refs = refs[:outs], refs[outs], refs[outs + 1 :]
-    x, d_pre, hid, spreads, (tower, in_sem) = refs[:2], refs[2:4], refs[4:6], refs[6:8], refs[8:]
+    far_refs = weight_refs
+    x, d_pre, hid, spreads = refs[:2], refs[2:4], refs[4:6], refs[6:8]
+    weight_refs, (tower, in_sem, out_sem) = refs[8 : 8 + outs], refs[8 + outs :]
     half = 2 * LANES
     places = [
         pair[k].at[(Ellipsis, pl.ds(h * half, half))] if pair is not spreads else pair[k].at[h]
@@ -745,6 +761,14 @@
         return [(weight_refs[low], (middle, high), 0, 2), (weight_refs[2 + middle], (low, high), 0, 2)]
 
     wide = 256
+    body, tail = slice(0, depth), slice(depth, depth + 8)
+
+    def stores(rows, lanes, n):
+        at = (Ellipsis, rows, lanes)
+        return [
+            pltpu.make_async_copy(a.at[at], b.at[at], out_sem.at[n, k])
+            for k, (a, b) in enumerate(zip(weight_refs, far_refs))
+        ]
 
     def columns(n, carry):
         at = pl.ds(pl.multiple_of(n * wide, wide), wide)
@@ -763,6 +787,8 @@
                     row : row + many * depth
                 ].reshape(many, depth, wide)
                 row += many * depth
+        for store in stores(body, at, n):
+            store.start()
         return carry
 
     lax.fori_loop(0, lots // wide, columns, 0)
@@ -800,6 +826,13 @@
                     jnp.concatenate(eights, axis=1) if len(eights) > 1 else eights[0]
                 )
                 d += 1
+    for store in stores(tail, slice(None), lots // wide):
+        store.start()
+    for n in range(lots // wide):
+        for store in stores(body, slice(n * wide, (n + 1) * wide), n):
+            store.wait()
+    for store in stores(tail, slice(None), lots // wide):
+        store.wait()
 
 
 def gradients(dims, devices, depth, tower_depth, order, peer, logits, operands, before):
@@ -818,11 +851,13 @@
         out_shape=[jax.ShapeDtypeStruct(shape, jnp.float32)] * outs
         + [jax.ShapeDtypeStruct((8, lots), jnp.float32)],
         in_specs=[SCALARS, WHOLE, WHOLE] + [FAR] * 16 + [ANYWHERE] * len(before),
-        out_specs=[WHOLE] * (outs + 1),
+        out_specs=[FAR] * outs + [WHOLE],
         scratch_shapes=[pltpu.VMEM(x, jnp.bfloat16) for x in held for _ in range(2)]
+        + [pltpu.VMEM(shape, jnp.float32)] * outs
         + [
             pltpu.VMEM((hidden_units, TOWER_LANES), jnp.float32),
             pltpu.SemaphoreType.DMA((16,)),
+            pltpu.SemaphoreType.DMA((lots // 256 + 1, outs)),
         ],
         compiler_params=pltpu.CompilerParams(vmem_limit_bytes=ROOM),
         cost_estimate=pl.CostEstimate(
@@ -1004,17 +1039,17 @@
         parts = [lax.all_gather(shared, PEERS, axis=0, tiled=True)]
     bias_mine = lax.dynamic_slice_in_dim(expert_bias, member * mine, mine, 0).reshape(lots, 1)
 
-    picked = fence(gather_rows(idx, tables, devices, each), early)
+    picked = fence(gather_rows(idx, tables, devices, each), early, ROOM)
     cols = width_here // LANES
     arrived = lax.all_to_all(
         picked.reshape(devices, cols * each, LANES), ALL, 0, 0, tiled=True
     ).reshape(pieces, halves, cols, each, LANES)
-    split_parts = split_weights(
-        parts, peer_at, order, depth, tower_depth, upper_width
-    )
-    weight_pair, weight_turned, tower_pair, gate_pair, tower_turned, gate_turned = [
-        split_parts[2 * k : 2 * k + 2] for k in range(6)
-    ]
+    def pairs(turn, before):
+        return split_weights(
+            parts, peer_at, order, depth, tower_depth, upper_width, turn, before
+        )
+
+    weight_turned, tower_turned, gate_turned = pairs(True, [])
     mine_x = pool(shifts, peer_at, place, arrived, parts)
     near_x = swap_near(mine_x)
     halves_x = [(mine_x, swap_core(mine_x))]
@@ -1031,6 +1066,7 @@
     halves_x.append((near_x, swap_core(near_x)))
     runs.append(half_forward(halves_x[1]))
     part_own, part_near = runs[0][7], runs[1][7]
+    weight_pair, tower_pair, gate_pair = pairs(False, [part_near])
     first = part_own[0] + swap_core(part_own[1])
     second = swap_near(part_near[0] + swap_core(part_near[1]))
     packed, grad_output, grad_head, few = score_step(
@@ -1043,6 +1079,7 @@
         head_bias[:, -1:],
         keep.T,
         targets.T,
+        gate_pair[0],
     )
 
     core_packed = swap_core(packed)
@@ -1078,7 +1115,7 @@
         [leaving[c * half_width + LANES : (c + 1) * half_width] for c in range(halves)], axis=0
     )
     ahead = swap_near(ahead)
-    others = swap_near(others)
+    others = swap_near(fence(others, [ahead], ROOM))
     terms = [back[0][5], swap_core(back[0][6])]
 
     def starts(first, stride):
@@ -1091,7 +1128,7 @@
     returned += list(
         spread(
             shifts,
-            terms + [fence(others, returned)],
+            terms + [fence(others, returned, ROOM)],
             starts(LANES, half_width - LANES),
             pieces,
             halves,
@@ -1113,7 +1150,7 @@
         + [x[k] for x in back for k in (0, 1)]
         + [x[k] for x in runs for k in (4, 5)]
         + [x[k] for x in back for k in (2, 3)],
-        [returned[0], others],
+        [returned[0]],
     )
 
     grad_head = jnp.concatenate([grad_head.reshape(tasks, tower_units), few[0]], axis=1)

time: 369 us -> 361 us (0.978)
  waiting for transfers between devices: 103 us -> 93.6 us
    ppermute x8, waiting for transfers between devices: 17.7 us -> 10.6 us  [swap_near(): return lax.ppermute(x, 'near', [(i, i ^ 1) for i in range(count)])]
    pallas_call x1 -> x2, Pallas kernels: 7.82 us -> 10.1 us  [split_weights(): pl.pallas_call(functools.partial(split_kernel, depth, tower_depth, order,...]
  transfers between devices with their start and end apart: 38 -> 38, of which waited for: 15 -> 16; matrix products, arithmetic and copies ran while one was open for 7% -> 8% of each run, Pallas kernels for 38% -> 39%
where the time goes in v4:
time: 361 us; the launch traced here: 360 us
  Pallas kernels  161 us (45%)
  waiting for transfers between devices  93.6 us (26%)
  starting transfers between devices  55.6 us (15%)
  local copies, waits for them, and re-layouts  23.1 us (6%)
  other arithmetic  23.1 us (6%)
    pallas_call x4, Pallas kernels, update_part(): pl.pallas_call(functools.partial(update_kernel, rows, part, devices, each...  80.7 us
    ppermute x12, waiting for transfers between devices, swap_peer(): lax.ppermute(x, 'rest', [(i, i ^ bit) for i in range(lax.axis_size('rest'...  44.7 us
    ppermute x2, waiting for transfers between devices, swap_peer(): return lax.ppermute(x, 'hi', [(0, 1), (1, 0)])  25.1 us
    pallas_call x2, Pallas kernels, forward(): pl.pallas_call(functools.partial(forward_kernel, dims), out_shape=[jax.Sh...  16.8 us
    pallas_call x2, Pallas kernels, backward(): pl.pallas_call(functools.partial(backward_kernel, dims, place), out_shape...  16.5 us
    pallas_call x1, Pallas kernels, gather_rows(): pl.pallas_call(functools.partial(gather_kernel, rows, cols, devices, each...  14.8 us
    ppermute x12, starting transfers between devices, swap_peer(): lax.ppermute(x, 'rest', [(i, i ^ bit) for i in range(lax.axis_size('rest'...  14.4 us
    pallas_call x1, Pallas kernels, gradients(): pl.pallas_call(functools.partial(gradient_kernel, dims, depth, tower_dept...  13.8 us
  transfers between devices with their start and end apart: 38, of which 16 were waited for; matrix products, arithmetic and copies ran while one was open for 8% of the time, Pallas kernels for 39%

profile of v4, /device:TPU:0, one launch (start us, length us, event | category | flops | bytes accessed | tf_op | source)
XLA Modules:
  0.0 359.9 jit_solution(11806366468851864687)
XLA Ops:
  10.2 6.0 %all-to-all-start = ((f32[32,8,128]{2,1,0:T(8,128)}), f32[32,8,128]{2,1,0:T(8,128)S(1)}, u32[]{:S(2)}, u32[]{:S(2)}) async-start(f32[32,8,128]{2,1,0:T(8,128)} %bitcast.65), calls=%async_computation | async-start | bytes 262144 | tf_op jit(solution)/shard_map/all_to_all | solution.py:1026
  16.3 8.1 %all-to-all-done = f32[32,8,128]{2,1,0:T(8,128)S(1)} async-done(((f32[32,8,128]{2,1,0:T(8,128)}), f32[32,8,128]{2,1,0:T(8,128)S(1)}, u32[]{:S(2)}, u32[]{:S(2)}) %all-to-all-start) | async-done | bytes 131104 | tf_op jit(solution)/shard_map/all_to_all | solution.py:1026
  28.1 14.8 %shard_map.434.refs_0_ = f32[32,4,32,128]{3,2,1,0:T(8,128)} custom-call(s32[8192]{0:T(1024)} %copy-done.35, f32[16384,512]{1,0:T(8,128)} %refs_0_.7), custom_call_target="tpu_custom_call" | custom-call | bytes 67108864 | tf_op jit(solution)/shard_map/pallas_call | solution.py:110
  43.1 15.4 %collective-permute-done.5.refs_3_.refs_5_ = f32[4,40,1024]{2,1,0:T(8,128)S(1)} collective-permute-done((f32[4,40,1024]{2,1,0:T(8,128)S(1)}, f32[4,40,1024]{2,1,0:T(8,128)S(1)}, u32[]{:S(2)}, u32[]{:S(2)}) %collective-permute-start.5) | collective-permute-done | bytes 655392 | tf_op jit(solution)/shard_map/ppermute | solution.py:907
  59.4 3.8 %all-to-all-start.1 = ((f32[32,128,128]{2,1,0:T(8,128)}), f32[32,128,128]{2,1,0:T(8,128)}, u32[]{:S(2)}, u32[]{:S(2)}) async-start(f32[32,128,128]{2,1,0:T(8,128)} %bitcast.153), calls=%async_computation.1 | async-start | bytes 4194304 | tf_op jit(solution)/shard_map/all_to_all | solution.py:1044
  67.5 31.6 %collective-permute-done.9.refs_7_ = f32[4,40,1024]{2,1,0:T(8,128)S(1)} collective-permute-done((f32[4,40,1024]{2,1,0:T(8,128)S(1)}, f32[4,40,1024]{2,1,0:T(8,128)S(1)}, u32[]{:S(2)}, u32[]{:S(2)}) %collective-permute-start.9) | collective-permute-done | bytes 655392 | tf_op jit(solution)/shard_map/ppermute | solution.py:908
  103.3 6.4 %collective-permute-done.6.refs_3_ = f32[2,40,1024]{2,1,0:T(8,128)S(1)} collective-permute-done((f32[2,40,1024]{2,1,0:T(8,128)S(1)}, f32[2,40,1024]{2,1,0:T(8,128)S(1)}, u32[]{:S(2)}, u32[]{:S(2)}) %collective-permute-start.6) | collective-permute-done | bytes 327712 | tf_op jit(solution)/shard_map/ppermute | solution.py:908
  109.6 6.5 %collective-permute-done.10.refs_8_ = f32[2,40,1024]{2,1,0:T(8,128)S(1)} collective-permute-done((f32[2,40,1024]{2,1,0:T(8,128)S(1)}, f32[2,40,1024]{2,1,0:T(8,128)S(1)}, u32[]{:S(2)}, u32[]{:S(2)}) %collective-permute-start.10) | collective-permute-done | bytes 327712 | tf_op jit(solution)/shard_map/ppermute | solution.py:908
  123.5 4.9 %shard_map.437 = (bf16[1024,1024]{1,0:T(8,128)(2,1)}, bf16[1024,1024]{1,0:T(8,128)(2,1)}, bf16[320,512]{1,0:T(8,128)(2,1)}, bf16[320,512]{1,0:T(8,128)(2,1)}, bf...) custom-call(s32[1]{0:T(128)} %bitcast.7.peer_ref, f32[4,40,1024]{2,1,0:T(8,128)} %copy-done.16, ...), custom_call_target="tpu_custom_call" | custom-call | tf_op jit(solution)/shard_map/pallas_call | solution.py:433
  129.2 8.4 %shard_map.438 = (f32[1024,256]{1,0:T(8,128)}, f32[2,320,256]{2,1,0:T(8,128)}, bf16[1024,256]{1,0:T(8,128)(2,1)}, bf16[1024,256]{1,0:T(8,128)(2,1)}, bf16[1024,2...) custom-call(s32[1]{0:T(128)} %bitcast.6.member_ref, ...), custom_call_target="tpu_custom_call" | custom-call | flops 2147483648 | bytes 12582912 | tf_op jit(solution)/shard_map/pallas_call | solution.py:558
  141.3 8.4 %shard_map.440 = (f32[1024,256]{1,0:T(8,128)}, f32[2,320,256]{2,1,0:T(8,128)}, bf16[1024,256]{1,0:T(8,128)(2,1)}, bf16[1024,256]{1,0:T(8,128)(2,1)}, bf16[1024,2...) custom-call(s32[1]{0:T(128)} %bitcast.6.member_ref, ...), custom_call_target="tpu_custom_call" | custom-call | flops 2147483648 | bytes 12582912 | tf_op jit(solution)/shard_map/pallas_call | solution.py:558
  153.7 5.2 %shard_map.441 = (bf16[1024,1024]{1,0:T(8,128)(2,1)}, bf16[1024,1024]{1,0:T(8,128)(2,1)}, bf16[512,320]{1,0:T(8,128)(2,1)}, bf16[512,320]{1,0:T(8,128)(2,1)}, bf...) custom-call(s32[1]{0:T(128)} %bitcast.7.peer_ref, f32[4,40,1024]{2,1,0:T(8,128)} %copy-done.16, ...), custom_call_target="tpu_custom_call" | custom-call | tf_op jit(solution)/shard_map/pallas_call | solution.py:433
  163.8 8.3 %shard_map.443 = (bf16[1024,256]{1,0:T(8,128)(2,1)}, bf16[1024,256]{1,0:T(8,128)(2,1)}, bf16[2,320,256]{2,1,0:T(8,128)(2,1)}, bf16[2,320,256]{2,1,0:T(8,128)(2,1...) custom-call(s32[1]{0:T(128)} %bitcast.6.member_ref, s32[1]{0:T(128)} %bitcast.7.peer_ref, ...), custom_call_target="tpu_custom_call" | custom-call | flops 2147483648 | bytes 12582912 | tf_op jit(solution)/shard_map/pallas_call | solution.py:715
  174.4 8.2 %shard_map.445 = (bf16[1024,256]{1,0:T(8,128)(2,1)}, bf16[1024,256]{1,0:T(8,128)(2,1)}, bf16[2,320,256]{2,1,0:T(8,128)(2,1)}, bf16[2,320,256]{2,1,0:T(8,128)(2,1...) custom-call(s32[1]{0:T(128)} %bitcast.6.member_ref, s32[1]{0:T(128)} %bitcast.7.peer_ref, ...), custom_call_target="tpu_custom_call" | custom-call | flops 2147483648 | bytes 12582912 | tf_op jit(solution)/shard_map/pallas_call | solution.py:715
  187.1 4.4 %collective-permute-done.23.refs_2_.refs_1_ = f32[256,128]{1,0:T(8,128)S(1)} collective-permute-done((f32[256,128]{1,0:T(8,128)S(1)}, f32[256,128]{1,0:T(8,128)S(1)}, u32[]{:S(2)}, u32[]{:S(2)}) %collective-permute-start.23) | collective-permute-done | bytes 131104 | tf_op jit(solution)/shard_map/ppermute | solution.py:873
  193.3 4.3 %all-to-all-start.2 = ((f32[32,32,128]{2,1,0:T(8,128)}), f32[32,32,128]{2,1,0:T(8,128)S(1)}, u32[]{:S(2)}, u32[]{:S(2)}) async-start(f32[32,32,128]{2,1,0:T(8,128)} %shard_map.446.refs_18_.refs_1_), calls=%async_computation.2 | async-start | bytes 1048576 | tf_op jit(solution)/shard_map/all_to_all | solution.py:1171
  197.7 13.8 %shard_map.447 = (f32[2,2,2,40,1024]{4,3,2,1,0:T(8,128)}, f32[2,2,2,40,1024]{4,3,2,1,0:T(8,128)}, f32[2,2,2,40,1024]{4,3,2,1,0:T(8,128)}, f32[2,2,2,40,1024]{4,3,2,1,0:T(8,128)}, f32[8,1024]{1,0:T(8,128)}) custom-call(s32[1]{0:T(128)} %bitcast.7.peer_ref, f32[64,256]{1,0:T(8,128)} %get-tuple-element.116.refs_1_.refs_0_, ...), custom_call_target="tpu_custom_call" | custom-call | flops 2147483648 | bytes 16777216 | tf_op jit(solution)/shard_map/pallas_call | solution.py:847
  219.7 5.5 %collective-permute-done.24.refs_0_ = f32[768,128]{1,0:T(8,128)S(1)} collective-permute-done((f32[768,128]{1,0:T(8,128)}, f32[768,128]{1,0:T(8,128)S(1)}, u32[]{:S(2)}, u32[]{:S(2)}) %collective-permute-start.24) | collective-permute-done | bytes 393248 | tf_op jit(solution)/shard_map/ppermute | solution.py:873
  230.6 4.6 %all-to-all-start.5 = ((f32[32,48,128]{2,1,0:T(8,128)}), f32[32,48,128]{2,1,0:T(8,128)S(1)}, u32[]{:S(2)}, u32[]{:S(2)}) async-start(f32[32,48,128]{2,1,0:T(8,128)} %pad_maximum_fusion), calls=%async_computation.5 | async-start | bytes 1572864 | tf_op jit(solution)/shard_map/all_to_all | solution.py:1171
  235.3 20.2 %shard_map.451 = (f32[16384,512]{1,0:T(8,128)}, f32[16384,512]{1,0:T(8,128)}, f32[16384,512]{1,0:T(8,128)}, f32[2,2,2,40,1024]{4,3,2,1,0:T(8,128)}, f32[2,2,2,40...) custom-call(s32[8192]{0:T(1024)} %copy-done.35, ...), custom_call_target="tpu_custom_call", output_to_operand_aliasing={{3}: (5, {}), {4}: (6, {}), {5}: (7, {}), {6}: (8, {})} | custom-call | flops 62914560 | bytes 50331648 | tf_op jit(solution)/shard_map/pallas_call | solution.py:281
  267.7 20.2 %shard_map.452 = (f32[16384,512]{1,0:T(8,128)}, f32[16384,512]{1,0:T(8,128)}, f32[16384,512]{1,0:T(8,128)}, f32[2,2,40,1024]{3,2,1,0:T(8,128)}, f32[2,2,40,1024]{3,2,1,0:T(8,128)}) custom-call(s32[8192]{0:T(1024)} %copy-done.35, f32[32,48,128]{2,1,0:T(8,128)} %copy-done.22, ...), custom_call_target="tpu_custom_call", output_to_operand_aliasing={{0}: (5, {}), {1}: (6, {}), {2}: (7, {}), {3}: (8, {}), {4}... | custom-call | flops 62914560 | bytes 50331648 | tf_op jit(solution)/shard_map/pallas_call | solution.py:281
  298.8 20.1 %shard_map.453 = (f32[16384,512]{1,0:T(8,128)}, f32[16384,512]{1,0:T(8,128)}, f32[16384,512]{1,0:T(8,128)}, f32[4,40,1024]{2,1,0:T(8,128)}) custom-call(s32[8192]{0:T(1024)} %copy-done.35, f32[32,32,128]{2,1,0:T(8,128)} %copy-done.31, f32[16384,512]{1,0:T(8,128)} %refs_0_.7, ...), custom_call_target="tpu_custom_call", output_to_operand_aliasing={{0}: (5, {}), {1}: (6, {}), {2}: (7, {}), {3}: (8, {})} | custom-call | flops 62914560 | bytes 50331648 | tf_op jit(solution)/shard_map/pallas_call | solution.py:281
  319.0 9.7 %collective-permute-done.29 = f32[4,40,1024]{2,1,0:T(8,128)S(1)} collective-permute-done((f32[4,40,1024]{2,1,0:T(8,128)S(1)}, f32[4,40,1024]{2,1,0:T(8,128)S(1)}, u32[]{:S(2)}, u32[]{:S(2)}) %collective-permute-start.29) | collective-permute-done | bytes 655392 | tf_op jit(solution)/shard_map/ppermute | solution.py:907
  335.4 20.2 %shard_map.454 = (f32[16384,512]{1,0:T(8,128)}, f32[16384,512]{1,0:T(8,128)}, f32[16384,512]{1,0:T(8,128)}) custom-call(s32[8192]{0:T(1024)} %copy-done.35, f32[32,32,128]{2,1,0:T(8,128)} %copy-done.32, f32[16384,512]{1,0:T(8,128)} %refs_0_.7, f32[16384,512]{1,0:T(8,128)} %refs_1_.7, ...), custom_call_target="tpu_custom_call", output_to_operand_aliasing={{0}: (5, {}), {1}: (6, {}), {2}: (7, {})} | custom-call | flops 62914560 | bytes 50331648 | tf_op jit(solution)/shard_map/pallas_call | solution.py:281
  (322 shorter events, 97.5 us)
Async XLA Ops:
  3.1 13.2 %collective-permute-start.2 = (f32[40,1024]{1,0:T(8,128)S(1)}, f32[40,1024]{1,0:T(8,128)S(1)}, u32[]{:S(2)}, u32[]{:S(2)}) collective-permute-start(f32[40,1024]{1,0:T(8,128)S(1)} %get-tuple-element.283), channel_id=1, source_target_pairs={{0,9},{1,8},{8,1},{9,0},{2,11},{3,10},{10,3},{11,2},{4,13},{5,12},... | collective-permute-start | bytes 491528 | tf_op jit(solution)/shard_map/ppermute | solution.py:898
  10.2 14.3 %all-to-all-start = ((f32[32,8,128]{2,1,0:T(8,128)}), f32[32,8,128]{2,1,0:T(8,128)S(1)}, u32[]{:S(2)}, u32[]{:S(2)}) async-start(f32[32,8,128]{2,1,0:T(8,128)} %bitcast.65), calls=%async_computation | async-start | bytes 262144 | tf_op jit(solution)/shard_map/all_to_all | solution.py:1026
  26.1 16.9 %collective-permute-start.3 = (f32[4,40,1024]{2,1,0:T(8,128)S(1)}, f32[4,40,1024]{2,1,0:T(8,128)S(1)}, u32[]{:S(2)}, u32[]{:S(2)}) collective-permute-start(f32[4,40,1024]{2,1,0:T(8,128)S(1)} %pad_maximum_fusion.2.refs_0_), channel_id=1, source_target_pairs={{0,2},{2,0},{4,6},{6,4},{1,3},{3,1},{5,7},{7,5},{8,10},{10,8},{12,... | collective-permute-start | bytes 1966088 | tf_op jit(solution)/shard_map/ppermute | solution.py:908
  26.6 16.5 %collective-permute-start.4 = (f32[4,40,1024]{2,1,0:T(8,128)S(1)}, f32[4,40,1024]{2,1,0:T(8,128)S(1)}, u32[]{:S(2)}, u32[]{:S(2)}) collective-permute-start(f32[4,40,1024]{2,1,0:T(8,128)S(1)} %pad_maximum_fusion.2.refs_0_), channel_id=1, source_target_pairs={{0,4},{2,6},{4,0},{6,2},{1,5},{3,7},{5,1},{7,3},{8,12},{10,14},{12... | collective-permute-start | bytes 1966088 | tf_op jit(solution)/shard_map/ppermute | solution.py:908
  27.6 30.9 %collective-permute-start.5 = (f32[4,40,1024]{2,1,0:T(8,128)S(1)}, f32[4,40,1024]{2,1,0:T(8,128)S(1)}, u32[]{:S(2)}, u32[]{:S(2)}) collective-permute-start(f32[4,40,1024]{2,1,0:T(8,128)S(1)} %pad_maximum_fusion.2.refs_0_), channel_id=1, source_target_pairs={{0,16},{16,0},{1,17},{17,1},{2,18},{18,2},{3,19},{19,3},{4,20},{20... | collective-permute-start | bytes 1966088 | tf_op jit(solution)/shard_map/ppermute | solution.py:907
  59.4 56.8 %all-to-all-start.1 = ((f32[32,128,128]{2,1,0:T(8,128)}), f32[32,128,128]{2,1,0:T(8,128)}, u32[]{:S(2)}, u32[]{:S(2)}) async-start(f32[32,128,128]{2,1,0:T(8,128)} %bitcast.153), calls=%async_computation.1 | async-start | bytes 4194304 | tf_op jit(solution)/shard_map/all_to_all | solution.py:1044
  63.2 35.9 %collective-permute-start.9 = (f32[4,40,1024]{2,1,0:T(8,128)S(1)}, f32[4,40,1024]{2,1,0:T(8,128)S(1)}, u32[]{:S(2)}, u32[]{:S(2)}) collective-permute-start(f32[4,40,1024]{2,1,0:T(8,128)S(1)} %copy-done.18), channel_id=1, source_target_pairs={{0,4},{2,6},{4,0},{6,2},{1,5},{3,7},{5,1},{7,3},{8,12},{10,14},{12... | collective-permute-start | bytes 1966088 | tf_op jit(solution)/shard_map/ppermute | solution.py:908
  64.7 36.4 %collective-permute-start.8 = (f32[4,40,1024]{2,1,0:T(8,128)S(1)}, f32[4,40,1024]{2,1,0:T(8,128)}, u32[]{:S(2)}, u32[]{:S(2)}) collective-permute-start(f32[4,40,1024]{2,1,0:T(8,128)S(1)} %copy-done.18), channel_id=1, source_target_pairs={{0,2},{2,0},{4,6},{6,4},{1,3},{3,1},{5,7},{7,5},{8,10},{10,8},{12,... | collective-permute-start | bytes 1966088 | tf_op jit(solution)/shard_map/ppermute | solution.py:908
  66.2 43.4 %collective-permute-start.6 = (f32[2,40,1024]{2,1,0:T(8,128)S(1)}, f32[2,40,1024]{2,1,0:T(8,128)S(1)}, u32[]{:S(2)}, u32[]{:S(2)}) collective-permute-start(f32[2,40,1024]{2,1,0:T(8,128)S(1)} %slice.213), channel_id=1, source_target_pairs={{0,2},{2,0},{4,6},{6,4},{1,3},{3,1},{5,7},{7,5},{8,10},{10,8},{12,... | collective-permute-start | bytes 983048 | tf_op jit(solution)/shard_map/ppermute | solution.py:908
  66.8 42.8 %collective-permute-start.7 = (f32[2,40,1024]{2,1,0:T(8,128)S(1)}, f32[2,40,1024]{2,1,0:T(8,128)S(1)}, u32[]{:S(2)}, u32[]{:S(2)}) collective-permute-start(f32[2,40,1024]{2,1,0:T(8,128)S(1)} %slice.214), channel_id=1, source_target_pairs={{0,4},{2,6},{4,0},{6,2},{1,5},{3,7},{5,1},{7,3},{8,12},{10,14},{12... | collective-permute-start | bytes 983048 | tf_op jit(solution)/shard_map/ppermute | solution.py:908
  99.1 17.0 %collective-permute-start.10 = (f32[2,40,1024]{2,1,0:T(8,128)S(1)}, f32[2,40,1024]{2,1,0:T(8,128)S(1)}, u32[]{:S(2)}, u32[]{:S(2)}) collective-permute-start(f32[2,40,1024]{2,1,0:T(8,128)S(1)} %slice.215), channel_id=1, source_target_pairs={{0,2},{2,0},{4,6},{6,4},{1,3},{3,1},{5,7},{7,5},{8,10},{10,8},{12,... | collective-permute-start | bytes 983048 | tf_op jit(solution)/shard_map/ppermute | solution.py:908
  102.1 14.1 %collective-permute-start.11 = (f32[2,40,1024]{2,1,0:T(8,128)S(1)}, f32[2,40,1024]{2,1,0:T(8,128)S(1)}, u32[]{:S(2)}, u32[]{:S(2)}) collective-permute-start(f32[2,40,1024]{2,1,0:T(8,128)S(1)} %slice.216), channel_id=1, source_target_pairs={{0,4},{2,6},{4,0},{6,2},{1,5},{3,7},{5,1},{7,3},{8,12},{10,14},{12... | collective-permute-start | bytes 983048 | tf_op jit(solution)/shard_map/ppermute | solution.py:908
  120.2 17.5 %collective-permute-start.14 = (f32[1024,128]{1,0:T(8,128)}, f32[1024,128]{1,0:T(8,128)S(1)}, u32[]{:S(2)}, u32[]{:S(2)}) collective-permute-start(f32[1024,128]{1,0:T(8,128)} %shard_map.436.refs_0_), channel_id=1, source_target_pairs={{0,8},{8,0},{1,9},{9,1},{2,10},{10,2},{3,11},{11,3},{4,12},{12,4},... | collective-permute-start | bytes 1572872 | tf_op jit(solution)/shard_map/ppermute | solution.py:873
  193.3 37.3 %all-to-all-start.2 = ((f32[32,32,128]{2,1,0:T(8,128)}), f32[32,32,128]{2,1,0:T(8,128)S(1)}, u32[]{:S(2)}, u32[]{:S(2)}) async-start(f32[32,32,128]{2,1,0:T(8,128)} %shard_map.446.refs_18_.refs_1_), calls=%async_computation.2 | async-start | bytes 1048576 | tf_op jit(solution)/shard_map/all_to_all | solution.py:1171
  211.5 44.0 %collective-permute-start.26 = (f32[2,2,2,40,1024]{4,3,2,1,0:T(8,128)}, f32[2,2,2,40,1024]{4,3,2,1,0:T(8,128)}, u32[]{:S(2)}, u32[]{:S(2)}) collective-permute-start(f32[2,2,2,40,1024]{4,3,2,1,0:T(8,128)} %get-tuple-element.156), channel_id=1, source_target_pairs={{0,4},{2,6},{4,0},{6,2},{1,5},{3,7},{5,1},{7,3},{8,12},{10,14},{12... | collective-permute-start | bytes 3932168 | tf_op jit(solution)/shard_map/ppermute | solution.py:908
  214.1 11.1 %collective-permute-start.24 = (f32[768,128]{1,0:T(8,128)}, f32[768,128]{1,0:T(8,128)S(1)}, u32[]{:S(2)}, u32[]{:S(2)}) collective-permute-start(f32[768,128]{1,0:T(8,128)} %shard_map.448), channel_id=1, source_target_pairs={{0,8},{8,0},{1,9},{9,1},{2,10},{10,2},{3,11},{11,3},{4,12},{12,4},... | collective-permute-start | bytes 1179656 | tf_op jit(solution)/shard_map/ppermute | solution.py:873
  215.8 44.2 %collective-permute-start.25 = (f32[2,2,2,40,1024]{4,3,2,1,0:T(8,128)}, f32[2,2,2,40,1024]{4,3,2,1,0:T(8,128)}, u32[]{:S(2)}, u32[]{:S(2)}) collective-permute-start(f32[2,2,2,40,1024]{4,3,2,1,0:T(8,128)} %get-tuple-element.154), channel_id=1, source_target_pairs={{0,2},{2,0},{4,6},{6,4},{1,3},{3,1},{5,7},{7,5},{8,10},{10,8},{12,... | collective-permute-start | bytes 3932168 | tf_op jit(solution)/shard_map/ppermute | solution.py:908
  230.6 33.2 %all-to-all-start.5 = ((f32[32,48,128]{2,1,0:T(8,128)}), f32[32,48,128]{2,1,0:T(8,128)S(1)}, u32[]{:S(2)}, u32[]{:S(2)}) async-start(f32[32,48,128]{2,1,0:T(8,128)} %pad_maximum_fusion), calls=%async_computation.5 | async-start | bytes 1572864 | tf_op jit(solution)/shard_map/all_to_all | solution.py:1171
  258.3 29.6 %collective-permute-start.28 = (f32[2,2,40,1024]{3,2,1,0:T(8,128)S(1)}, f32[2,2,40,1024]{3,2,1,0:T(8,128)S(1)}, u32[]{:S(2)}, u32[]{:S(2)}) collective-permute-start(f32[2,2,40,1024]{3,2,1,0:T(8,128)S(1)} %get-tuple-element.258.refs_9_), channel_id=1, source_target_pairs={{0,2},{2,0},{4,6},{6,4},{1,3},{3,1},{5,7},{7,5},{8,10},{10,8},{12,... | collective-permute-start | bytes 1966088 | tf_op jit(solution)/shard_map/ppermute | solution.py:908
  262.4 26.7 %collective-permute-start.27 = (f32[2,2,40,1024]{3,2,1,0:T(8,128)S(1)}, f32[2,2,40,1024]{3,2,1,0:T(8,128)}, u32[]{:S(2)}, u32[]{:S(2)}) collective-permute-start(f32[2,2,40,1024]{3,2,1,0:T(8,128)S(1)} %get-tuple-element.260.refs_8_), channel_id=1, source_target_pairs={{0,4},{2,6},{4,0},{6,2},{1,5},{3,7},{5,1},{7,3},{8,12},{10,14},{12... | collective-permute-start | bytes 1966088 | tf_op jit(solution)/shard_map/ppermute | solution.py:908
  263.9 31.2 %all-to-all-start.4 = ((f32[32,32,128]{2,1,0:T(8,128)}), f32[32,32,128]{2,1,0:T(8,128)S(1)}, u32[]{:S(2)}, u32[]{:S(2)}) async-start(f32[32,32,128]{2,1,0:T(8,128)} %get-tuple-element.144), calls=%async_computation.4 | async-start | bytes 1048576 | tf_op jit(solution)/shard_map/all_to_all | solution.py:1194
  290.5 38.2 %collective-permute-start.29 = (f32[4,40,1024]{2,1,0:T(8,128)S(1)}, f32[4,40,1024]{2,1,0:T(8,128)S(1)}, u32[]{:S(2)}, u32[]{:S(2)}) collective-permute-start(f32[4,40,1024]{2,1,0:T(8,128)S(1)} %pad_maximum_fusion.4.refs_7_), channel_id=1, source_target_pairs={{0,16},{16,0},{1,17},{17,1},{2,18},{18,2},{3,19},{19,3},{4,20},{20... | collective-permute-start | bytes 1966088 | tf_op jit(solution)/shard_map/ppermute | solution.py:907
  295.1 39.5 %all-to-all-start.3 = ((f32[32,32,128]{2,1,0:T(8,128)}), f32[32,32,128]{2,1,0:T(8,128)S(1)}, u32[]{:S(2)}, u32[]{:S(2)}) async-start(f32[32,32,128]{2,1,0:T(8,128)} %get-tuple-element.143), calls=%async_computation.3 | async-start | bytes 1048576 | tf_op jit(solution)/shard_map/all_to_all | solution.py:1194
  331.7 24.0 %collective-permute-start.31 = (f32[2,40,1024]{2,1,0:T(8,128)S(1)}, f32[2,40,1024]{2,1,0:T(8,128)S(1)}, u32[]{:S(2)}, u32[]{:S(2)}) collective-permute-start(f32[2,40,1024]{2,1,0:T(8,128)S(1)} %pad_maximum_fusion.10), channel_id=1, source_target_pairs={{0,8},{8,0},{1,9},{9,1},{2,10},{10,2},{3,11},{11,3},{4,12},{12,4},... | collective-permute-start | bytes 983048 | tf_op jit(solution)/shard_map/ppermute | solution.py:873
  (81 other events, 416.8 us)
